TPU v7x, 512 devices: a whole 4x4x16 slice. The times are simulated.
512 devices in a mesh: dp: 32 (over z_lo, y), ctx: 16 (over z_hi, x, core).
Axes of the slice: x: 4, y: 4, z: 16 (z_hi: 2, z_lo: 8; z = z_hi * 8 + z_lo), core: 2. Of those that a mesh axis runs over, the one named last changes fastest.
Arguments:
- queries_q: bfloat16 [32, 2048, 1792], P('dp', 'ctx'), may hold values from -5 to 5
- keys: bfloat16 [32, 2048, 256], P('dp', 'ctx'), may hold values from -5 to 5
- values: bfloat16 [32, 2048, 256], P('dp', 'ctx'), may hold values from -6 to 6
- lengths: int32 [32, 4], P('dp'), may hold values from 1 to 1536, 2048 in all within a row
- query_emb: bfloat16 [4096, 1792], P('dp'), may hold values from -6 to 6
- positive: int32 [4096], P('dp'), may hold values from 0 to 127
Outputs:
- query_grad: float32 [4096, 1792], P('dp')
- grad_queries: bfloat16 [32, 2048, 1792], P('dp', 'ctx')
- grad_keys: bfloat16 [32, 2048, 256], P('dp', 'ctx')
- grad_values: bfloat16 [32, 2048, 256], P('dp', 'ctx')
Inputs may be any that keep to these rules, and one draw needn't show every extreme that they name: The 4 lengths of each row sum to 2048, and the longest is 1536.
All inputs are finite; a program needn't handle non-finite values.
Results may differ from a plain program's by a relative error of at most 0.012.
The roundings to bfloat16 on the way count: a program that leaves them out, or rounds other values in their place, can miss the bound.
Values may be sent and summed in bfloat16 or wider, within the bound.
No kernel may reach another device: no remote copies, remote signals or barrier semaphores. Data moves between devices by JAX's collectives and lax.ppermute only.
A program may use at most 64 MiB of HBM per device.

v0:
```python
import jax
import jax.numpy as jnp
from jax import lax
from jax.sharding import PartitionSpec as P

HEAD_DIM = 128
HEADS = 14
KV_HEADS = 2


INVERSE_TEMPER = 0.05
EPSILON = 1e-06
FULL_ACCURACY = lax.Precision.HIGHEST


def document_ids(lengths_row, positions):
    doc_ends = jnp.cumsum(lengths_row)
    return jnp.sum((positions[:, None] >= doc_ends[None, :]).astype(jnp.int32), axis=1)


def rescale_back(inverse, unit_vec, upstream):
    inner_sum = jnp.sum(unit_vec * upstream, axis=1, keepdims=True)
    return inverse * (upstream - unit_vec * inner_sum)


def predicted_less_label(similarity_logits, positive):
    exp_logits = jnp.exp(similarity_logits)
    target = (
        jnp.arange(similarity_logits.shape[1], dtype=jnp.int32)[None, :] == positive[:, None]
    ).astype(jnp.float32)
    return exp_logits / jnp.sum(exp_logits, axis=1, keepdims=True) - target


def per_device(queries_q, keys, values, lengths, query_emb, positive):
    tok_rows = queries_q.shape[1]
    emb_width = queries_q.shape[2]
    kv_width = keys.shape[2]
    per_group = HEADS // KV_HEADS
    factor = HEAD_DIM ** (-0.5)
    whole_keys, whole_values = (
        lax.all_gather(keys, "ctx", axis=1, tiled=True),
        lax.all_gather(values, "ctx", axis=1, tiled=True),
    )
    seq_len = whole_keys.shape[1]
    tile_of_lookups = min(512, seq_len)
    first_pos = lax.axis_index("ctx") * tok_rows
    key_pos = jnp.arange(seq_len, dtype=jnp.int32)
    query_pos = first_pos + jnp.arange(tok_rows, dtype=jnp.int32)
    len_row = lengths[0]
    key_doc = document_ids(len_row, key_pos)
    query_doc = document_ids(len_row, query_pos)
    doc_index = jnp.arange(len_row.shape[0], dtype=jnp.int32)
    doc_starts = jnp.cumsum(len_row) - len_row
    doc_begin = jnp.sum(jnp.where(doc_index == query_doc[0], doc_starts, 0))
    low_block = doc_begin // tile_of_lookups
    high_block = (first_pos + tok_rows - 1) // tile_of_lookups + 1
    q_heads = queries_q[0].reshape(tok_rows, KV_HEADS, per_group, HEAD_DIM)
    k_all = whole_keys[0].reshape(seq_len, KV_HEADS, HEAD_DIM)
    v_all = whole_values[0].reshape(seq_len, KV_HEADS, HEAD_DIM)

    def block_rows(block_idx, table):
        return lax.dynamic_slice_in_dim(table, block_idx * tile_of_lookups, tile_of_lookups, 0)

    def block_scores(block_idx):
        k_rows = block_rows(block_idx, k_all)
        doc_rows = block_rows(block_idx, key_doc)
        pos_rows = block_idx * tile_of_lookups + jnp.arange(tile_of_lookups, dtype=jnp.int32)
        raw_scores = (
            jnp.einsum("tgqd,sgd->gqts", q_heads, k_rows, preferred_element_type=jnp.float32)
            * factor
        )
        allowed = (query_doc[:, None] == doc_rows[None, :]) & (
            pos_rows[None, :] <= query_pos[:, None]
        )
        return jnp.where(allowed, raw_scores, -jnp.inf)

    def stat_step(block_idx, carry):
        row_top, row_total = carry
        scores = block_scores(block_idx)
        new_top = jnp.maximum(row_top, jnp.max(scores, axis=-1, keepdims=True))
        row_total = row_total * jnp.exp(row_top - new_top) + jnp.sum(
            jnp.exp(scores - new_top), axis=-1, keepdims=True
        )
        return (new_top, row_total)

    stat_shape = (KV_HEADS, per_group, tok_rows, 1)
    running_figures_start = (
        jnp.full(stat_shape, -1e30, jnp.float32),
        jnp.zeros(stat_shape, jnp.float32),
    )
    row_top, row_total = lax.fori_loop(low_block, high_block, stat_step, running_figures_start)
    log_total = row_top + jnp.log(row_total)

    def out_step(block_idx, out_acc):
        weights = jnp.exp(block_scores(block_idx) - log_total).astype(jnp.bfloat16)
        v_rows = block_rows(block_idx, v_all)
        return out_acc + jnp.einsum(
            "gqts,sgd->tgqd", weights, v_rows, preferred_element_type=jnp.float32
        )

    head_shape = (tok_rows, KV_HEADS, per_group, HEAD_DIM)
    attended = lax.fori_loop(
        low_block, high_block, out_step, jnp.zeros(head_shape, jnp.float32)
    ).reshape(tok_rows, emb_width)
    member = (doc_index[:, None] == query_doc[None, :]).astype(jnp.float32)
    doc_sum = lax.psum(jnp.dot(member, attended, precision=FULL_ACCURACY), "ctx")
    doc_len = len_row.astype(jnp.float32)[:, None]
    doc_emb = doc_sum / doc_len
    doc_inv = lax.rsqrt(jnp.sum(doc_emb * doc_emb, axis=1, keepdims=True) + EPSILON)
    document_normalized = doc_emb * doc_inv
    query_f = query_emb.astype(jnp.float32)
    query_inv = lax.rsqrt(jnp.sum(query_f * query_f, axis=1, keepdims=True) + EPSILON)
    query_normalized = query_f * query_inv
    every_document = lax.all_gather(document_normalized, "dp", axis=0, tiled=True)
    similarity_logits = (
        jnp.dot(query_normalized, every_document.T, precision=FULL_ACCURACY) / INVERSE_TEMPER
    )
    scaling_coefficient = predicted_less_label(similarity_logits, positive)
    query_upstream_gradient = (
        jnp.dot(scaling_coefficient, every_document, precision=FULL_ACCURACY) / INVERSE_TEMPER
    )
    passage_contributions = (
        jnp.dot(scaling_coefficient.T, query_normalized, precision=FULL_ACCURACY) / INVERSE_TEMPER
    )
    document_upstream_gradient = lax.psum_scatter(
        passage_contributions, "dp", scatter_dimension=0, tiled=True
    )
    query_grad = rescale_back(query_inv, query_normalized, query_upstream_gradient)
    passage_derivative = (
        rescale_back(doc_inv, document_normalized, document_upstream_gradient) / doc_len
    )
    out_grad = jnp.dot(member.T, passage_derivative, precision=FULL_ACCURACY)
    out_heads = out_grad.astype(jnp.bfloat16).reshape(head_shape)
    row_delta = jnp.sum((out_grad * attended).reshape(head_shape), axis=-1)
    row_delta = jnp.transpose(row_delta, (1, 2, 0))[..., None]

    def back_step(block_idx, carry):
        query_acc, key_terms, value_terms = carry
        probability = jnp.exp(block_scores(block_idx) - log_total)
        weights = probability.astype(jnp.bfloat16)
        k_rows = block_rows(block_idx, k_all)
        v_rows = block_rows(block_idx, v_all)
        flow_grad = jnp.einsum(
            "tgqd,sgd->gqts", out_heads, v_rows, preferred_element_type=jnp.float32
        )
        score_grad = (probability * (flow_grad - row_delta)).astype(jnp.bfloat16)
        query_acc = query_acc + jnp.einsum(
            "gqts,sgd->tgqd", score_grad, k_rows, preferred_element_type=jnp.float32
        )
        key_part = (
            jnp.einsum("gqts,tgqd->sgd", score_grad, q_heads, preferred_element_type=jnp.float32)
            * factor
        )
        value_part = jnp.einsum(
            "gqts,tgqd->sgd", weights, out_heads, preferred_element_type=jnp.float32
        )
        key_terms = lax.dynamic_update_slice_in_dim(
            key_terms, key_part, block_idx * tile_of_lookups, 0
        )
        value_terms = lax.dynamic_update_slice_in_dim(
            value_terms, value_part, block_idx * tile_of_lookups, 0
        )
        return (query_acc, key_terms, value_terms)

    term_shape = (seq_len, KV_HEADS, HEAD_DIM)
    back_init = (
        jnp.zeros(head_shape, jnp.float32),
        jnp.zeros(term_shape, jnp.float32),
        jnp.zeros(term_shape, jnp.float32),
    )
    query_acc, key_terms, value_terms = lax.fori_loop(low_block, high_block, back_step, back_init)
    grad_queries = (query_acc * factor).astype(jnp.bfloat16).reshape(1, tok_rows, emb_width)
    key_sum, value_sum = (
        lax.psum_scatter(
            key_terms.reshape(1, seq_len, kv_width).astype(jnp.bfloat16),
            "ctx",
            scatter_dimension=1,
            tiled=True,
        ).astype(jnp.float32),
        lax.psum_scatter(
            value_terms.reshape(1, seq_len, kv_width).astype(jnp.bfloat16),
            "ctx",
            scatter_dimension=1,
            tiled=True,
        ).astype(jnp.float32),
    )
    return (query_grad, grad_queries, key_sum.astype(jnp.bfloat16), value_sum.astype(jnp.bfloat16))


def solution(mesh):
    placed = (
        P("dp", "ctx", None),
        P("dp", "ctx", None),
        P("dp", "ctx", None),
        P("dp", None),
        P("dp", None),
        P("dp"),
    )
    return jax.shard_map(
        per_device,
        mesh=mesh,
        in_specs=placed,
        out_specs=(P("dp", None), P("dp", "ctx", None), P("dp", "ctx", None), P("dp", "ctx", None)),
        check_vma=False,
    )
```

profile of v0, /device:TPU:8, one launch (start us, length us, event | category | flops | bytes accessed | tf_op | source)
XLA Modules:
  0.0 1121.3 jit_solution(4340067111308906770)
XLA Ops:
  7.2 1.6 copy.63
  8.9 1.6 copy.62
  10.5 0.7 bitcast_convert_fusion
  11.2 0.8 reduce-window.8
  12.1 1.3 fusion.81
  16.1 1.2 fusion.65
  17.3 1.3 copy.64
  18.9 74.2 %all-gather.6.cloned.1.call-done = bf16[1,2048,256]{1,2,0:T(8,128)(2,1)} async-done(((bf16[1,128,256]{1,2,0:T(8,128)(2,1)}), bf16[1,2048,256]{1,2,0:T(8,128)(2,1)}) %all-gather.6.cloned.1.call-update) | async-done | bytes 1048592 | tf_op jit(solution)/shard_map/all_gather | solution.py:41
  93.1 1.6 copy.67
  94.7 1.8 while.39
  95.1 0.7 fusion.118
  95.8 0.7 exponential_reduce_fusion.2
  96.6 68.1 %all-gather.4.cloned.1.call-done = bf16[1,2048,256]{1,2,0:T(8,128)(2,1)} async-done(((bf16[1,128,256]{1,2,0:T(8,128)(2,1)}), bf16[1,2048,256]{1,2,0:T(8,128)(2,1)}) %all-gather.4.cloned.1.call-update) | async-done | bytes 1048592 | tf_op jit(solution)/shard_map/all_gather | solution.py:42
  164.7 2.6 while.40
  165.1 2.3 fusion.122
  167.4 0.5 fusion.78
  167.9 122.8 %psum.7 = f32[4,1792]{1,0:T(4,128)S(1)} all-reduce(f32[4,1792]{1,0:T(4,128)S(1)} %fusion.78), channel_id=1, replica_groups=mesh['dp'=32,'ctx'=16] {'ctx'}, use_global_device_ids=true, to_apply=%region_11.12 | all-reduce | flops 7168 | bytes 57344 | tf_op jit(solution)/shard_map/psum | solution.py:106
  291.0 123.0 %all-gather = f32[32,4,1792]{2,1,0:T(4,128)} all-gather(f32[1,4,1792]{2,1,0:T(4,128)S(1)} %multiply_bitcast_fusion), channel_id=1, replica_groups=mesh['dp'=32,'ctx'=16] {'dp'}, dimensions={0}, use_global_device_ids=true | all-gather | bytes 946176 | tf_op jit(solution)/shard_map/all_gather | solution.py:114
  414.0 1.5 reshape.126
  415.5 1.1 fusion.84
  416.6 1.9 convolution_multiply_fusion
  418.6 1.3 dynamic-slice
  420.5 2.4 copy.70
  422.9 443.1 %all-reduce.3.cloned.1.call-done = f32[128,1792]{1,0:T(8,128)} async-done(((f32[128,1792]{1,0:T(8,128)}), f32[128,1792]{1,0:T(8,128)}) %all-reduce.3.cloned.1.call-update) | async-done | bytes 917520
  865.9 1.0 multiply_reduce_fusion
  867.0 2.9 fusion.83
  869.8 1.5 copy.71
  871.3 1.3 copy.69
  872.6 1.0 copy.75
  873.7 1.1 broadcast.80.clone
  874.8 1.1 broadcast.80
  875.9 7.7 while.41
  876.2 0.6 fusion.133
  877.1 1.0 fusion.137
  878.1 2.5 fusion.134
  880.6 0.6 fusion.135
  881.3 0.5 copy-done.6
  881.9 0.7 fusion.136
  882.6 1.0 copy-done.7
  883.6 2.8 copy.77
  886.5 1.5 convert_element_type.77
  888.1 3.7 copy.76
  891.8 2.5 convert_element_type.75
  894.3 1.1 fusion.62
  895.4 1.2 fusion.64
  896.8 1.0 copy.78
  897.7 113.6 %reduce-scatter.5.cloned.1.call-done = bf16[1,128,256]{2,1,0:T(8,128)(2,1)} async-done(((bf16[1,2048,256]{2,1,0:T(8,128)(2,1)}), bf16[1,128,256]{2,1,0:T(8,128)(2,1)}) %reduce-scatter.5.cloned.1.call-update) | async-done | bytes 65552 | tf_op jit(solution)/shard_map/reduce_scatter | solution.py:180
  1011.3 103.4 %reduce-scatter.3.cloned.1.call-done = bf16[1,128,256]{2,1,0:T(8,128)(2,1)} async-done(((bf16[1,2048,256]{2,1,0:T(8,128)(2,1)}), bf16[1,128,256]{2,1,0:T(8,128)(2,1)}) %reduce-scatter.3.cloned.1.call-update) | async-done | bytes 65552 | tf_op jit(solution)/shard_map/reduce_scatter | solution.py:174
  (58 shorter events, 2.6 us)
Async XLA Ops:
  7.2 85.9 %all-gather.6.cloned.1.call-start = ((), (), s32[]{:S(2)}) async-start(), calls=%async_computation.3 | async-start | bytes 1114112 | tf_op jit(solution)/shard_map/all_gather | solution.py:41
  8.8 155.8 %all-gather.4.cloned.1.call-start = ((), (), s32[]{:S(2)}) async-start(), calls=%async_computation.2 | async-start | bytes 1114112 | tf_op jit(solution)/shard_map/all_gather | solution.py:42
  10.5 855.5 %all-reduce.3.cloned.1.call-start = ((), (), s32[]{:S(2)}) async-start(), calls=%async_computation.6 | async-start | bytes 1835008
  167.4 123.6 %copy-start.3 = (f32[128,2,7,128]{0,3,2,1:T(8,128)}, f32[128,2,7,128]{0,3,2,1:T(8,128)S(1)}, u32[]{:S(2)}) copy-start(f32[128,2,7,128]{0,3,2,1:T(8,128)S(1)} %get-tuple-element.183) | copy-start | bytes 2752516
  167.4 248.1 %copy-start = (bf16[128,1792]{1,0:T(8,128)(2,1)S(1)}, bf16[128,1792]{1,0:T(8,128)(2,1)}, u32[]{:S(2)}) copy-start(bf16[128,1792]{1,0:T(8,128)(2,1)} %param.16) | copy-start | bytes 1376260
  167.4 249.2 %copy-start.9 = (s32[128]{0:T(128)S(1)}, s32[128]{0:T(128)}, u32[]{:S(2)}) copy-start(s32[128]{0:T(128)} %param.17) | copy-start | bytes 1540
  415.5 454.3 %copy-start.1 = (f32[128,1792]{1,0:T(8,128)}, f32[128,1792]{1,0:T(8,128)S(1)}, u32[]{:S(2)}) copy-start(f32[128,1792]{1,0:T(8,128)S(1)} %reshape.126) | copy-start | bytes 2752516
  418.5 592.8 %reduce-scatter.5.cloned.1.call-start = ((), (), s32[]{:S(2)}) async-start(), calls=%async_computation.5 | async-start | bytes 1114112 | tf_op jit(solution)/shard_map/reduce_scatter | solution.py:180
  873.6 2.3 copy-start.8
  875.9 1.2 copy-start.4
  878.1 3.2 copy-start.5
  880.6 1.2 copy-start.6
  882.6 1.0 copy-start.7
  888.0 6.3 copy-start.2
  888.0 226.7 %reduce-scatter.3.cloned.1.call-start = ((), (), s32[]{:S(2)}) async-start(), calls=%async_computation.4 | async-start | bytes 1114112 | tf_op jit(solution)/shard_map/reduce_scatter | solution.py:174
Sparse Core Ops, SparseCore 0:
  11.7 81.3 all-gather.5
  96.8 67.7 all-gather.3
  418.6 447.2 all-reduce.2
  888.1 123.1 reduce-scatter.4
  1016.4 98.2 reduce-scatter.2
where the time goes:
time: 1130 us; the launch traced here: 1120 us
  waiting for transfers between devices  802 us (71%)
  blocking collectives  246 us (22%)
  local copies, waits for them, and re-layouts  31.2 us (3%)
  between operations  17.2 us (2%)
  matrix products  15.9 us (1%)
    unnamed x6, waiting for transfers between devices  443 us
    all_gather x1, blocking collectives, per_device(): lax.all_gather(document_normalized, 'dp', axis=0, tiled=True)  123 us
    psum x1, blocking collectives, per_device(): lax.psum(jnp.dot(member, attended, precision=FULL_ACCURACY), 'ctx')  123 us
    reduce_scatter x1, waiting for transfers between devices, per_device(): lax.psum_scatter(value_terms.reshape(1, seq_len, kv_width).astype(jnp.bfl...  114 us
    reduce_scatter x1, waiting for transfers between devices, per_device(): lax.psum_scatter(key_terms.reshape(1, seq_len, kv_width).astype(jnp.bfloa...  103 us
    all_gather x1, waiting for transfers between devices, per_device(): lax.all_gather(keys, 'ctx', axis=1, tiled=True)  74.2 us
    all_gather x1, waiting for transfers between devices, per_device(): lax.all_gather(values, 'ctx', axis=1, tiled=True)  68.1 us
  transfers between devices with their start and end apart: 5, of which 5 were waited for; matrix products, arithmetic and copies ran while one was open for 2% of the time, Pallas kernels for 0%

commit v1 on v0

v1 whole, which is shorter than its diff:
```python
import jax
import jax.numpy as jnp
from jax import lax
from jax.experimental import pallas as pl
from jax.experimental.pallas import tpu as pltpu
from jax.sharding import Mesh
from jax.sharding import PartitionSpec as P

HEAD_DIM = 128
HEADS = 14
KV_HEADS = 2
PER_GROUP = HEADS // KV_HEADS
DOCS = 4
TOK = 128
SEQ = 2048
EMB = HEADS * HEAD_DIM
KVW = KV_HEADS * HEAD_DIM
GROUP_W = PER_GROUP * TOK
CHUNK = 2 * TOK
HALF = SEQ // 2
HALF_CHUNKS = HALF // CHUNK
CHUNKS = 2 * HALF_CHUNKS
PIECE = EMB // 2
NDOC = 128

FACTOR = HEAD_DIM ** (-0.5)
INVERSE_TEMPER = 0.05
EPSILON = 1e-06
FULL_ACCURACY = lax.Precision.HIGHEST
MASKED = -1e30
NT = (((1,), (1,)), ((), ()))
TN = (((0,), (0,)), ((), ()))
NN = (((1,), (0,)), ((), ()))
NEAR = ("x", "core")
VMEM_BYTES = 40 * 1024 * 1024


def mm(a, b, dims, precision=None):
    return lax.dot_general(a, b, dims, precision=precision, preferred_element_type=jnp.float32)


class Row:
    def __init__(self, info):
        self.first, self.core, self.high = info[0], info[1], info[2]
        self.ends = [info[3], info[4], info[5]]
        self.qpos = self.first + lax.broadcasted_iota(jnp.int32, (1, TOK), 1)
        start = jnp.zeros((1, TOK), jnp.int32)
        doc = jnp.zeros((1, TOK), jnp.int32)
        first_start = jnp.int32(0)
        for end in self.ends:
            start = jnp.where(self.qpos >= end, end, start)
            doc = doc + (self.qpos >= end).astype(jnp.int32)
            first_start = jnp.where(self.first >= end, end, first_start)
        self.start = start
        rows = lax.broadcasted_iota(jnp.int32, (8, TOK), 0)
        self.member = (rows == doc).astype(jnp.float32)
        self.skip = HALF_CHUNKS * (1 - self.high)
        self.low_chunk = lax.div(first_start, CHUNK) + self.skip
        self.high_chunk = lax.div(self.first + (TOK - 1), CHUNK) + self.skip + 1

    def bias(self, chunk):
        place = lax.broadcasted_iota(jnp.int32, (CHUNK, TOK), 0)
        half = lax.div(place, TOK)
        turned = jnp.where(self.core == 1, 1 - half, half)
        pos = (chunk - self.skip) * CHUNK + turned * TOK + (place - half * TOK)
        allowed = (pos >= self.start) & (pos <= self.qpos)
        one = jnp.where(allowed, 0.0, MASKED).astype(jnp.float32)
        return jnp.concatenate([one] * PER_GROUP, axis=1)


def chunk_of(mine, other, chunk, column):
    at = slice(column * HEAD_DIM, (column + 1) * HEAD_DIM)
    return jnp.concatenate([mine[chunk, :, at], other[chunk, :, at]], axis=0)


def head_rows(ref, group):
    return jnp.concatenate(
        [
            ref[:, (group * PER_GROUP + h) * HEAD_DIM : (group * PER_GROUP + h + 1) * HEAD_DIM]
            for h in range(PER_GROUP)
        ],
        axis=0,
    )


def attend_kernel(info, q, mine, other, att, lse, doc_sum, held):
    row = Row(info)
    for group in range(KV_HEADS):
        q_rows = head_rows(q, group)
        columns = slice(group * GROUP_W, (group + 1) * GROUP_W)

        def score_step(chunk, top):
            scores = mm(chunk_of(mine, other, chunk, group), q_rows, NT) * FACTOR
            scores = scores + row.bias(chunk)
            held[chunk] = scores
            return jnp.maximum(top, jnp.max(scores, axis=0, keepdims=True))

        top = lax.fori_loop(
            row.low_chunk,
            row.high_chunk,
            score_step,
            jnp.full((1, GROUP_W), MASKED, jnp.float32),
        )

        def total_step(chunk, total):
            return total + jnp.sum(jnp.exp(held[chunk] - top), axis=0, keepdims=True)

        total = lax.fori_loop(
            row.low_chunk, row.high_chunk, total_step, jnp.zeros((1, GROUP_W), jnp.float32)
        )
        log_total = top + jnp.log(total)
        lse[:, columns] = jnp.broadcast_to(log_total, (8, GROUP_W))
        att[:, columns] = jnp.zeros((HEAD_DIM, GROUP_W), jnp.float32)

        def out_step(chunk, carry):
            weights = jnp.exp(held[chunk] - log_total).astype(jnp.bfloat16)
            v_rows = chunk_of(mine, other, chunk, KV_HEADS + group)
            att[:, columns] += mm(v_rows, weights, TN)
            return carry

        lax.fori_loop(row.low_chunk, row.high_chunk, out_step, 0)
        for h in range(PER_GROUP):
            at = slice(group * GROUP_W + h * TOK, group * GROUP_W + (h + 1) * TOK)
            doc_sum[:, at] = mm(row.member, att[:, at], NT, FULL_ACCURACY)


def back_kernel(info, q, mine, other, att, lse, doc_grad, dq, d_mine, d_other, dq_acc):
    row = Row(info)
    d_mine[...] = jnp.zeros(d_mine.shape, d_mine.dtype)
    d_other[...] = jnp.zeros(d_other.shape, d_other.dtype)
    member_low = row.member.astype(jnp.bfloat16)
    for group in range(KV_HEADS):
        columns = slice(group * GROUP_W, (group + 1) * GROUP_W)
        q_rows = head_rows(q, group)
        log_total = lse[0:1, columns]
        out_rows, deltas = [], []
        for h in range(PER_GROUP):
            at = slice(group * GROUP_W + h * TOK, group * GROUP_W + (h + 1) * TOK)
            grad = doc_grad[:, at]
            out_rows.append(mm(member_low, grad.astype(jnp.bfloat16), TN).astype(jnp.bfloat16))
            by_doc = mm(grad, att[:, at], NN, FULL_ACCURACY)
            deltas.append(jnp.sum(row.member * by_doc, axis=0, keepdims=True))
        out_low = jnp.concatenate(out_rows, axis=0)
        delta = jnp.concatenate(deltas, axis=1)
        dq_acc[...] = jnp.zeros(dq_acc.shape, jnp.float32)

        def step(chunk, carry):
            k_rows = chunk_of(mine, other, chunk, group)
            v_rows = chunk_of(mine, other, chunk, KV_HEADS + group)
            scores = mm(k_rows, q_rows, NT) * FACTOR + row.bias(chunk)
            probs = jnp.exp(scores - log_total)
            flow = mm(v_rows, out_low, NT)
            score_grad = (probs * (flow - delta)).astype(jnp.bfloat16)
            dq_acc[...] += mm(k_rows, score_grad, TN)
            k_part = (mm(score_grad, q_rows, NN) * FACTOR).astype(jnp.bfloat16)
            v_part = mm(probs.astype(jnp.bfloat16), out_low, NN).astype(jnp.bfloat16)
            k_at = slice(group * HEAD_DIM, (group + 1) * HEAD_DIM)
            v_at = slice(KVW + group * HEAD_DIM, KVW + (group + 1) * HEAD_DIM)
            d_mine[chunk, :, k_at] = k_part[:TOK]
            d_other[chunk, :, k_at] = k_part[TOK:]
            d_mine[chunk, :, v_at] = v_part[:TOK]
            d_other[chunk, :, v_at] = v_part[TOK:]
            return carry

        lax.fori_loop(row.low_chunk, row.high_chunk, step, 0)
        for h in range(PER_GROUP):
            at = slice((group * PER_GROUP + h) * HEAD_DIM, (group * PER_GROUP + h + 1) * HEAD_DIM)
            block = dq_acc[:, h * TOK : (h + 1) * TOK]
            dq[:, at] = (block.T * FACTOR).astype(jnp.bfloat16)


def vmem():
    return pl.BlockSpec(memory_space=pltpu.VMEM)


def attend(info, q, mine, other):
    return pl.pallas_call(
        attend_kernel,
        out_shape=(
            jax.ShapeDtypeStruct((HEAD_DIM, HEADS * TOK), jnp.float32),
            jax.ShapeDtypeStruct((8, HEADS * TOK), jnp.float32),
            jax.ShapeDtypeStruct((8, EMB), jnp.float32),
        ),
        in_specs=[pl.BlockSpec(memory_space=pltpu.SMEM)] + [vmem()] * 3,
        out_specs=(vmem(),) * 3,
        scratch_shapes=[pltpu.VMEM((CHUNKS, CHUNK, GROUP_W), jnp.float32)],
        compiler_params=pltpu.CompilerParams(vmem_limit_bytes=VMEM_BYTES),
        name="attend",
    )(info, q, mine, other)


def attend_back(info, q, mine, other, att, lse, doc_grad):
    return pl.pallas_call(
        back_kernel,
        out_shape=(
            jax.ShapeDtypeStruct((TOK, EMB), jnp.bfloat16),
            jax.ShapeDtypeStruct((CHUNKS, TOK, 2 * KVW), jnp.bfloat16),
            jax.ShapeDtypeStruct((CHUNKS, TOK, 2 * KVW), jnp.bfloat16),
        ),
        in_specs=[pl.BlockSpec(memory_space=pltpu.SMEM)] + [vmem()] * 6,
        out_specs=(vmem(),) * 3,
        scratch_shapes=[pltpu.VMEM((HEAD_DIM, GROUP_W), jnp.float32)],
        compiler_params=pltpu.CompilerParams(vmem_limit_bytes=VMEM_BYTES),
        name="attend_back",
    )(info, q, mine, other, att, lse, doc_grad)


def to_all(block, axes, count):
    return lax.all_to_all(jnp.broadcast_to(block[None], (count,) + block.shape), axes, 0, 0)


def swap_cores(block):
    return lax.ppermute(block, "core", [(0, 1), (1, 0)])


def rescale_back(inverse, unit_vec, upstream):
    inner_sum = jnp.sum(unit_vec * upstream, axis=1, keepdims=True)
    return inverse * (upstream - unit_vec * inner_sum)


def per_device(queries_q, keys, values, lengths, query_emb, positive):
    z_lo, y, z_hi, x, core = (lax.axis_index(a) for a in ("zlo", "y", "zhi", "x", "core"))
    q = queries_q[0]
    len_row = lengths[0]
    ends = jnp.cumsum(len_row)
    first_pos = ((z_hi * 4 + x) * 2 + core) * TOK
    info = jnp.stack([first_pos, core, z_hi, ends[0], ends[1], ends[2], ends[3], z_lo])
    info = info.astype(jnp.int32)

    kv = jnp.concatenate([keys[0], values[0]], axis=1)
    kv_low = lax.ppermute(kv, "zhi", [(0, 1)])
    own_part = to_all(kv, "x", 4)
    low_part = to_all(kv_low, "x", 4)
    mine = jnp.concatenate([low_part, own_part], axis=0)
    other = swap_cores(mine)

    att, lse, doc_sum = attend(info, q, mine, other)

    doc_len = len_row.astype(jnp.float32)[:, None]
    doc_part = (doc_sum[:DOCS] / doc_len).reshape(8, 7, 128)
    doc_part = jnp.sum(lax.all_to_all(doc_part, NEAR, 0, 0), axis=0)
    column = to_all(doc_part, ("zlo", "zhi"), 16).reshape(8, 2, 7, 128)
    column = column[:, 0] + column[:, 1]
    every = to_all(column, ("y", "x", "core"), 32).reshape(4, 4, 2, 8, PIECE)
    every = every.transpose(3, 0, 1, 2, 4).reshape(NDOC, EMB)

    every_inv = lax.rsqrt(jnp.sum(every * every, axis=1, keepdims=True) + EPSILON)
    every_unit = every * every_inv
    query_f = query_emb.astype(jnp.float32)
    query_inv = lax.rsqrt(jnp.sum(query_f * query_f, axis=1, keepdims=True) + EPSILON)
    query_unit = query_f * query_inv
    logits = jnp.dot(query_unit, every_unit.T, precision=FULL_ACCURACY) / INVERSE_TEMPER
    exp_logits = jnp.exp(logits)
    target = jnp.arange(NDOC, dtype=jnp.int32)[None, :] == positive[:, None]
    coefficient = exp_logits / jnp.sum(exp_logits, axis=1, keepdims=True) - target.astype(
        jnp.float32
    )

    near_coefficient = lax.dynamic_index_in_dim(
        coefficient.T.reshape(32, DOCS, 128), x, axis=1, keepdims=False
    )
    near_unit = lax.dynamic_slice_in_dim(query_unit, core * PIECE, PIECE, 1)
    terms = jnp.dot(near_coefficient, near_unit, precision=FULL_ACCURACY) / INVERSE_TEMPER
    terms = lax.all_to_all(terms.reshape(32, 7, 128), ("zlo", "y"), 0, 0)
    upstream = to_all(jnp.sum(terms, axis=0), NEAR, 8).reshape(DOCS, EMB)

    row_at = (z_lo * 4 + y) * DOCS
    doc_unit = lax.dynamic_slice_in_dim(every_unit, row_at, DOCS, 0)
    doc_inv = lax.dynamic_slice_in_dim(every_inv, row_at, DOCS, 0)
    doc_grad = rescale_back(doc_inv, doc_unit, upstream) / doc_len
    doc_grad = jnp.concatenate([doc_grad, jnp.zeros_like(doc_grad)], axis=0)

    dq, d_mine, d_other = attend_back(info, q, mine, other, att, lse, doc_grad)

    got = swap_cores(d_other)
    paired = (d_mine.astype(jnp.float32) + got.astype(jnp.float32)).astype(jnp.bfloat16)
    low_terms = lax.all_to_all(paired[:HALF_CHUNKS], "x", 0, 0)
    low_sum = jnp.sum(low_terms.astype(jnp.float32), axis=0).astype(jnp.bfloat16)
    from_high = lax.ppermute(low_sum, "zhi", [(1, 0)])
    own_terms = lax.all_to_all(paired[HALF_CHUNKS:], "x", 0, 0)
    own_sum = jnp.sum(own_terms.astype(jnp.float32), axis=0)
    total = (own_sum + from_high.astype(jnp.float32)).astype(jnp.bfloat16)

    query_up = jnp.dot(coefficient, every_unit, precision=FULL_ACCURACY) / INVERSE_TEMPER
    query_grad = rescale_back(query_inv, query_unit, query_up)
    return (query_grad, dq[None], total[None, :, :KVW], total[None, :, KVW:])


def solution(mesh):
    fine = Mesh(mesh.devices.reshape(8, 4, 2, 4, 2), ("zlo", "y", "zhi", "x", "core"))
    dp, ctx = ("zlo", "y"), ("zhi", "x", "core")
    tokens = P(dp, ctx, None)
    return jax.shard_map(
        per_device,
        mesh=fine,
        in_specs=(tokens, tokens, tokens, P(dp, None), P(dp, None), P(dp)),
        out_specs=(P(dp, None), tokens, tokens, tokens),
        check_vma=False,
    )
```

time: 1130 us -> 232 us (0.21)
  the two profiles are of different devices: /device:TPU:8 before, /device:TPU:35 now
where the time goes in v1:
time: 232 us; the launch traced here: 230 us
  waiting for transfers between devices  69.8 us (30%)
  blocking collectives  63.1 us (27%)
  starting transfers between devices  55.3 us (24%)
  local copies, waits for them, and re-layouts  17 us (7%)
  other arithmetic  11.6 us (5%)
  Pallas kernels  8.2 us (4%)
  matrix products  4.54 us (2%)
    all_to_all x2, blocking collectives, to_all(): lax.all_to_all(jnp.broadcast_to(block[None], (count,) + block.shape), axe...  40.4 us
    all_to_all x3, waiting for transfers between devices, to_all(): lax.all_to_all(jnp.broadcast_to(block[None], (count,) + block.shape), axe...  22.5 us
    all_to_all x3, starting transfers between devices, to_all(): lax.all_to_all(jnp.broadcast_to(block[None], (count,) + block.shape), axe...  19.9 us
    ppermute x1, waiting for transfers between devices, per_device(): from_high = lax.ppermute(low_sum, 'zhi', [(1, 0)])  19.8 us
    ppermute x1, starting transfers between devices, per_device(): kv_low = lax.ppermute(kv, 'zhi', [(0, 1)])  14.5 us
    all_to_all x1, blocking collectives, per_device(): low_terms = lax.all_to_all(paired[:HALF_CHUNKS], 'x', 0, 0)  12.3 us
    all_to_all x1, waiting for transfers between devices, per_device(): terms = lax.all_to_all(terms.reshape(32, 7, 128), ('zlo', 'y'), 0, 0)  11.1 us
    ppermute x1, waiting for transfers between devices, per_device(): kv_low = lax.ppermute(kv, 'zhi', [(0, 1)])  10.5 us
  transfers between devices with their start and end apart: 9, of which 8 were waited for; matrix products, arithmetic and copies ran while one was open for 3% of the time, Pallas kernels for 0%

profile of v1, /device:TPU:35, one launch (start us, length us, event | category | flops | bytes accessed | tf_op | source)
XLA Modules:
  0.0 230.4 jit_solution(1733233161082029119)
XLA Ops:
  0.6 0.9 pad_maximum_fusion
  1.5 14.5 %collective-permute-start = (bf16[128,512]{1,0:T(8,128)(2,1)S(1)}, bf16[128,512]{1,0:T(8,128)(2,1)S(1)}, u32[]{:S(2)}, u32[]{:S(2)}) collective-permute-start(bf16[128,512]{1,0:T(8,128)(2,1)S(1)} %pad_maximum_fusion), channel_id=1, source_target_pairs={{0,8},{1,9},{2,10},{3,11},{4,12},{5,13},{6,14},{7,15},{16,24},{17,... | collective-permute-start | bytes 393224 | tf_op jit(solution)/shard_map/ppermute | solution.py:231
  16.1 10.5 %collective-permute-done = bf16[128,512]{1,0:T(8,128)(2,1)S(1)} collective-permute-done((bf16[128,512]{1,0:T(8,128)(2,1)S(1)}, bf16[128,512]{1,0:T(8,128)(2,1)S(1)}, u32[]{:S(2)}, u32[]{:S(2)}) %collective-permute-start) | collective-permute-done | bytes 131104 | tf_op jit(solution)/shard_map/ppermute | solution.py:231
  26.7 10.6 %all_to_all.45 = bf16[4,128,512]{2,1,0:T(8,128)(2,1)S(1)} all-to-all(bf16[4,128,512]{2,1,0:T(8,128)(2,1)S(1)} %broadcast_in_dim.16), channel_id=1, replica_groups=mesh['zlo'=8,'y'=4,'zhi'=2,'x'=4,'core'=2] {'x'}, dimensions={0} | all-to-all | bytes 1048576 | tf_op jit(solution)/shard_map/all_to_all | solution.py:209
  37.2 0.8 broadcast_in_dim.17
  38.1 4.6 %all-to-all-start.1 = ((bf16[4,128,512]{2,1,0:T(8,128)(2,1)}), bf16[4,128,512]{2,1,0:T(8,128)(2,1)S(1)}, u32[]{:S(2)}, u32[]{:S(2)}) async-start(bf16[4,128,512]{2,1,0:T(8,128)(2,1)} %broadcast_in_dim.17), calls=%async_computation.1 | async-start | bytes 1048576 | tf_op jit(solution)/shard_map/all_to_all | solution.py:209
  42.7 5.7 %all-to-all-done.1 = bf16[4,128,512]{2,1,0:T(8,128)(2,1)S(1)} async-done(((bf16[4,128,512]{2,1,0:T(8,128)(2,1)}), bf16[4,128,512]{2,1,0:T(8,128)(2,1)S(1)}, u32[]{:S(2)}, u32[]{:S(2)}) %all-to-all-start.1) | async-done | bytes 524320 | tf_op jit(solution)/shard_map/all_to_all | solution.py:209
  48.5 5.8 %collective-permute-start.1 = (bf16[8,128,512]{2,1,0:T(8,128)(2,1)S(1)}, bf16[8,128,512]{2,1,0:T(8,128)(2,1)S(1)}, u32[]{:S(2)}, u32[]{:S(2)}) collective-permute-start(bf16[8,128,512]{2,1,0:T(8,128)(2,1)S(1)} %constant_dynamic-update-slice_fusion.mine), channel_id=1, source_target_pairs={{0,1},{1,0},{2,3},{3,2},{4,5},{5,4},{6,7},{7,6},{8,9},{9,8},{10,11... | collective-permute-start | bytes 3145736 | tf_op jit(solution)/shard_map/ppermute | solution.py:213
  55.1 2.6 %stack.19.info = s32[8]{0:T(128)S(1)} concatenate(s32[1]{0:T(128)} %bitcast, s32[1]{0:T(128)} %bitcast.1, s32[1]{0:T(128)} %bitcast.2, s32[1]{0:T(128)} %bitcast.4, s32[1]{0:T(128)} %bitcast.5, s32[1]{0:T(128)} %bitcast.6, s32[1]{0:T(128)} %bitcast.7, s32[1]{0:T(128)} %bitcast.8), dimensions={0} | concatenate | bytes 64 | tf_op jit(solution)/shard_map/stack | solution.py:227
  57.7 3.8 %attend.1 = (f32[128,1792]{1,0:T(8,128)S(1)}, f32[8,1792]{1,0:T(8,128)S(1)}, f32[8,1792]{1,0:T(8,128)S(1)}) custom-call(s32[8]{0:T(128)S(1)} %stack.19.info, bf16[128,1792]{1,0:T(8,128)(2,1)S(1)} %bitcast.36, bf16[8,128,512]{2,1,0:T(8,128)(2,1)S(1)} %constant_dynamic-update-slice_fusion.mine, bf16[8,128,512]{2,1,0:T(8,128)(2,1)S(1)} %collective-permute-done.1.other), custom_call_target="tpu_custom_call" | custom-call | tf_op jit(solution)/shard_map/attend/pallas_call | solution.py:177
  61.5 0.7 slice_divide_fusion
  62.2 1.4 reshape.93
  63.6 10.4 %all_to_all.46 = f32[8,7,128]{2,1,0:T(8,128)} all-to-all(f32[8,7,128]{2,1,0:T(8,128)} %reshape.93), channel_id=1, replica_groups=mesh['zlo'=8,'y'=4,'zhi'=2,'x'=4,'core'=2] {'x','core'}, dimensions={0} | all-to-all | bytes 57344 | tf_op jit(solution)/shard_map/all_to_all | solution.py:241
  74.0 0.8 reduce_sum.85
  74.8 29.9 %all_to_all.47 = f32[16,7,128]{2,1,0:T(8,128)S(1)} all-to-all(f32[16,7,128]{2,1,0:T(8,128)S(1)} %broadcast_in_dim.18), channel_id=1, replica_groups=mesh['zlo'=8,'y'=4,'zhi'=2,'x'=4,'core'=2] {'zlo','zhi'}, dimensions={0} | all-to-all | bytes 114688 | tf_op jit(solution)/shard_map/all_to_all | solution.py:209
  104.7 1.0 broadcast_in_dim.19
  105.7 8.0 %all-to-all-start.4 = ((f32[32,8,7,128]{3,1,2,0:T(8,128)}), f32[32,8,7,128]{3,1,2,0:T(8,128)}, u32[]{:S(2)}, u32[]{:S(2)}) async-start(f32[32,8,7,128]{3,1,2,0:T(8,128)} %broadcast_in_dim.19), calls=%async_computation.4 | async-start | bytes 1835008 | tf_op jit(solution)/shard_map/all_to_all | solution.py:209
  113.6 1.2 fusion.1
  114.8 13.6 %all-to-all-done.4 = f32[32,8,7,128]{3,1,2,0:T(8,128)} async-done(((f32[32,8,7,128]{3,1,2,0:T(8,128)}), f32[32,8,7,128]{3,1,2,0:T(8,128)}, u32[]{:S(2)}, u32[]{:S(2)}) %all-to-all-start.4) | async-done | bytes 917536 | tf_op jit(solution)/shard_map/all_to_all | solution.py:209
  128.5 1.3 multiply_reduce_fusion.1
  129.8 1.7 copy.12
  131.5 1.0 copy.15
  133.0 0.8 copy.13
  134.5 1.4 broadcast_multiply_fusion
  135.9 1.1 fusion.11
  136.9 2.4 %convert_multiply_fusion = (f32[128,1792]{1,0:T(8,128)S(1)}, f32[128]{0:T(128)}, f32[128,1792]{1,0:T(8,128)}) fusion(bf16[128,1792]{1,0:T(8,128)(2,1)S(1)} %copy-done.2, f32[128]{0:T(128)S(1)} %add_rsqrt_fusion.1, f32[128,1792]{1,0:T(8,128)S(1)} %broadcast_multiply_fusion, s32[128]{0:T(128)S(1)} %copy-done.6, f32[128,128]{0,1:T(8,128)S(1)} %get-tuple-element.27, ...), kind=kOutput, calls=%fused_computation.2 | convolution fusion | flops 353533824 | bytes 3278848 | tf_op jit(solution)/shard_map/dot_general | solution.py:284
  139.4 1.0 convolution_multiply_fusion.1
  140.5 1.6 reshape.98
  142.0 4.8 %all-to-all-start.5 = ((f32[32,7,128]{2,1,0:T(8,128)}), f32[32,7,128]{2,1,0:T(8,128)}, u32[]{:S(2)}, u32[]{:S(2)}) async-start(f32[32,7,128]{2,1,0:T(8,128)} %reshape.98), calls=%async_computation.5 | async-start | bytes 262144 | tf_op jit(solution)/shard_map/all_to_all | solution.py:264
  147.5 11.1 %all-to-all-done.5 = f32[32,7,128]{2,1,0:T(8,128)} async-done(((f32[32,7,128]{2,1,0:T(8,128)}), f32[32,7,128]{2,1,0:T(8,128)}, u32[]{:S(2)}, u32[]{:S(2)}) %all-to-all-start.5) | async-done | bytes 114720 | tf_op jit(solution)/shard_map/all_to_all | solution.py:264
  158.6 0.9 reduce_sum.89
  160.1 7.3 %all-to-all-start.6 = ((f32[8,7,128]{2,1,0:T(8,128)}), f32[8,7,128]{2,1,0:T(8,128)}, u32[]{:S(2)}, u32[]{:S(2)}) async-start(f32[8,7,128]{2,1,0:T(8,128)} %broadcast_in_dim.20), calls=%async_computation.6 | async-start | bytes 65536 | tf_op jit(solution)/shard_map/all_to_all | solution.py:209
  167.5 0.7 fusion.8
  168.1 3.1 %all-to-all-done.6 = f32[8,7,128]{2,1,0:T(8,128)} async-done(((f32[8,7,128]{2,1,0:T(8,128)}), f32[8,7,128]{2,1,0:T(8,128)}, u32[]{:S(2)}, u32[]{:S(2)}) %all-to-all-start.6) | async-done | bytes 28704 | tf_op jit(solution)/shard_map/all_to_all | solution.py:209
  171.2 1.4 reshape.99
  172.6 1.0 multiply_reduce_fusion.2
  173.6 0.9 multiply_divide_fusion
  174.5 4.4 %attend_back.1 = (bf16[128,1792]{1,0:T(8,128)(2,1)}, bf16[8,128,512]{2,1,0:T(8,128)(2,1)S(1)}, bf16[8,128,512]{2,1,0:T(8,128)(2,1)S(1)}) custom-call(s32[8]{0:T(128)S(1)} %stack.19.info, bf16[128,1792]{1,0:T(8,128)(2,1)S(1)} %bitcast.37, bf16[8,128,512]{2,1,0:T(8,128)(2,1)S(1)} %constant_dynamic-update-slice_fusion.mine, ...), custom_call_target="tpu_custom_call" | custom-call | tf_op jit(solution)/shard_map/attend_back/pallas_call | solution.py:193
  178.9 4.3 %collective-permute-start.2 = (bf16[8,128,512]{2,1,0:T(8,128)(2,1)S(1)}, bf16[8,128,512]{2,1,0:T(8,128)(2,1)S(1)}, u32[]{:S(2)}, u32[]{:S(2)}) collective-permute-start(bf16[8,128,512]{2,1,0:T(8,128)(2,1)S(1)} %get-tuple-element.15), channel_id=1, source_target_pairs={{0,1},{1,0},{2,3},{3,2},{4,5},{5,4},{6,7},{7,6},{8,9},{9,8},{10,11... | collective-permute-start | bytes 3145736 | tf_op jit(solution)/shard_map/ppermute | solution.py:213
  183.2 2.3 collective-permute-done.2
  185.8 0.9 fusion.9
  186.6 12.3 %all_to_all.48 = bf16[4,128,512]{2,1,0:T(8,128)(2,1)S(1)} all-to-all(bf16[4,128,512]{2,1,0:T(8,128)(2,1)S(1)} %get-tuple-element.16), channel_id=1, replica_groups=mesh['zlo'=8,'y'=4,'zhi'=2,'x'=4,'core'=2] {'x'}, dimensions={0} | all-to-all | bytes 1048576 | tf_op jit(solution)/shard_map/all_to_all | solution.py:277
  199.0 4.6 %all-to-all-start.7 = ((bf16[4,128,512]{2,1,0:T(8,128)(2,1)}), bf16[4,128,512]{2,1,0:T(8,128)(2,1)S(1)}, u32[]{:S(2)}, u32[]{:S(2)}) async-start(bf16[4,128,512]{2,1,0:T(8,128)(2,1)} %get-tuple-element.17), calls=%async_computation.7 | async-start | bytes 1048576 | tf_op jit(solution)/shard_map/all_to_all | solution.py:280
  203.6 1.2 subtract_multiply_fusion
  204.9 1.3 collective-permute-start.3
  206.2 3.6 %all-to-all-done.7 = bf16[4,128,512]{2,1,0:T(8,128)(2,1)S(1)} async-done(((bf16[4,128,512]{2,1,0:T(8,128)(2,1)}), bf16[4,128,512]{2,1,0:T(8,128)(2,1)S(1)}, u32[]{:S(2)}, u32[]{:S(2)}) %all-to-all-start.7) | async-done | bytes 524320 | tf_op jit(solution)/shard_map/all_to_all | solution.py:280
  209.9 19.8 %collective-permute-done.3 = bf16[128,512]{1,0:T(8,128)(2,1)S(1)} collective-permute-done((bf16[128,512]{1,0:T(8,128)(2,1)S(1)}, bf16[128,512]{1,0:T(8,128)(2,1)S(1)}, u32[]{:S(2)}, u32[]{:S(2)}) %collective-permute-start.3) | collective-permute-done | bytes 131104 | tf_op jit(solution)/shard_map/ppermute | solution.py:279
  229.7 0.7 slice_bitcast_fusion
  (40 shorter events, 4.0 us)
Async XLA Ops:
  1.5 25.1 %collective-permute-start = (bf16[128,512]{1,0:T(8,128)(2,1)S(1)}, bf16[128,512]{1,0:T(8,128)(2,1)S(1)}, u32[]{:S(2)}, u32[]{:S(2)}) collective-permute-start(bf16[128,512]{1,0:T(8,128)(2,1)S(1)} %pad_maximum_fusion), channel_id=1, source_target_pairs={{0,8},{1,9},{2,10},{3,11},{4,12},{5,13},{6,14},{7,15},{16,24},{17,... | collective-permute-start | bytes 393224 | tf_op jit(solution)/shard_map/ppermute | solution.py:231
  38.1 10.4 %all-to-all-start.1 = ((bf16[4,128,512]{2,1,0:T(8,128)(2,1)}), bf16[4,128,512]{2,1,0:T(8,128)(2,1)S(1)}, u32[]{:S(2)}, u32[]{:S(2)}) async-start(bf16[4,128,512]{2,1,0:T(8,128)(2,1)} %broadcast_in_dim.17), calls=%async_computation.1 | async-start | bytes 1048576 | tf_op jit(solution)/shard_map/all_to_all | solution.py:209
  42.7 11.6 %copy-start.8 = (s32[1,4]{1,0:T(1,128)S(1)}, s32[1,4]{1,0:T(1,128)}, u32[]{:S(2)}) copy-start(s32[1,4]{1,0:T(1,128)} %param.9) | copy-start | bytes 52
  42.7 15.0 %copy-start = (bf16[1,128,1792]{2,1,0:T(8,128)(2,1)S(1)}, bf16[1,128,1792]{2,1,0:T(8,128)(2,1)}, u32[]{:S(2)}) copy-start(bf16[1,128,1792]{2,1,0:T(8,128)(2,1)} %param.6) | copy-start | bytes 1376260
  48.5 9.2 %collective-permute-start.1 = (bf16[8,128,512]{2,1,0:T(8,128)(2,1)S(1)}, bf16[8,128,512]{2,1,0:T(8,128)(2,1)S(1)}, u32[]{:S(2)}, u32[]{:S(2)}) collective-permute-start(bf16[8,128,512]{2,1,0:T(8,128)(2,1)S(1)} %constant_dynamic-update-slice_fusion.mine), channel_id=1, source_target_pairs={{0,1},{1,0},{2,3},{3,2},{4,5},{5,4},{6,7},{7,6},{8,9},{9,8},{10,11... | collective-permute-start | bytes 3145736 | tf_op jit(solution)/shard_map/ppermute | solution.py:213
  57.7 3.8 %copy-start.5 = (f32[4]{0:T(128)}, f32[4]{0:T(128)S(1)}, u32[]{:S(2)}) copy-start(f32[4]{0:T(128)S(1)} %convert_bitcast_fusion) | copy-start | bytes 52
  105.7 22.8 %all-to-all-start.4 = ((f32[32,8,7,128]{3,1,2,0:T(8,128)}), f32[32,8,7,128]{3,1,2,0:T(8,128)}, u32[]{:S(2)}, u32[]{:S(2)}) async-start(f32[32,8,7,128]{3,1,2,0:T(8,128)} %broadcast_in_dim.19), calls=%async_computation.4 | async-start | bytes 1835008 | tf_op jit(solution)/shard_map/all_to_all | solution.py:209
  134.5 1.4 copy-start.2
  135.8 3.6 %copy-start.1 = (f32[128,1792]{1,0:T(8,128)}, f32[128,1792]{1,0:T(8,128)S(1)}, u32[]{:S(2)}) copy-start(f32[128,1792]{1,0:T(8,128)S(1)} %broadcast_multiply_fusion) | copy-start | bytes 2752516
  135.8 1.1 copy-start.6
  142.0 16.5 %all-to-all-start.5 = ((f32[32,7,128]{2,1,0:T(8,128)}), f32[32,7,128]{2,1,0:T(8,128)}, u32[]{:S(2)}, u32[]{:S(2)}) async-start(f32[32,7,128]{2,1,0:T(8,128)} %reshape.98), calls=%async_computation.5 | async-start | bytes 262144 | tf_op jit(solution)/shard_map/all_to_all | solution.py:264
  160.1 11.1 %all-to-all-start.6 = ((f32[8,7,128]{2,1,0:T(8,128)}), f32[8,7,128]{2,1,0:T(8,128)}, u32[]{:S(2)}, u32[]{:S(2)}) async-start(f32[8,7,128]{2,1,0:T(8,128)} %broadcast_in_dim.20), calls=%async_computation.6 | async-start | bytes 65536 | tf_op jit(solution)/shard_map/all_to_all | solution.py:209
  178.9 6.6 %collective-permute-start.2 = (bf16[8,128,512]{2,1,0:T(8,128)(2,1)S(1)}, bf16[8,128,512]{2,1,0:T(8,128)(2,1)S(1)}, u32[]{:S(2)}, u32[]{:S(2)}) collective-permute-start(bf16[8,128,512]{2,1,0:T(8,128)(2,1)S(1)} %get-tuple-element.15), channel_id=1, source_target_pairs={{0,1},{1,0},{2,3},{3,2},{4,5},{5,4},{6,7},{7,6},{8,9},{9,8},{10,11... | collective-permute-start | bytes 3145736 | tf_op jit(solution)/shard_map/ppermute | solution.py:213
  186.6 17.0 %copy-start.3 = (bf16[128,1792]{1,0:T(8,128)(2,1)S(1)}, bf16[128,1792]{1,0:T(8,128)(2,1)}, u32[]{:S(2)}) copy-start(bf16[128,1792]{1,0:T(8,128)(2,1)} %param.10) | copy-start | bytes 1376260
  186.6 17.0 %copy-start.4 = (f32[128,1792]{1,0:T(8,128)S(1)}, f32[128,1792]{1,0:T(8,128)}, u32[]{:S(2)}) copy-start(f32[128,1792]{1,0:T(8,128)} %get-tuple-element.28) | copy-start | bytes 2752516
  186.6 17.0 %copy-start.7 = (f32[128]{0:T(128)S(1)}, f32[128]{0:T(128)}, u32[]{:S(2)}) copy-start(f32[128]{0:T(128)} %get-tuple-element.19) | copy-start | bytes 1540
  199.0 10.8 %all-to-all-start.7 = ((bf16[4,128,512]{2,1,0:T(8,128)(2,1)}), bf16[4,128,512]{2,1,0:T(8,128)(2,1)S(1)}, u32[]{:S(2)}, u32[]{:S(2)}) async-start(bf16[4,128,512]{2,1,0:T(8,128)(2,1)} %get-tuple-element.17), calls=%async_computation.7 | async-start | bytes 1048576 | tf_op jit(solution)/shard_map/all_to_all | solution.py:280
  204.9 24.8 %collective-permute-start.3 = (bf16[128,512]{1,0:T(8,128)(2,1)S(1)}, bf16[128,512]{1,0:T(8,128)(2,1)S(1)}, u32[]{:S(2)}, u32[]{:S(2)}) collective-permute-start(bf16[128,512]{1,0:T(8,128)(2,1)S(1)} %reduce_sum.92), channel_id=1, source_target_pairs={{8,0},{9,1},{10,2},{11,3},{12,4},{13,5},{14,6},{15,7},{24,16},{25,... | collective-permute-start | bytes 393224 | tf_op jit(solution)/shard_map/ppermute | solution.py:279

commit v2 on v1

v2 whole, which is shorter than its diff:
```python
import jax
import jax.numpy as jnp
from jax import lax
from jax.experimental import pallas as pl
from jax.experimental.pallas import tpu as pltpu
from jax.sharding import Mesh
from jax.sharding import PartitionSpec as P

HEAD_DIM = 128
HEADS = 14
KV_HEADS = 2
PER_GROUP = HEADS // KV_HEADS
DOCS = 4
TOK = 128
SEQ = 2048
EMB = HEADS * HEAD_DIM
KVW = KV_HEADS * HEAD_DIM
GROUP_W = PER_GROUP * TOK
CHUNK = 2 * TOK
HALF = SEQ // 2
CHUNKS = HALF // CHUNK
PIECE = EMB // 2
NDOC = 128

FACTOR = HEAD_DIM ** (-0.5)
INVERSE_TEMPER = 0.05
EPSILON = 1e-06
FULL_ACCURACY = lax.Precision.HIGHEST
MASKED = -1e30
TINY = 1e-30
NT = (((1,), (1,)), ((), ()))
TN = (((0,), (0,)), ((), ()))
NN = (((1,), (0,)), ((), ()))
NEAR = ("x", "core")
VMEM_BYTES = 40 * 1024 * 1024


def mm(a, b, dims, precision=None):
    return lax.dot_general(a, b, dims, precision=precision, preferred_element_type=jnp.float32)


def place():
    return tuple(lax.axis_index(axis) for axis in ("zlo", "y", "zhi", "x", "core"))


class Row:
    def __init__(self, lengths):
        _, _, self.high, x, self.core = place()
        self.first = ((self.high * 4 + x) * 2 + self.core) * TOK
        self.lengths = [lengths[0, d] for d in range(DOCS)]
        qpos = self.first + lax.broadcasted_iota(jnp.int32, (1, TOK), 1)
        start = jnp.zeros((1, TOK), jnp.int32)
        doc = jnp.zeros((1, TOK), jnp.int32)
        first_start = jnp.int32(0)
        end = jnp.int32(0)
        for d in range(DOCS - 1):
            end = end + self.lengths[d]
            start = jnp.where(qpos >= end, end, start)
            doc = doc + (qpos >= end).astype(jnp.int32)
            first_start = jnp.where(self.first >= end, end, first_start)
        self.qpos, self.start = qpos, start
        self.member = (lax.broadcasted_iota(jnp.int32, (8, TOK), 0) == doc).astype(jnp.float32)
        own_base = self.high * HALF
        self.own = (
            own_base,
            lax.div(jnp.maximum(first_start - own_base, 0), CHUNK),
            lax.div(self.first + (TOK - 1) - own_base, CHUNK) + 1,
        )
        self.low = (jnp.int32(0), lax.div(first_start, CHUNK), CHUNKS * self.high)

    def length_column(self):
        rows = lax.broadcasted_iota(jnp.int32, (8, 1), 0)
        column = jnp.ones((8, 1), jnp.float32)
        for d in range(DOCS):
            column = jnp.where(rows == d, self.lengths[d].astype(jnp.float32), column)
        return column

    def bias(self, base, chunk, split):
        at = lax.broadcasted_iota(jnp.int32, (CHUNK, TOK), 0)
        if split:
            half = lax.div(at, TOK)
            turned = jnp.where(self.core == 1, 1 - half, half)
            at = turned * TOK + (at - half * TOK)
        pos = base + chunk * CHUNK + at
        allowed = (pos >= self.start) & (pos <= self.qpos)
        one = jnp.where(allowed, 0.0, MASKED).astype(jnp.float32)
        return jnp.concatenate([one] * PER_GROUP, axis=1)


def chunk_of(kv, chunk, column):
    at = slice(column * HEAD_DIM, (column + 1) * HEAD_DIM)
    if len(kv) == 1:
        return kv[0][chunk, :, at]
    return jnp.concatenate([half[chunk, :, at] for half in kv], axis=0)


def put_chunk(refs, chunk, column, rows):
    at = slice(column * HEAD_DIM, (column + 1) * HEAD_DIM)
    if len(refs) == 1:
        refs[0][chunk, :, at] = rows
    else:
        refs[0][chunk, :, at] = rows[:TOK]
        refs[1][chunk, :, at] = rows[TOK:]


def head_rows(ref, group):
    return jnp.concatenate(
        [
            ref[:, (group * PER_GROUP + h) * HEAD_DIM : (group * PER_GROUP + h + 1) * HEAD_DIM]
            for h in range(PER_GROUP)
        ],
        axis=0,
    )


def head_columns(group, h):
    at = (group * PER_GROUP + h) * HEAD_DIM
    return slice(at, at + HEAD_DIM)


def part_attention(row, part, group, q, kv, held, out):
    base, low, high = part
    q_rows = head_rows(q, group)

    def score_step(chunk, top):
        scores = mm(chunk_of(kv, chunk, group), q_rows, NT) * FACTOR
        scores = scores + row.bias(base, chunk, len(kv) > 1)
        held[chunk] = scores
        return jnp.maximum(top, jnp.max(scores, axis=0, keepdims=True))

    top = lax.fori_loop(low, high, score_step, jnp.full((1, GROUP_W), MASKED, jnp.float32))

    def total_step(chunk, total):
        exps = jnp.exp(held[chunk] - top)
        held[chunk] = exps
        return total + jnp.sum(exps, axis=0, keepdims=True)

    total = lax.fori_loop(low, high, total_step, jnp.zeros((1, GROUP_W), jnp.float32))
    total = jnp.maximum(total, TINY)
    inverse = 1.0 / total
    out[...] = jnp.zeros((HEAD_DIM, GROUP_W), jnp.float32)

    def out_step(chunk, carry):
        weights = (held[chunk] * inverse).astype(jnp.bfloat16)
        out[...] += mm(chunk_of(kv, chunk, KV_HEADS + group), weights, TN)
        return carry

    lax.fori_loop(low, high, out_step, 0)
    return top + jnp.log(total)


def attend_own_kernel(lengths, q, kv, att, lse, held, out):
    row = Row(lengths)
    for group in range(KV_HEADS):
        columns = slice(group * GROUP_W, (group + 1) * GROUP_W)
        log_total = part_attention(row, row.own, group, q, (kv,), held, out)
        att[:, columns] = out[...]
        lse[:, columns] = jnp.broadcast_to(log_total, (8, GROUP_W))


def attend_low_kernel(
    lengths, q, mine, other, own_att, own_lse, att, lse, pieces, held, out, doc_sum
):
    row = Row(lengths)
    for group in range(KV_HEADS):
        columns = slice(group * GROUP_W, (group + 1) * GROUP_W)
        low_total = part_attention(row, row.low, group, q, (mine, other), held, out)
        own_total = own_lse[0:1, columns]
        top = jnp.maximum(low_total, own_total)
        log_total = top + jnp.log(jnp.exp(low_total - top) + jnp.exp(own_total - top))
        att[:, columns] = own_att[:, columns] * jnp.exp(own_total - log_total) + out[
            ...
        ] * jnp.exp(low_total - log_total)
        lse[:, columns] = jnp.broadcast_to(log_total, (8, GROUP_W))
        for h in range(PER_GROUP):
            at = head_columns(group, h)
            doc_sum[:, at] = mm(row.member, att[:, at], NT, FULL_ACCURACY)
    mean = doc_sum[...] / row.length_column()
    for d in range(DOCS):
        for c in range(2):
            pieces[2 * d + c] = mean[d : d + 1, c * PIECE : (c + 1) * PIECE]


def contrast_kernel(q, positive, docs_mine, docs_other, coefficient, terms, own_docs):
    z_lo, y, _, x, core = place()
    d_mine, d_other = docs_mine[...], docs_other[...]
    doc_inv = lax.rsqrt(
        jnp.sum(d_mine * d_mine, axis=1, keepdims=True)
        + jnp.sum(d_other * d_other, axis=1, keepdims=True)
        + EPSILON
    )
    q_all = q[...].astype(jnp.float32)
    query_inv = lax.rsqrt(jnp.sum(q_all * q_all, axis=1, keepdims=True) + EPSILON)
    q_unit = q_all * query_inv
    q_mine = jnp.where(core == 1, q_unit[:, PIECE:], q_unit[:, :PIECE])
    q_other = jnp.where(core == 1, q_unit[:, :PIECE], q_unit[:, PIECE:])
    logits = mm(d_mine * doc_inv, q_mine, NT, FULL_ACCURACY)
    logits = (logits + mm(d_other * doc_inv, q_other, NT, FULL_ACCURACY)) / INVERSE_TEMPER
    exps = jnp.exp(logits)
    at = lax.broadcasted_iota(jnp.int32, (NDOC, 128), 0)
    doc = ((at % 8) * 4 + at // 32) * DOCS + (at // 8) % 4
    target = (doc == positive[...]).astype(jnp.float32)
    coefficient[...] = exps / jnp.sum(exps, axis=0, keepdims=True) - target
    near = jnp.concatenate(
        [coefficient[pl.ds(pl.multiple_of(b * 32 + x * 8, 8), 8), :] for b in range(4)], axis=0
    )
    near_terms = mm(near, q_mine, NN, FULL_ACCURACY) / INVERSE_TEMPER
    for r in range(32):
        terms[r] = near_terms[r : r + 1]
    own_docs[...] = jnp.zeros((8, EMB), jnp.float32)
    for d in range(DOCS):
        r = y * 32 + d * 8 + z_lo
        a, b = docs_mine[pl.ds(r, 1), :], docs_other[pl.ds(r, 1), :]
        own_docs[d : d + 1, :PIECE] = jnp.where(core == 1, b, a)
        own_docs[d : d + 1, PIECE:] = jnp.where(core == 1, a, b)


def query_kernel(q, docs_mine, docs_other, coefficient, query_grad):
    _, _, _, _, core = place()
    d_mine, d_other = docs_mine[...], docs_other[...]
    doc_inv = lax.rsqrt(
        jnp.sum(d_mine * d_mine, axis=1, keepdims=True)
        + jnp.sum(d_other * d_other, axis=1, keepdims=True)
        + EPSILON
    )
    scaled = coefficient[...] * doc_inv
    u_mine = mm(scaled, d_mine, TN, FULL_ACCURACY) / INVERSE_TEMPER
    u_other = mm(scaled, d_other, TN, FULL_ACCURACY) / INVERSE_TEMPER
    u_left = jnp.where(core == 1, u_other, u_mine)
    u_right = jnp.where(core == 1, u_mine, u_other)
    q_all = q[...].astype(jnp.float32)
    query_inv = lax.rsqrt(jnp.sum(q_all * q_all, axis=1, keepdims=True) + EPSILON)
    q_unit = q_all * query_inv
    q_left, q_right = q_unit[:, :PIECE], q_unit[:, PIECE:]
    inner = jnp.sum(q_left * u_left, axis=1, keepdims=True) + jnp.sum(
        q_right * u_right, axis=1, keepdims=True
    )
    query_grad[:, :PIECE] = query_inv * (u_left - q_left * inner)
    query_grad[:, PIECE:] = query_inv * (u_right - q_right * inner)


def back_part(row, part, group, q, kv, log_total, out_rows, delta, dq, d_kv):
    base, low, high = part
    q_rows = head_rows(q, group)

    def step(chunk, carry):
        k_rows = chunk_of(kv, chunk, group)
        v_rows = chunk_of(kv, chunk, KV_HEADS + group)
        scores = mm(k_rows, q_rows, NT) * FACTOR + row.bias(base, chunk, len(kv) > 1)
        probs = jnp.exp(scores - log_total)
        flow = mm(v_rows, out_rows, NT)
        score_grad = (probs * (flow - delta)).astype(jnp.bfloat16)
        dq[...] += mm(k_rows, score_grad, TN)
        k_part = (mm(score_grad, q_rows, NN) * FACTOR).astype(jnp.bfloat16)
        v_part = mm(probs.astype(jnp.bfloat16), out_rows, NN).astype(jnp.bfloat16)
        put_chunk(d_kv, chunk, group, k_part)
        put_chunk(d_kv, chunk, KV_HEADS + group, v_part)
        return carry

    lax.fori_loop(low, high, step, 0)


def back_low_kernel(
    lengths,
    q,
    mine,
    other,
    att,
    lse,
    own_docs,
    upstream,
    out_low,
    delta,
    dq_low,
    d_mine,
    d_other,
    dq,
):
    row = Row(lengths)
    d_mine[...] = jnp.zeros(d_mine.shape, d_mine.dtype)
    d_other[...] = jnp.zeros(d_other.shape, d_other.dtype)
    w = jnp.concatenate(
        [
            jnp.concatenate([upstream[2 * d + c] for d in range(DOCS)] * 2, axis=0)
            for c in range(2)
        ],
        axis=1,
    )
    docs = own_docs[...]
    doc_inv = lax.rsqrt(jnp.sum(docs * docs, axis=1, keepdims=True) + EPSILON)
    unit = docs * doc_inv
    inner = jnp.sum(unit * w, axis=1, keepdims=True)
    doc_grad = doc_inv * (w - unit * inner) / row.length_column()
    low_grad = doc_grad.astype(jnp.bfloat16)
    member_low = row.member.astype(jnp.bfloat16)
    out_low[...] = mm(member_low, low_grad, TN).astype(jnp.bfloat16)
    for group in range(KV_HEADS):
        columns = slice(group * GROUP_W, (group + 1) * GROUP_W)
        for h in range(PER_GROUP):
            at = head_columns(group, h)
            by_doc = mm(doc_grad[:, at], att[:, at], NN, FULL_ACCURACY)
            one = jnp.sum(row.member * by_doc, axis=0, keepdims=True)
            delta[:, at] = jnp.broadcast_to(one, (8, TOK))
        dq[...] = jnp.zeros(dq.shape, jnp.float32)
        back_part(
            row,
            row.low,
            group,
            q,
            (mine, other),
            lse[0:1, columns],
            head_rows(out_low, group),
            delta[0:1, columns],
            dq,
            (d_mine, d_other),
        )
        dq_low[:, columns] = dq[...]


def back_own_kernel(lengths, q, kv, lse, out_low, delta, dq_low, grad_q, d_kv, dq):
    row = Row(lengths)
    d_kv[...] = jnp.zeros(d_kv.shape, d_kv.dtype)
    for group in range(KV_HEADS):
        columns = slice(group * GROUP_W, (group + 1) * GROUP_W)
        dq[...] = dq_low[:, columns]
        back_part(
            row,
            row.own,
            group,
            q,
            (kv,),
            lse[0:1, columns],
            head_rows(out_low, group),
            delta[0:1, columns],
            dq,
            (d_kv,),
        )
        for h in range(PER_GROUP):
            block = dq[:, h * TOK : (h + 1) * TOK]
            grad_q[:, head_columns(group, h)] = (block.T * FACTOR).astype(jnp.bfloat16)


F32, BF16 = jnp.float32, jnp.bfloat16


def shape(dims, dtype):
    return jax.ShapeDtypeStruct(dims, dtype)


def run(kernel, name, outs, scratch, lengths, *arrays, flops=0):
    vmem = pl.BlockSpec(memory_space=pltpu.VMEM)
    smem = pl.BlockSpec(memory_space=pltpu.SMEM)
    first = () if lengths is None else (lengths,)
    return pl.pallas_call(
        kernel,
        out_shape=outs,
        in_specs=[smem] * len(first) + [vmem] * len(arrays),
        out_specs=tuple(vmem for _ in outs),
        scratch_shapes=scratch,
        compiler_params=pltpu.CompilerParams(vmem_limit_bytes=VMEM_BYTES),
        cost_estimate=pl.CostEstimate(flops=flops, bytes_accessed=0, transcendentals=0),
        name=name,
    )(*first, *arrays)


TERMS = shape((CHUNKS, TOK, 2 * KVW), BF16)
HELD = pltpu.VMEM((CHUNKS, CHUNK, GROUP_W), F32)
WIDE = pltpu.VMEM((HEAD_DIM, GROUP_W), F32)


def attend_own(lengths, *arrays):
    outs = (shape((HEAD_DIM, EMB), F32), shape((8, EMB), F32))
    return run(attend_own_kernel, "attend_own", outs, [HELD, WIDE], lengths, *arrays)


def attend_low(lengths, *arrays):
    outs = (shape((HEAD_DIM, EMB), F32), shape((8, EMB), F32), shape((8, 1, PIECE), F32))
    scratch = [HELD, WIDE, pltpu.VMEM((8, EMB), F32)]
    return run(attend_low_kernel, "attend_low", outs, scratch, lengths, *arrays)


def contrast(*arrays):
    outs = (shape((NDOC, 128), F32), shape((32, 1, PIECE), F32), shape((8, EMB), F32))
    return run(contrast_kernel, "contrast", outs, [], None, *arrays)


def query_back(*arrays):
    return run(query_kernel, "query_back", (shape((128, EMB), F32),), [], None, *arrays)[0]


def back_low(lengths, *arrays):
    outs = (
        shape((TOK, EMB), BF16),
        shape((8, EMB), F32),
        shape((HEAD_DIM, EMB), F32),
        TERMS,
        TERMS,
    )
    return run(back_low_kernel, "back_low", outs, [WIDE], lengths, *arrays)


def back_own(lengths, *arrays):
    outs = (shape((TOK, EMB), BF16), shape((CHUNKS, CHUNK, 2 * KVW), BF16))
    return run(back_own_kernel, "back_own", outs, [WIDE], lengths, *arrays)


def to_all(block, axes, count):
    return lax.all_to_all(jnp.broadcast_to(block[None], (count,) + block.shape), axes, 0, 0)


def swap_cores(block):
    return lax.ppermute(block, "core", [(0, 1), (1, 0)])


def per_device(queries_q, keys, values, lengths, query_emb, positive):
    q = queries_q[0]
    kv = jnp.concatenate([keys[0], values[0]], axis=1)
    kv_low = lax.ppermute(kv, "zhi", [(0, 1)])
    own_kv = to_all(kv, NEAR, 8).reshape(CHUNKS, CHUNK, 2 * KVW)
    own_att, own_lse = attend_own(lengths, q, own_kv)
    kv_low, own_att = lax.optimization_barrier((kv_low, own_att))
    low_mine = to_all(kv_low, "x", 4)
    low_other = swap_cores(low_mine)
    att, lse, pieces = attend_low(lengths, q, low_mine, low_other, own_att, own_lse)

    part = jnp.sum(lax.all_to_all(pieces, NEAR, 0, 0), axis=0)
    column = to_all(part, ("zlo", "zhi"), 16).reshape(8, 2, PIECE)
    column = column[:, 0] + column[:, 1]
    docs_mine = to_all(column, ("y", "x"), 16).reshape(NDOC, PIECE)
    docs_other = swap_cores(docs_mine)

    coefficient, terms, own_docs = contrast(
        query_emb, positive.reshape(1, 128), docs_mine, docs_other
    )
    terms = jnp.sum(lax.all_to_all(terms, ("y", "zlo"), 0, 0), axis=0)
    upstream = to_all(terms, NEAR, 8)

    out_low, delta, dq_low, d_mine, d_other = back_low(
        lengths, q, low_mine, low_other, att, lse, own_docs, upstream
    )
    got = swap_cores(d_other)
    grad_q, own_d = back_own(lengths, q, own_kv, lse, out_low, delta, dq_low)
    own_d, got = lax.optimization_barrier((own_d, got))
    paired = (d_mine.astype(F32) + got.astype(F32)).astype(BF16)
    low_terms = lax.all_to_all(paired, "x", 0, 0)
    low_sum = jnp.sum(low_terms.astype(F32), axis=0).astype(BF16)
    low_sum, own_d = lax.optimization_barrier((low_sum, own_d))
    from_high = lax.ppermute(low_sum, "zhi", [(1, 0)])
    own_terms = lax.all_to_all(own_d.reshape(8, TOK, 2 * KVW), NEAR, 0, 0)
    own_sum = jnp.sum(own_terms.astype(F32), axis=0)
    coefficient, low_sum = lax.optimization_barrier((coefficient, low_sum))
    query_grad = query_back(query_emb, docs_mine, docs_other, coefficient)
    query_grad, from_high = lax.optimization_barrier((query_grad, from_high))
    total = (own_sum + from_high.astype(F32)).astype(BF16)
    return (query_grad, grad_q[None], total[None, :, :KVW], total[None, :, KVW:])


def solution(mesh):
    fine = Mesh(mesh.devices.reshape(8, 4, 2, 4, 2), ("zlo", "y", "zhi", "x", "core"))
    dp, ctx = ("zlo", "y"), ("zhi", "x", "core")
    tokens = P(dp, ctx, None)
    return jax.shard_map(
        per_device,
        mesh=fine,
        in_specs=(tokens, tokens, tokens, P(dp, None), P(dp, None), P(dp)),
        out_specs=(P(dp, None), tokens, tokens, tokens),
        check_vma=False,
    )
```

time: 232 us -> 198 us (0.85)
  waiting for transfers between devices: 69.8 us -> 30.3 us
  blocking collectives: 63.1 us -> 100 us
  starting transfers between devices: 55.3 us -> 39.4 us
  local copies, waits for them, and re-layouts: 17 us -> 6.87 us
  other arithmetic: 11.6 us -> 2.47 us
  Pallas kernels: 8.2 us -> 17.2 us
  matrix products: 4.54 us -> 0 us
    all_to_all x3 -> x1, waiting for transfers between devices: 22.5 us -> 0.01 us  [to_all(): lax.all_to_all(jnp.broadcast_to(block[None], (count,) + block.shape), axe...]
    all_to_all x2 -> x4, blocking collectives: 40.4 us -> 62.7 us  [to_all(): lax.all_to_all(jnp.broadcast_to(block[None], (count,) + block.shape), axe...]
    all_to_all x2 -> x3, blocking collectives: 22.7 us -> 37.7 us  [the longest x1 15.5 us: per_device(): terms = jnp.sum(lax.all_to_all(terms, ('y', 'zlo'), 0, 0), axis=0)]
    all_to_all x2 -> x1, waiting for transfers between devices: 14.7 us -> 0.01 us  [per_device(): own_terms = lax.all_to_all(own_d.reshape(8, TOK, 2 * KVW), NEAR, 0, 0)]
    all_to_all x3 -> x1, starting transfers between devices: 19.9 us -> 5.28 us  [to_all(): lax.all_to_all(jnp.broadcast_to(block[None], (count,) + block.shape), axe...]
    pallas_call x2 -> x6, Pallas kernels: 8.2 us -> 17.2 us  [run(): pl.pallas_call(kernel, out_shape=outs, in_specs=[smem] * len(first) + [vm...]
    dot_general x3 -> x0, matrix products: 4.54 us -> none  [the longest x1 2.44 us: per_device(): jnp.dot(coefficient, every_unit, precision=FULL_ACCURACY) / INVERSE_TEMPER]
    reshape x3 -> x1, local copies, waits for them, and re-layouts: 4.33 us -> 0.04 us  [per_device(): column = to_all(part, ('zlo', 'zhi'), 16).reshape(8, 2, PIECE)]
  transfers between devices with their start and end apart: 9 -> 7, of which waited for: 8 -> 4; matrix products, arithmetic and copies ran while one was open for 3% -> 0% of each run, Pallas kernels for 0% -> 6%
where the time goes in v2:
time: 198 us; the launch traced here: 197 us
  blocking collectives  100 us (51%)
  starting transfers between devices  39.4 us (20%)
  waiting for transfers between devices  30.3 us (15%)
  Pallas kernels  17.2 us (9%)
  local copies, waits for them, and re-layouts  6.87 us (3%)
  other arithmetic  2.47 us (1%)
    all_to_all x4, blocking collectives, to_all(): lax.all_to_all(jnp.broadcast_to(block[None], (count,) + block.shape), axe...  62.7 us
    ppermute x1, waiting for transfers between devices, per_device(): from_high = lax.ppermute(low_sum, 'zhi', [(1, 0)])  20 us
    pallas_call x6, Pallas kernels, run(): pl.pallas_call(kernel, out_shape=outs, in_specs=[smem] * len(first) + [vm...  17.2 us
    all_to_all x1, blocking collectives, per_device(): terms = jnp.sum(lax.all_to_all(terms, ('y', 'zlo'), 0, 0), axis=0)  15.5 us
    all_to_all x1, blocking collectives, per_device(): low_terms = lax.all_to_all(paired, 'x', 0, 0)  14.6 us
    ppermute x1, starting transfers between devices, per_device(): kv_low = lax.ppermute(kv, 'zhi', [(0, 1)])  14.5 us
    ppermute x3, starting transfers between devices, swap_cores(): return lax.ppermute(block, 'core', [(0, 1), (1, 0)])  12.5 us
    all_to_all x1, blocking collectives, per_device(): part = jnp.sum(lax.all_to_all(pieces, NEAR, 0, 0), axis=0)  7.55 us
  transfers between devices with their start and end apart: 7, of which 4 were waited for; matrix products, arithmetic and copies ran while one was open for 0% of the time, Pallas kernels for 6%

profile of v2, /device:TPU:35, one launch (start us, length us, event | category | flops | bytes accessed | tf_op | source)
XLA Modules:
  0.0 197.4 jit_solution(14940557140553748793)
XLA Ops:
  0.6 0.9 pad_maximum_fusion
  1.5 1.1 broadcast_in_dim.16
  2.6 5.3 %all-to-all-start = ((bf16[8,128,512]{2,1,0:T(8,128)(2,1)}), bf16[8,128,512]{2,1,0:T(8,128)(2,1)S(1)}, u32[]{:S(2)}, u32[]{:S(2)}) async-start(bf16[8,128,512]{2,1,0:T(8,128)(2,1)} %broadcast_in_dim.16), calls=%async_computation | async-start | bytes 2097152 | tf_op jit(solution)/shard_map/all_to_all | solution.py:408
  7.9 14.5 %collective-permute-start = (bf16[128,512]{1,0:T(8,128)(2,1)S(1)}, bf16[128,512]{1,0:T(8,128)(2,1)S(1)}, u32[]{:S(2)}, u32[]{:S(2)}) collective-permute-start(bf16[128,512]{1,0:T(8,128)(2,1)S(1)} %pad_maximum_fusion), channel_id=1, source_target_pairs={{0,8},{1,9},{2,10},{3,11},{4,12},{5,13},{6,14},{7,15},{16,24},{17,... | collective-permute-start | bytes 393224 | tf_op jit(solution)/shard_map/ppermute | solution.py:418
  22.4 0.0 all-to-all-done
  22.4 0.0 copy-done
  22.4 0.0 copy-done.10
  22.4 3.5 %attend_own.1 = (f32[128,1792]{1,0:T(8,128)S(1)}, f32[8,1792]{1,0:T(8,128)S(1)}) custom-call(s32[1,4]{1,0:T(1,128)S(1)} %copy-done.10, bf16[128,1792]{1,0:T(8,128)(2,1)S(1)} %bitcast.17, bf16[4,256,512]{2,1,0:T(8,128)(2,1)S(1)} %bitcast.15), custom_call_target="tpu_custom_call" | custom-call | tf_op jit(solution)/shard_map/attend_own/pallas_call | solution.py:354
  26.0 7.4 %collective-permute-done = bf16[128,512]{1,0:T(8,128)(2,1)S(1)} collective-permute-done((bf16[128,512]{1,0:T(8,128)(2,1)S(1)}, bf16[128,512]{1,0:T(8,128)(2,1)S(1)}, u32[]{:S(2)}, u32[]{:S(2)}) %collective-permute-start) | collective-permute-done | bytes 131104 | tf_op jit(solution)/shard_map/ppermute | solution.py:418
  33.4 10.7 %all_to_all.45.mine = bf16[4,128,512]{2,1,0:T(8,128)(2,1)S(1)} all-to-all(bf16[4,128,512]{2,1,0:T(8,128)(2,1)S(1)} %broadcast_in_dim.17), channel_id=1, replica_groups=mesh['zlo'=8,'y'=4,'zhi'=2,'x'=4,'core'=2] {'x'}, dimensions={0} | all-to-all | bytes 1048576 | tf_op jit(solution)/shard_map/all_to_all | solution.py:408
  44.0 4.5 %collective-permute-start.1 = (bf16[4,128,512]{2,1,0:T(8,128)(2,1)S(1)}, bf16[4,128,512]{2,1,0:T(8,128)(2,1)S(1)}, u32[]{:S(2)}, u32[]{:S(2)}) collective-permute-start(bf16[4,128,512]{2,1,0:T(8,128)(2,1)S(1)} %all_to_all.45.mine), channel_id=1, source_target_pairs={{0,1},{1,0},{2,3},{3,2},{4,5},{5,4},{6,7},{7,6},{8,9},{9,8},{10,11... | collective-permute-start | bytes 1572872 | tf_op jit(solution)/shard_map/ppermute | solution.py:412
  48.6 1.5 collective-permute-done.1.other
  50.1 2.4 %attend_low.1 = (f32[128,1792]{1,0:T(8,128)S(1)}, f32[8,1792]{1,0:T(8,128)S(1)}, f32[8,1,896]{2,1,0:T(1,128)S(1)}) custom-call(s32[1,4]{1,0:T(1,128)S(1)} %copy-done.10, bf16[128,1792]{1,0:T(8,128)(2,1)S(1)} %bitcast.18, bf16[4,128,512]{2,1,0:T(8,128)(2,1)S(1)} %all_to_all.45.mine, bf16[4,128,512]{2,1,0:T(8,128)(2,1)S(1)} %collective-permute-done.1.other, ...), custom_call_target="tpu_custom_call" | custom-call | tf_op jit(solution)/shard_map/attend_low/pallas_call | solution.py:354
  52.5 0.9 copy-done.4
  53.4 7.6 %all_to_all.46 = f32[8,1,896]{2,1,0:T(1,128)S(1)} all-to-all(f32[8,1,896]{2,1,0:T(1,128)S(1)} %get-tuple-element.32), channel_id=1, replica_groups=mesh['zlo'=8,'y'=4,'zhi'=2,'x'=4,'core'=2] {'x','core'}, dimensions={0} | all-to-all | bytes 57344 | tf_op jit(solution)/shard_map/all_to_all | solution.py:426
  61.0 29.3 %all_to_all.47 = f32[16,1,896]{2,1,0:T(1,128)S(1)} all-to-all(f32[16,1,896]{2,1,0:T(1,128)S(1)} %broadcast_in_dim.18), channel_id=1, replica_groups=mesh['zlo'=8,'y'=4,'zhi'=2,'x'=4,'core'=2] {'zlo','zhi'}, dimensions={0} | all-to-all | bytes 114688 | tf_op jit(solution)/shard_map/all_to_all | solution.py:408
  90.3 0.1 reduce.3
  90.6 13.4 %all_to_all.48 = f32[16,8,896]{2,1,0:T(8,128)S(1)} all-to-all(f32[16,8,896]{2,1,0:T(8,128)S(1)} %broadcast_in_dim.19), channel_id=1, replica_groups=mesh['zlo'=8,'y'=4,'zhi'=2,'x'=4,'core'=2] {'y','x'}, dimensions={0} | all-to-all | bytes 917504 | tf_op jit(solution)/shard_map/all_to_all | solution.py:408
  104.0 5.3 %collective-permute-start.2 = (f32[128,896]{1,0:T(8,128)S(1)}, f32[128,896]{1,0:T(8,128)S(1)}, u32[]{:S(2)}, u32[]{:S(2)}) collective-permute-start(f32[128,896]{1,0:T(8,128)S(1)} %bitcast.21), channel_id=1, source_target_pairs={{0,1},{1,0},{2,3},{3,2},{4,5},{5,4},{6,7},{7,6},{8,9},{9,8},{10,11... | collective-permute-start | bytes 1376264 | tf_op jit(solution)/shard_map/ppermute | solution.py:412
  109.4 1.4 collective-permute-done.2.docs_other
  110.8 0.0 copy-done.1
  110.8 0.0 copy-done.11
  110.8 1.7 contrast.1
  112.4 0.0 copy-start.2
  112.5 0.8 copy-done.2
  113.2 0.6 copy-done.6
  113.9 0.6 copy-done.8
  114.5 15.5 %all_to_all.49 = f32[32,1,896]{2,1,0:T(1,128)} all-to-all(f32[32,1,896]{2,1,0:T(1,128)S(1)} %get-tuple-element.37), channel_id=1, replica_groups=mesh['zlo'=8,'y'=4,'zhi'=2,'x'=4,'core'=2] {'y','zlo'}, dimensions={0} | all-to-all | bytes 229376 | tf_op jit(solution)/shard_map/all_to_all | solution.py:435
  130.0 1.0 reduce_sum.40
  131.0 9.3 %all_to_all.50.upstream = f32[8,1,896]{2,1,0:T(1,128)S(1)} all-to-all(f32[8,1,896]{2,1,0:T(1,128)S(1)} %broadcast_in_dim.20), channel_id=1, replica_groups=mesh['zlo'=8,'y'=4,'zhi'=2,'x'=4,'core'=2] {'x','core'}, dimensions={0} | all-to-all | bytes 57344 | tf_op jit(solution)/shard_map/all_to_all | solution.py:408
  140.3 1.2 copy-done.5
  141.5 0.8 copy-done.9
  142.3 1.9 back_low.1
  144.2 2.6 %collective-permute-start.3 = (bf16[4,128,512]{2,1,0:T(8,128)(2,1)S(1)}, bf16[4,128,512]{2,1,0:T(8,128)(2,1)S(1)}, u32[]{:S(2)}, u32[]{:S(2)}) collective-permute-start(bf16[4,128,512]{2,1,0:T(8,128)(2,1)S(1)} %get-tuple-element.43), channel_id=1, source_target_pairs={{0,1},{1,0},{2,3},{3,2},{4,5},{5,4},{6,7},{7,6},{8,9},{9,8},{10,11... | collective-permute-start | bytes 1572872 | tf_op jit(solution)/shard_map/ppermute | solution.py:412
  146.9 5.5 %back_own.1 = (bf16[128,1792]{1,0:T(8,128)(2,1)}, bf16[4,256,512]{2,1,0:T(8,128)(2,1)}) custom-call(s32[1,4]{1,0:T(1,128)S(1)} %copy-done.10, bf16[128,1792]{1,0:T(8,128)(2,1)S(1)} %bitcast.20, bf16[4,256,512]{2,1,0:T(8,128)(2,1)S(1)} %bitcast.16, f32[8,1792]{1,0:T(8,128)S(1)} %get-tuple-element.35.lse, bf16[128,1792]{1,0:T(8,128)(2,1)S(1)} %get-tuple-element.39.out_low, ...), custom_call_target="tpu_custom_call" | custom-call | tf_op jit(solution)/shard_map/back_own/pallas_call | solution.py:354
  152.4 0.0 collective-permute-done.3
  152.4 0.1 add_convert_fusion
  152.5 14.6 %all_to_all.51 = bf16[4,128,512]{2,1,0:T(8,128)(2,1)S(1)} all-to-all(bf16[4,128,512]{2,1,0:T(8,128)(2,1)S(1)} %add_convert_fusion), channel_id=1, replica_groups=mesh['zlo'=8,'y'=4,'zhi'=2,'x'=4,'core'=2] {'x'}, dimensions={0} | all-to-all | bytes 1048576 | tf_op jit(solution)/shard_map/all_to_all | solution.py:445
  167.1 0.1 reduce_sum.41
  167.2 0.0 copy-start.3
  167.2 0.0 copy-start.7
  167.2 5.8 %all-to-all-start.8 = ((bf16[8,128,512]{2,1,0:T(8,128)(2,1)}), bf16[8,128,512]{2,1,0:T(8,128)(2,1)S(1)}, u32[]{:S(2)}, u32[]{:S(2)}) async-start(bf16[8,128,512]{2,1,0:T(8,128)(2,1)} %bitcast.7), calls=%async_computation.8 | async-start | bytes 2097152 | tf_op jit(solution)/shard_map/all_to_all | solution.py:449
  173.1 1.3 collective-permute-start.4
  174.4 2.2 %query_back.1 = f32[128,1792]{1,0:T(8,128)} custom-call(bf16[128,1792]{1,0:T(8,128)(2,1)S(1)} %copy-done.1, f32[128,896]{1,0:T(8,128)S(1)} %bitcast.23, f32[128,896]{1,0:T(8,128)S(1)} %copy-done.3, f32[128,128]{1,0:T(8,128)S(1)} %copy-done.7), custom_call_target="tpu_custom_call" | custom-call | tf_op jit(solution)/shard_map/query_back/pallas_call | solution.py:354
  176.6 20.0 %collective-permute-done.4 = bf16[128,512]{1,0:T(8,128)(2,1)S(1)} collective-permute-done((bf16[128,512]{1,0:T(8,128)(2,1)S(1)}, bf16[128,512]{1,0:T(8,128)(2,1)S(1)}, u32[]{:S(2)}, u32[]{:S(2)}) %collective-permute-start.4) | collective-permute-done | bytes 131104 | tf_op jit(solution)/shard_map/ppermute | solution.py:448
  196.5 0.0 all-to-all-done.8
  196.5 0.1 convert_reduce_fusion
  196.7 0.7 slice_bitcast_fusion
  (20 shorter events, 0.3 us)
Async XLA Ops:
  2.6 19.8 %copy-start = (bf16[1,128,1792]{2,1,0:T(8,128)(2,1)S(1)}, bf16[1,128,1792]{2,1,0:T(8,128)(2,1)}, u32[]{:S(2)}) copy-start(bf16[1,128,1792]{2,1,0:T(8,128)(2,1)} %param.6) | copy-start | bytes 1376260
  2.6 19.8 %copy-start.10 = (s32[1,4]{1,0:T(1,128)S(1)}, s32[1,4]{1,0:T(1,128)}, u32[]{:S(2)}) copy-start(s32[1,4]{1,0:T(1,128)} %lengths.7) | copy-start | bytes 52
  2.6 19.8 %all-to-all-start = ((bf16[8,128,512]{2,1,0:T(8,128)(2,1)}), bf16[8,128,512]{2,1,0:T(8,128)(2,1)S(1)}, u32[]{:S(2)}, u32[]{:S(2)}) async-start(bf16[8,128,512]{2,1,0:T(8,128)(2,1)} %broadcast_in_dim.16), calls=%async_computation | async-start | bytes 2097152 | tf_op jit(solution)/shard_map/all_to_all | solution.py:408
  7.9 25.5 %collective-permute-start = (bf16[128,512]{1,0:T(8,128)(2,1)S(1)}, bf16[128,512]{1,0:T(8,128)(2,1)S(1)}, u32[]{:S(2)}, u32[]{:S(2)}) collective-permute-start(bf16[128,512]{1,0:T(8,128)(2,1)S(1)} %pad_maximum_fusion), channel_id=1, source_target_pairs={{0,8},{1,9},{2,10},{3,11},{4,12},{5,13},{6,14},{7,15},{16,24},{17,... | collective-permute-start | bytes 393224 | tf_op jit(solution)/shard_map/ppermute | solution.py:418
  44.0 6.0 %collective-permute-start.1 = (bf16[4,128,512]{2,1,0:T(8,128)(2,1)S(1)}, bf16[4,128,512]{2,1,0:T(8,128)(2,1)S(1)}, u32[]{:S(2)}, u32[]{:S(2)}) collective-permute-start(bf16[4,128,512]{2,1,0:T(8,128)(2,1)S(1)} %all_to_all.45.mine), channel_id=1, source_target_pairs={{0,1},{1,0},{2,3},{3,2},{4,5},{5,4},{6,7},{7,6},{8,9},{9,8},{10,11... | collective-permute-start | bytes 1572872 | tf_op jit(solution)/shard_map/ppermute | solution.py:412
  52.5 0.9 copy-start.4
  53.4 57.4 %copy-start.1 = (bf16[128,1792]{1,0:T(8,128)(2,1)S(1)}, bf16[128,1792]{1,0:T(8,128)(2,1)}, u32[]{:S(2)}) copy-start(bf16[128,1792]{1,0:T(8,128)(2,1)} %q.3) | copy-start | bytes 1376260
  53.4 57.4 %copy-start.11 = (s32[128]{0:T(128)S(1)}, s32[128]{0:T(128)}, u32[]{:S(2)}) copy-start(s32[128]{0:T(128)} %param.11) | copy-start | bytes 1540
  104.0 6.8 %collective-permute-start.2 = (f32[128,896]{1,0:T(8,128)S(1)}, f32[128,896]{1,0:T(8,128)S(1)}, u32[]{:S(2)}, u32[]{:S(2)}) collective-permute-start(f32[128,896]{1,0:T(8,128)S(1)} %bitcast.21), channel_id=1, source_target_pairs={{0,1},{1,0},{2,3},{3,2},{4,5},{5,4},{6,7},{7,6},{8,9},{9,8},{10,11... | collective-permute-start | bytes 1376264 | tf_op jit(solution)/shard_map/ppermute | solution.py:412
  112.4 0.8 copy-start.2
  113.2 0.6 copy-start.6
  113.9 0.6 copy-start.8
  140.3 1.2 copy-start.5
  141.5 0.8 copy-start.9
  144.2 8.2 %collective-permute-start.3 = (bf16[4,128,512]{2,1,0:T(8,128)(2,1)S(1)}, bf16[4,128,512]{2,1,0:T(8,128)(2,1)S(1)}, u32[]{:S(2)}, u32[]{:S(2)}) collective-permute-start(bf16[4,128,512]{2,1,0:T(8,128)(2,1)S(1)} %get-tuple-element.43), channel_id=1, source_target_pairs={{0,1},{1,0},{2,3},{3,2},{4,5},{5,4},{6,7},{7,6},{8,9},{9,8},{10,11... | collective-permute-start | bytes 1572872 | tf_op jit(solution)/shard_map/ppermute | solution.py:412
  167.2 7.1 %copy-start.3 = (f32[128,896]{1,0:T(8,128)S(1)}, f32[128,896]{1,0:T(8,128)}, u32[]{:S(2)}) copy-start(f32[128,896]{1,0:T(8,128)} %copy-done.2) | copy-start | bytes 1376260
  167.2 7.1 %copy-start.7 = (f32[128,128]{1,0:T(8,128)S(1)}, f32[128,128]{1,0:T(8,128)}, u32[]{:S(2)}) copy-start(f32[128,128]{1,0:T(8,128)} %copy-done.6) | copy-start | bytes 196612
  167.2 29.3 %all-to-all-start.8 = ((bf16[8,128,512]{2,1,0:T(8,128)(2,1)}), bf16[8,128,512]{2,1,0:T(8,128)(2,1)S(1)}, u32[]{:S(2)}, u32[]{:S(2)}) async-start(bf16[8,128,512]{2,1,0:T(8,128)(2,1)} %bitcast.7), calls=%async_computation.8 | async-start | bytes 2097152 | tf_op jit(solution)/shard_map/all_to_all | solution.py:449
  173.1 23.5 %collective-permute-start.4 = (bf16[128,512]{1,0:T(8,128)(2,1)S(1)}, bf16[128,512]{1,0:T(8,128)(2,1)S(1)}, u32[]{:S(2)}, u32[]{:S(2)}) collective-permute-start(bf16[128,512]{1,0:T(8,128)(2,1)S(1)} %reduce_sum.41), channel_id=1, source_target_pairs={{8,0},{9,1},{10,2},{11,3},{12,4},{13,5},{14,6},{15,7},{24,16},{25,... | collective-permute-start | bytes 393224 | tf_op jit(solution)/shard_map/ppermute | solution.py:448

commit v3 on v2

--- a/solution.py
+++ b/solution.py
@@ -32,7 +32,7 @@
 TN = (((0,), (0,)), ((), ()))
 NN = (((1,), (0,)), ((), ()))
 NEAR = ("x", "core")
-VMEM_BYTES = 40 * 1024 * 1024
+VMEM_BYTES = 24 * 1024 * 1024
 
 
 def mm(a, b, dims, precision=None):
@@ -149,11 +149,11 @@
     return top + jnp.log(total)
 
 
-def attend_own_kernel(lengths, q, kv, att, lse, held, out):
+def attend_own_kernel(lengths, q, mine, other, att, lse, held, out):
     row = Row(lengths)
     for group in range(KV_HEADS):
         columns = slice(group * GROUP_W, (group + 1) * GROUP_W)
-        log_total = part_attention(row, row.own, group, q, (kv,), held, out)
+        log_total = part_attention(row, row.own, group, q, (mine, other), held, out)
         att[:, columns] = out[...]
         lse[:, columns] = jnp.broadcast_to(log_total, (8, GROUP_W))
 
@@ -317,9 +317,12 @@
         dq_low[:, columns] = dq[...]
 
 
-def back_own_kernel(lengths, q, kv, lse, out_low, delta, dq_low, grad_q, d_kv, dq):
+def back_own_kernel(
+    lengths, q, mine, other, lse, out_low, delta, dq_low, grad_q, d_mine, d_other, dq
+):
     row = Row(lengths)
-    d_kv[...] = jnp.zeros(d_kv.shape, d_kv.dtype)
+    d_mine[...] = jnp.zeros(d_mine.shape, d_mine.dtype)
+    d_other[...] = jnp.zeros(d_other.shape, d_other.dtype)
     for group in range(KV_HEADS):
         columns = slice(group * GROUP_W, (group + 1) * GROUP_W)
         dq[...] = dq_low[:, columns]
@@ -328,12 +331,12 @@
             row.own,
             group,
             q,
-            (kv,),
+            (mine, other),
             lse[0:1, columns],
             head_rows(out_low, group),
             delta[0:1, columns],
             dq,
-            (d_kv,),
+            (d_mine, d_other),
         )
         for h in range(PER_GROUP):
             block = dq[:, h * TOK : (h + 1) * TOK]
@@ -400,7 +403,7 @@
 
 
 def back_own(lengths, *arrays):
-    outs = (shape((TOK, EMB), BF16), shape((CHUNKS, CHUNK, 2 * KVW), BF16))
+    outs = (shape((TOK, EMB), BF16), TERMS, TERMS)
     return run(back_own_kernel, "back_own", outs, [WIDE], lengths, *arrays)
 
 
@@ -410,44 +413,57 @@
 
 def swap_cores(block):
     return lax.ppermute(block, "core", [(0, 1), (1, 0)])
+
+
+def added(blocks):
+    total = blocks[0].astype(F32)
+    for i in range(1, blocks.shape[0]):
+        total = total + blocks[i].astype(F32)
+    return total
+
+
+def pair_terms(d_mine, d_other):
+    got = swap_cores(d_other)
+    return (d_mine.astype(F32) + got.astype(F32)).astype(BF16)
 
 
 def per_device(queries_q, keys, values, lengths, query_emb, positive):
     q = queries_q[0]
     kv = jnp.concatenate([keys[0], values[0]], axis=1)
     kv_low = lax.ppermute(kv, "zhi", [(0, 1)])
-    own_kv = to_all(kv, NEAR, 8).reshape(CHUNKS, CHUNK, 2 * KVW)
-    own_att, own_lse = attend_own(lengths, q, own_kv)
-    kv_low, own_att = lax.optimization_barrier((kv_low, own_att))
+    own_mine = to_all(kv, "x", 4)
+    kv_low, own_mine = lax.optimization_barrier((kv_low, own_mine))
+    own_other = swap_cores(own_mine)
+    own_att, own_lse = attend_own(lengths, q, own_mine, own_other)
     low_mine = to_all(kv_low, "x", 4)
     low_other = swap_cores(low_mine)
     att, lse, pieces = attend_low(lengths, q, low_mine, low_other, own_att, own_lse)
 
-    part = jnp.sum(lax.all_to_all(pieces, NEAR, 0, 0), axis=0)
-    column = to_all(part, ("zlo", "zhi"), 16).reshape(8, 2, PIECE)
-    column = column[:, 0] + column[:, 1]
+    part = added(lax.all_to_all(pieces, NEAR, 0, 0))
+    column = to_all(part, ("zlo", "zhi"), 16)
+    column = (column[0::2] + column[1::2]).reshape(8, PIECE)
     docs_mine = to_all(column, ("y", "x"), 16).reshape(NDOC, PIECE)
     docs_other = swap_cores(docs_mine)
 
     coefficient, terms, own_docs = contrast(
         query_emb, positive.reshape(1, 128), docs_mine, docs_other
     )
-    terms = jnp.sum(lax.all_to_all(terms, ("y", "zlo"), 0, 0), axis=0)
+    terms = added(lax.all_to_all(terms, ("y", "zlo"), 0, 0))
     upstream = to_all(terms, NEAR, 8)
 
     out_low, delta, dq_low, d_mine, d_other = back_low(
         lengths, q, low_mine, low_other, att, lse, own_docs, upstream
     )
-    got = swap_cores(d_other)
-    grad_q, own_d = back_own(lengths, q, own_kv, lse, out_low, delta, dq_low)
-    own_d, got = lax.optimization_barrier((own_d, got))
-    paired = (d_mine.astype(F32) + got.astype(F32)).astype(BF16)
-    low_terms = lax.all_to_all(paired, "x", 0, 0)
-    low_sum = jnp.sum(low_terms.astype(F32), axis=0).astype(BF16)
-    low_sum, own_d = lax.optimization_barrier((low_sum, own_d))
+    grad_q, own_d_mine, own_d_other = back_own(
+        lengths, q, own_mine, own_other, lse, out_low, delta, dq_low
+    )
+    low_terms = lax.all_to_all(pair_terms(d_mine, d_other), "x", 0, 0)
+    low_sum = added(low_terms).astype(BF16)
+    own_paired = pair_terms(own_d_mine, own_d_other)
+    low_sum, own_paired = lax.optimization_barrier((low_sum, own_paired))
     from_high = lax.ppermute(low_sum, "zhi", [(1, 0)])
-    own_terms = lax.all_to_all(own_d.reshape(8, TOK, 2 * KVW), NEAR, 0, 0)
-    own_sum = jnp.sum(own_terms.astype(F32), axis=0)
+    own_terms = lax.all_to_all(own_paired, "x", 0, 0)
+    own_sum = added(own_terms)
     coefficient, low_sum = lax.optimization_barrier((coefficient, low_sum))
     query_grad = query_back(query_emb, docs_mine, docs_other, coefficient)
     query_grad, from_high = lax.optimization_barrier((query_grad, from_high))

time: 198 us -> 195 us (0.985)
  the two profiles are of different devices: /device:TPU:35 before, /device:TPU:42 now
where the time goes in v3:
time: 195 us
  blocking collectives  77.4 us (40%)
  starting transfers between devices  48.3 us (25%)
  waiting for transfers between devices  45.9 us (24%)
  Pallas kernels  16.8 us (9%)
  other arithmetic  3.04 us (2%)
  local copies, waits for them, and re-layouts  2.43 us (1%)
    all_to_all x3, blocking collectives, to_all(): lax.all_to_all(jnp.broadcast_to(block[None], (count,) + block.shape), axe...  50.1 us
    ppermute x1, waiting for transfers between devices, per_device(): from_high = lax.ppermute(low_sum, 'zhi', [(1, 0)])  21.2 us
    pallas_call x6, Pallas kernels, run(): pl.pallas_call(kernel, out_shape=outs, in_specs=[smem] * len(first) + [vm...  16.8 us
    all_to_all x1, blocking collectives, per_device(): terms = added(lax.all_to_all(terms, ('y', 'zlo'), 0, 0))  16.7 us
    ppermute x1, starting transfers between devices, per_device(): kv_low = lax.ppermute(kv, 'zhi', [(0, 1)])  14.8 us
    all_to_all x1, blocking collectives, per_device(): part = added(lax.all_to_all(pieces, NEAR, 0, 0))  10.6 us
    ppermute x1, waiting for transfers between devices, per_device(): kv_low = lax.ppermute(kv, 'zhi', [(0, 1)])  10.6 us
    ppermute x5, starting transfers between devices, swap_cores(): return lax.ppermute(block, 'core', [(0, 1), (1, 0)])  10.3 us
  transfers between devices with their start and end apart: 11, of which 5 were waited for; matrix products, arithmetic and copies ran while one was open for 1% of the time, Pallas kernels for 6%

profile of v3, /device:TPU:42, one launch (start us, length us, event | category | flops | bytes accessed | tf_op | source)
XLA Modules:
  0.0 194.7 jit_solution(17508606369013186171)
XLA Ops:
  0.6 0.9 pad_maximum_fusion
  1.5 0.8 broadcast_in_dim.44
  2.4 4.8 %all-to-all-start = ((bf16[4,128,512]{2,1,0:T(8,128)(2,1)}), bf16[4,128,512]{2,1,0:T(8,128)(2,1)S(1)}, u32[]{:S(2)}, u32[]{:S(2)}) async-start(bf16[4,128,512]{2,1,0:T(8,128)(2,1)} %broadcast_in_dim.44), calls=%async_computation | async-start | bytes 1048576 | tf_op jit(solution)/shard_map/all_to_all | solution.py:411
  7.2 14.8 %collective-permute-start = (bf16[128,512]{1,0:T(8,128)(2,1)S(1)}, bf16[128,512]{1,0:T(8,128)(2,1)S(1)}, u32[]{:S(2)}, u32[]{:S(2)}) collective-permute-start(bf16[128,512]{1,0:T(8,128)(2,1)S(1)} %pad_maximum_fusion), channel_id=1, source_target_pairs={{0,8},{1,9},{2,10},{3,11},{4,12},{5,13},{6,14},{7,15},{16,24},{17,... | collective-permute-start | bytes 393224 | tf_op jit(solution)/shard_map/ppermute | solution.py:433
  22.0 10.6 %collective-permute-done = bf16[128,512]{1,0:T(8,128)(2,1)S(1)} collective-permute-done((bf16[128,512]{1,0:T(8,128)(2,1)S(1)}, bf16[128,512]{1,0:T(8,128)(2,1)S(1)}, u32[]{:S(2)}, u32[]{:S(2)}) %collective-permute-start) | collective-permute-done | bytes 131104 | tf_op jit(solution)/shard_map/ppermute | solution.py:433
  32.6 0.0 all-to-all-done.mine
  32.6 0.8 broadcast_in_dim.45
  33.4 0.0 copy-start
  33.4 4.9 %all-to-all-start.1 = ((bf16[4,128,512]{2,1,0:T(8,128)(2,1)}), bf16[4,128,512]{2,1,0:T(8,128)(2,1)S(1)}, u32[]{:S(2)}, u32[]{:S(2)}) async-start(bf16[4,128,512]{2,1,0:T(8,128)(2,1)} %broadcast_in_dim.45), calls=%async_computation.1 | async-start | bytes 1048576 | tf_op jit(solution)/shard_map/all_to_all | solution.py:411
  38.4 2.0 %collective-permute-start.2 = (bf16[4,128,512]{2,1,0:T(8,128)(2,1)S(1)}, bf16[4,128,512]{2,1,0:T(8,128)(2,1)S(1)}, u32[]{:S(2)}, u32[]{:S(2)}) collective-permute-start(bf16[4,128,512]{2,1,0:T(8,128)(2,1)S(1)} %all-to-all-done.mine), channel_id=1, source_target_pairs={{0,1},{1,0},{2,3},{3,2},{4,5},{5,4},{6,7},{7,6},{8,9},{9,8},{10,11... | collective-permute-start | bytes 1572872 | tf_op jit(solution)/shard_map/ppermute | solution.py:415
  40.4 5.0 %all-to-all-done.1.mine = bf16[4,128,512]{2,1,0:T(8,128)(2,1)S(1)} async-done(((bf16[4,128,512]{2,1,0:T(8,128)(2,1)}), bf16[4,128,512]{2,1,0:T(8,128)(2,1)S(1)}, u32[]{:S(2)}, u32[]{:S(2)}) %all-to-all-start.1) | async-done | bytes 524320 | tf_op jit(solution)/shard_map/all_to_all | solution.py:411
  45.4 1.9 collective-permute-start.1
  47.4 0.0 collective-permute-done.2.other
  47.4 0.0 copy-done
  47.4 0.0 copy-done.2
  47.4 3.5 %attend_own.1 = (f32[128,1792]{1,0:T(8,128)S(1)}, f32[8,1792]{1,0:T(8,128)S(1)}) custom-call(s32[1,4]{1,0:T(1,128)S(1)} %copy-done.2, bf16[128,1792]{1,0:T(8,128)(2,1)S(1)} %bitcast.19, bf16[4,128,512]{2,1,0:T(8,128)(2,1)S(1)} %all-to-all-done.mine, bf16[4,128,512]{2,1,0:T(8,128)(2,1)S(1)} %collective-permute-done.2.other), custom_call_target="tpu_custom_call" | custom-call | tf_op jit(solution)/shard_map/attend_own/pallas_call | solution.py:357
  50.9 0.0 collective-permute-done.1.other
  50.9 2.4 %attend_low.1 = (f32[128,1792]{1,0:T(8,128)S(1)}, f32[8,1792]{1,0:T(8,128)S(1)}, f32[8,1,896]{2,1,0:T(1,128)S(1)}) custom-call(s32[1,4]{1,0:T(1,128)S(1)} %copy-done.2, bf16[128,1792]{1,0:T(8,128)(2,1)S(1)} %bitcast.20, bf16[4,128,512]{2,1,0:T(8,128)(2,1)S(1)} %all-to-all-done.1.mine, bf16[4,128,512]{2,1,0:T(8,128)(2,1)S(1)} %collective-permute-done.1.other, ...), custom_call_target="tpu_custom_call" | custom-call | tf_op jit(solution)/shard_map/attend_low/pallas_call | solution.py:357
  53.3 10.6 %all_to_all.45 = f32[8,1,896]{2,1,0:T(1,128)S(1)} all-to-all(f32[8,1,896]{2,1,0:T(1,128)S(1)} %get-tuple-element.31), channel_id=1, replica_groups=mesh['zlo'=8,'y'=4,'zhi'=2,'x'=4,'core'=2] {'x','core'}, dimensions={0} | all-to-all | bytes 57344 | tf_op jit(solution)/shard_map/all_to_all | solution.py:442
  64.0 28.7 %all_to_all.46 = f32[16,1,896]{2,1,0:T(1,128)S(1)} all-to-all(f32[16,1,896]{2,1,0:T(1,128)S(1)} %broadcast_in_dim.47), channel_id=1, replica_groups=mesh['zlo'=8,'y'=4,'zhi'=2,'x'=4,'core'=2] {'zlo','zhi'}, dimensions={0} | all-to-all | bytes 114688 | tf_op jit(solution)/shard_map/all_to_all | solution.py:411
  92.8 0.0 copy-start.1
  92.8 13.6 %all_to_all.47 = f32[16,8,896]{2,1,0:T(8,128)S(1)} all-to-all(f32[16,8,896]{2,1,0:T(8,128)S(1)} %broadcast_in_dim.49), channel_id=1, replica_groups=mesh['zlo'=8,'y'=4,'zhi'=2,'x'=4,'core'=2] {'y','x'}, dimensions={0} | all-to-all | bytes 917504 | tf_op jit(solution)/shard_map/all_to_all | solution.py:411
  106.4 2.0 %collective-permute-start.3 = (f32[128,896]{1,0:T(8,128)S(1)}, f32[128,896]{1,0:T(8,128)S(1)}, u32[]{:S(2)}, u32[]{:S(2)}) collective-permute-start(f32[128,896]{1,0:T(8,128)S(1)} %bitcast.23), channel_id=1, source_target_pairs={{0,1},{1,0},{2,3},{3,2},{4,5},{5,4},{6,7},{7,6},{8,9},{9,8},{10,11... | collective-permute-start | bytes 1376264 | tf_op jit(solution)/shard_map/ppermute | solution.py:415
  108.5 1.8 collective-permute-done.3.docs_other
  110.3 0.0 copy-done.1
  110.3 0.0 copy-done.3
  110.3 1.6 contrast.1
  111.9 16.7 %all_to_all.48 = f32[32,1,896]{2,1,0:T(1,128)S(1)} all-to-all(f32[32,1,896]{2,1,0:T(1,128)S(1)} %get-tuple-element.36), channel_id=1, replica_groups=mesh['zlo'=8,'y'=4,'zhi'=2,'x'=4,'core'=2] {'y','zlo'}, dimensions={0} | all-to-all | bytes 229376 | tf_op jit(solution)/shard_map/all_to_all | solution.py:451
  128.6 0.1 fusion.2
  128.7 7.8 %all_to_all.49.upstream = f32[8,1,896]{2,1,0:T(1,128)S(1)} all-to-all(f32[8,1,896]{2,1,0:T(1,128)S(1)} %broadcast_in_dim.51), channel_id=1, replica_groups=mesh['zlo'=8,'y'=4,'zhi'=2,'x'=4,'core'=2] {'x','core'}, dimensions={0} | all-to-all | bytes 57344 | tf_op jit(solution)/shard_map/all_to_all | solution.py:411
  136.5 1.9 back_low.1
  138.4 1.9 collective-permute-start.4
  140.3 5.2 %back_own.1 = (bf16[128,1792]{1,0:T(8,128)(2,1)}, bf16[4,128,512]{2,1,0:T(8,128)(2,1)S(1)}, bf16[4,128,512]{2,1,0:T(8,128)(2,1)}) custom-call(s32[1,4]{1,0:T(1,128)S(1)} %copy-done.2, bf16[128,1792]{1,0:T(8,128)(2,1)S(1)} %bitcast.22, bf16[4,128,512]{2,1,0:T(8,128)(2,1)S(1)} %all-to-all-done.mine, bf16[4,128,512]{2,1,0:T(8,128)(2,1)S(1)} %collective-permute-done.2.other, ...), custom_call_target="tpu_custom_call" | custom-call | tf_op jit(solution)/shard_map/back_own/pallas_call | solution.py:357
  145.5 2.4 %collective-permute-start.5 = (bf16[4,128,512]{2,1,0:T(8,128)(2,1)}, bf16[4,128,512]{2,1,0:T(8,128)(2,1)S(1)}, u32[]{:S(2)}, u32[]{:S(2)}) collective-permute-start(bf16[4,128,512]{2,1,0:T(8,128)(2,1)} %get-tuple-element.43), channel_id=1, source_target_pairs={{0,1},{1,0},{2,3},{3,2},{4,5},{5,4},{6,7},{7,6},{8,9},{9,8},{10,11... | collective-permute-start | bytes 1572872 | tf_op jit(solution)/shard_map/ppermute | solution.py:415
  147.9 0.0 collective-permute-done.4
  147.9 0.9 add_convert_fusion.1
  148.9 7.2 %all-to-all-start.7 = ((bf16[4,128,512]{2,1,0:T(8,128)(2,1)}), bf16[4,128,512]{2,1,0:T(8,128)(2,1)S(1)}, u32[]{:S(2)}, u32[]{:S(2)}) async-start(bf16[4,128,512]{2,1,0:T(8,128)(2,1)} %add_convert_fusion.1), calls=%async_computation.7 | async-start | bytes 1048576 | tf_op jit(solution)/shard_map/all_to_all | solution.py:460
  156.1 0.0 collective-permute-done.5
  156.1 0.9 add_convert_fusion
  157.0 7.3 %all-to-all-done.7 = bf16[4,128,512]{2,1,0:T(8,128)(2,1)S(1)} async-done(((bf16[4,128,512]{2,1,0:T(8,128)(2,1)}), bf16[4,128,512]{2,1,0:T(8,128)(2,1)S(1)}, u32[]{:S(2)}, u32[]{:S(2)}) %all-to-all-start.7) | async-done | bytes 524320 | tf_op jit(solution)/shard_map/all_to_all | solution.py:460
  164.3 0.1 fusion.1
  164.4 4.9 %all-to-all-start.8 = ((bf16[4,128,512]{2,1,0:T(8,128)(2,1)}), bf16[4,128,512]{2,1,0:T(8,128)(2,1)S(1)}, u32[]{:S(2)}, u32[]{:S(2)}) async-start(bf16[4,128,512]{2,1,0:T(8,128)(2,1)} %add_convert_fusion), calls=%async_computation.8 | async-start | bytes 1048576 | tf_op jit(solution)/shard_map/all_to_all | solution.py:465
  169.3 1.3 collective-permute-start.6
  170.6 2.2 %query_back.1 = f32[128,1792]{1,0:T(8,128)} custom-call(bf16[128,1792]{1,0:T(8,128)(2,1)S(1)} %copy-done.1, f32[128,896]{1,0:T(8,128)S(1)} %bitcast.25, f32[128,896]{1,0:T(8,128)S(1)} %collective-permute-done.3.docs_other, f32[128,128]{1,0:T(8,128)S(1)} %get-tuple-element.45.coefficient), custom_call_target="tpu_custom_call" | custom-call | tf_op jit(solution)/shard_map/query_back/pallas_call | solution.py:357
  172.7 21.2 %collective-permute-done.6 = bf16[128,512]{1,0:T(8,128)(2,1)S(1)} collective-permute-done((bf16[128,512]{1,0:T(8,128)(2,1)S(1)}, bf16[128,512]{1,0:T(8,128)(2,1)S(1)}, u32[]{:S(2)}, u32[]{:S(2)}) %collective-permute-start.6) | collective-permute-done | bytes 131104 | tf_op jit(solution)/shard_map/ppermute | solution.py:464
  193.9 0.0 all-to-all-done.8
  193.9 0.1 fusion
  194.0 0.7 slice_bitcast_fusion
  (8 shorter events, 0.1 us)
Async XLA Ops:
  2.4 30.2 %all-to-all-start = ((bf16[4,128,512]{2,1,0:T(8,128)(2,1)}), bf16[4,128,512]{2,1,0:T(8,128)(2,1)S(1)}, u32[]{:S(2)}, u32[]{:S(2)}) async-start(bf16[4,128,512]{2,1,0:T(8,128)(2,1)} %broadcast_in_dim.44), calls=%async_computation | async-start | bytes 1048576 | tf_op jit(solution)/shard_map/all_to_all | solution.py:411
  7.2 25.4 %collective-permute-start = (bf16[128,512]{1,0:T(8,128)(2,1)S(1)}, bf16[128,512]{1,0:T(8,128)(2,1)S(1)}, u32[]{:S(2)}, u32[]{:S(2)}) collective-permute-start(bf16[128,512]{1,0:T(8,128)(2,1)S(1)} %pad_maximum_fusion), channel_id=1, source_target_pairs={{0,8},{1,9},{2,10},{3,11},{4,12},{5,13},{6,14},{7,15},{16,24},{17,... | collective-permute-start | bytes 393224 | tf_op jit(solution)/shard_map/ppermute | solution.py:433
  33.4 13.9 %copy-start = (bf16[1,128,1792]{2,1,0:T(8,128)(2,1)S(1)}, bf16[1,128,1792]{2,1,0:T(8,128)(2,1)}, u32[]{:S(2)}) copy-start(bf16[1,128,1792]{2,1,0:T(8,128)(2,1)} %param.6) | copy-start | bytes 1376260
  33.4 12.0 %all-to-all-start.1 = ((bf16[4,128,512]{2,1,0:T(8,128)(2,1)}), bf16[4,128,512]{2,1,0:T(8,128)(2,1)S(1)}, u32[]{:S(2)}, u32[]{:S(2)}) async-start(bf16[4,128,512]{2,1,0:T(8,128)(2,1)} %broadcast_in_dim.45), calls=%async_computation.1 | async-start | bytes 1048576 | tf_op jit(solution)/shard_map/all_to_all | solution.py:411
  38.4 9.0 %copy-start.2 = (s32[1,4]{1,0:T(1,128)S(1)}, s32[1,4]{1,0:T(1,128)}, u32[]{:S(2)}) copy-start(s32[1,4]{1,0:T(1,128)} %lengths.7) | copy-start | bytes 52
  38.4 9.0 %collective-permute-start.2 = (bf16[4,128,512]{2,1,0:T(8,128)(2,1)S(1)}, bf16[4,128,512]{2,1,0:T(8,128)(2,1)S(1)}, u32[]{:S(2)}, u32[]{:S(2)}) collective-permute-start(bf16[4,128,512]{2,1,0:T(8,128)(2,1)S(1)} %all-to-all-done.mine), channel_id=1, source_target_pairs={{0,1},{1,0},{2,3},{3,2},{4,5},{5,4},{6,7},{7,6},{8,9},{9,8},{10,11... | collective-permute-start | bytes 1572872 | tf_op jit(solution)/shard_map/ppermute | solution.py:415
  45.4 5.5 %collective-permute-start.1 = (bf16[4,128,512]{2,1,0:T(8,128)(2,1)S(1)}, bf16[4,128,512]{2,1,0:T(8,128)(2,1)S(1)}, u32[]{:S(2)}, u32[]{:S(2)}) collective-permute-start(bf16[4,128,512]{2,1,0:T(8,128)(2,1)S(1)} %all-to-all-done.1.mine), channel_id=1, source_target_pairs={{0,1},{1,0},{2,3},{3,2},{4,5},{5,4},{6,7},{7,6},{8,9},{9,8},{10,11... | collective-permute-start | bytes 1572872 | tf_op jit(solution)/shard_map/ppermute | solution.py:415
  92.8 17.5 %copy-start.1 = (bf16[128,1792]{1,0:T(8,128)(2,1)S(1)}, bf16[128,1792]{1,0:T(8,128)(2,1)}, u32[]{:S(2)}) copy-start(bf16[128,1792]{1,0:T(8,128)(2,1)} %q.3) | copy-start | bytes 1376260
  106.4 3.8 %copy-start.3 = (s32[128]{0:T(128)S(1)}, s32[128]{0:T(128)}, u32[]{:S(2)}) copy-start(s32[128]{0:T(128)} %param.11) | copy-start | bytes 1540
  106.4 3.8 %collective-permute-start.3 = (f32[128,896]{1,0:T(8,128)S(1)}, f32[128,896]{1,0:T(8,128)S(1)}, u32[]{:S(2)}, u32[]{:S(2)}) collective-permute-start(f32[128,896]{1,0:T(8,128)S(1)} %bitcast.23), channel_id=1, source_target_pairs={{0,1},{1,0},{2,3},{3,2},{4,5},{5,4},{6,7},{7,6},{8,9},{9,8},{10,11... | collective-permute-start | bytes 1376264 | tf_op jit(solution)/shard_map/ppermute | solution.py:415
  138.4 9.5 %collective-permute-start.4 = (bf16[4,128,512]{2,1,0:T(8,128)(2,1)S(1)}, bf16[4,128,512]{2,1,0:T(8,128)(2,1)S(1)}, u32[]{:S(2)}, u32[]{:S(2)}) collective-permute-start(bf16[4,128,512]{2,1,0:T(8,128)(2,1)S(1)} %get-tuple-element.38), channel_id=1, source_target_pairs={{0,1},{1,0},{2,3},{3,2},{4,5},{5,4},{6,7},{7,6},{8,9},{9,8},{10,11... | collective-permute-start | bytes 1572872 | tf_op jit(solution)/shard_map/ppermute | solution.py:415
  145.5 10.6 %collective-permute-start.5 = (bf16[4,128,512]{2,1,0:T(8,128)(2,1)}, bf16[4,128,512]{2,1,0:T(8,128)(2,1)S(1)}, u32[]{:S(2)}, u32[]{:S(2)}) collective-permute-start(bf16[4,128,512]{2,1,0:T(8,128)(2,1)} %get-tuple-element.43), channel_id=1, source_target_pairs={{0,1},{1,0},{2,3},{3,2},{4,5},{5,4},{6,7},{7,6},{8,9},{9,8},{10,11... | collective-permute-start | bytes 1572872 | tf_op jit(solution)/shard_map/ppermute | solution.py:415
  148.9 15.4 %all-to-all-start.7 = ((bf16[4,128,512]{2,1,0:T(8,128)(2,1)}), bf16[4,128,512]{2,1,0:T(8,128)(2,1)S(1)}, u32[]{:S(2)}, u32[]{:S(2)}) async-start(bf16[4,128,512]{2,1,0:T(8,128)(2,1)} %add_convert_fusion.1), calls=%async_computation.7 | async-start | bytes 1048576 | tf_op jit(solution)/shard_map/all_to_all | solution.py:460
  164.4 29.6 %all-to-all-start.8 = ((bf16[4,128,512]{2,1,0:T(8,128)(2,1)}), bf16[4,128,512]{2,1,0:T(8,128)(2,1)S(1)}, u32[]{:S(2)}, u32[]{:S(2)}) async-start(bf16[4,128,512]{2,1,0:T(8,128)(2,1)} %add_convert_fusion), calls=%async_computation.8 | async-start | bytes 1048576 | tf_op jit(solution)/shard_map/all_to_all | solution.py:465
  169.3 24.6 %collective-permute-start.6 = (bf16[128,512]{1,0:T(8,128)(2,1)S(1)}, bf16[128,512]{1,0:T(8,128)(2,1)S(1)}, u32[]{:S(2)}, u32[]{:S(2)}) collective-permute-start(bf16[128,512]{1,0:T(8,128)(2,1)S(1)} %fusion.1), channel_id=1, source_target_pairs={{8,0},{9,1},{10,2},{11,3},{12,4},{13,5},{14,6},{15,7},{24,16},{25,... | collective-permute-start | bytes 393224 | tf_op jit(solution)/shard_map/ppermute | solution.py:464

commit v4 on v3

--- a/solution.py
+++ b/solution.py
@@ -75,32 +75,39 @@
             column = jnp.where(rows == d, self.lengths[d].astype(jnp.float32), column)
         return column
 
-    def bias(self, base, chunk, split):
+    def bias(self, base, chunk):
         at = lax.broadcasted_iota(jnp.int32, (CHUNK, TOK), 0)
-        if split:
-            half = lax.div(at, TOK)
-            turned = jnp.where(self.core == 1, 1 - half, half)
-            at = turned * TOK + (at - half * TOK)
-        pos = base + chunk * CHUNK + at
+        half = lax.div(at, TOK)
+        turned = jnp.where(self.core == 1, 1 - half, half)
+        pos = base + chunk * CHUNK + turned * TOK + (at - half * TOK)
         allowed = (pos >= self.start) & (pos <= self.qpos)
-        one = jnp.where(allowed, 0.0, MASKED).astype(jnp.float32)
-        return jnp.concatenate([one] * PER_GROUP, axis=1)
+        return jnp.where(allowed, 0.0, MASKED).astype(jnp.float32)
 
 
 def chunk_of(kv, chunk, column):
     at = slice(column * HEAD_DIM, (column + 1) * HEAD_DIM)
-    if len(kv) == 1:
-        return kv[0][chunk, :, at]
     return jnp.concatenate([half[chunk, :, at] for half in kv], axis=0)
 
 
 def put_chunk(refs, chunk, column, rows):
     at = slice(column * HEAD_DIM, (column + 1) * HEAD_DIM)
-    if len(refs) == 1:
-        refs[0][chunk, :, at] = rows
-    else:
-        refs[0][chunk, :, at] = rows[:TOK]
-        refs[1][chunk, :, at] = rows[TOK:]
+    refs[0][chunk, :, at] = rows[:TOK]
+    refs[1][chunk, :, at] = rows[TOK:]
+
+
+def fill_bias(row, part, bias):
+    base, low, high = part
+
+    def step(chunk, carry):
+        bias[chunk] = row.bias(base, chunk)
+        return carry
+
+    lax.fori_loop(low, high, step, 0)
+
+
+def halves(values):
+    top = values.astype(jnp.bfloat16)
+    return top, (values - top.astype(jnp.float32)).astype(jnp.bfloat16)
 
 
 def head_rows(ref, group):
@@ -113,68 +120,79 @@
     )
 
 
-def head_columns(group, h):
-    at = (group * PER_GROUP + h) * HEAD_DIM
-    return slice(at, at + HEAD_DIM)
-
-
-def part_attention(row, part, group, q, kv, held, out):
-    base, low, high = part
-    q_rows = head_rows(q, group)
-
-    def score_step(chunk, top):
-        scores = mm(chunk_of(kv, chunk, group), q_rows, NT) * FACTOR
-        scores = scores + row.bias(base, chunk, len(kv) > 1)
-        held[chunk] = scores
-        return jnp.maximum(top, jnp.max(scores, axis=0, keepdims=True))
-
-    top = lax.fori_loop(low, high, score_step, jnp.full((1, GROUP_W), MASKED, jnp.float32))
-
-    def total_step(chunk, total):
-        exps = jnp.exp(held[chunk] - top)
-        held[chunk] = exps
-        return total + jnp.sum(exps, axis=0, keepdims=True)
-
-    total = lax.fori_loop(low, high, total_step, jnp.zeros((1, GROUP_W), jnp.float32))
-    total = jnp.maximum(total, TINY)
-    inverse = 1.0 / total
-    out[...] = jnp.zeros((HEAD_DIM, GROUP_W), jnp.float32)
-
-    def out_step(chunk, carry):
-        weights = (held[chunk] * inverse).astype(jnp.bfloat16)
-        out[...] += mm(chunk_of(kv, chunk, KV_HEADS + group), weights, TN)
+def head(h):
+    return slice(h * HEAD_DIM, (h + 1) * HEAD_DIM)
+
+
+def part_attention(part, q, kv, bias, stats, weights, out):
+    _, low, high = part
+    stats[0] = jnp.full((HEADS, TOK), MASKED, jnp.float32)
+    stats[1] = jnp.zeros((HEADS, TOK), jnp.float32)
+    out[...] = jnp.zeros(out.shape, jnp.float32)
+
+    def step(chunk, carry):
+        blocked = bias[chunk]
+        for group in range(KV_HEADS):
+            k_rows = chunk_of(kv, chunk, group)
+            scales = []
+            for h in range(group * PER_GROUP, (group + 1) * PER_GROUP):
+                scores = mm(k_rows, q[:, head(h)], NT) + blocked
+                old = stats[0, h : h + 1]
+                top = jnp.maximum(old, jnp.max(scores, axis=0, keepdims=True))
+                exps = jnp.exp((scores - top) * FACTOR)
+                weights[:, head(h)] = exps.astype(jnp.bfloat16)
+                scale = jnp.exp((old - top) * FACTOR)
+                stats[0, h : h + 1] = top
+                stats[1, h : h + 1] = stats[1, h : h + 1] * scale + jnp.sum(
+                    exps, axis=0, keepdims=True
+                )
+                scales.append(scale)
+            columns = slice(group * GROUP_W, (group + 1) * GROUP_W)
+            sums = mm(chunk_of(kv, chunk, KV_HEADS + group), weights[:, columns], TN)
+            for i in range(PER_GROUP):
+                at = head(group * PER_GROUP + i)
+                out[:, at] = out[:, at] * scales[i] + sums[:, head(i)]
         return carry
 
-    lax.fori_loop(low, high, out_step, 0)
-    return top + jnp.log(total)
-
-
-def attend_own_kernel(lengths, q, mine, other, att, lse, held, out):
+    lax.fori_loop(low, high, step, 0)
+
+
+def part_result(h, stats):
+    total = jnp.maximum(stats[1, h : h + 1], TINY)
+    return stats[0, h : h + 1] * FACTOR + jnp.log(total), 1.0 / total
+
+
+def attend_own_kernel(lengths, q, mine, other, att, lse, bias, stats, weights, out):
     row = Row(lengths)
-    for group in range(KV_HEADS):
-        columns = slice(group * GROUP_W, (group + 1) * GROUP_W)
-        log_total = part_attention(row, row.own, group, q, (mine, other), held, out)
-        att[:, columns] = out[...]
-        lse[:, columns] = jnp.broadcast_to(log_total, (8, GROUP_W))
+    fill_bias(row, row.own, bias)
+    part_attention(row.own, q, (mine, other), bias, stats, weights, out)
+    for h in range(HEADS):
+        log_total, inverse = part_result(h, stats)
+        att[:, head(h)] = out[:, head(h)] * inverse
+        lse[:, head(h)] = jnp.broadcast_to(log_total, (8, TOK))
 
 
 def attend_low_kernel(
-    lengths, q, mine, other, own_att, own_lse, att, lse, pieces, held, out, doc_sum
+    lengths, q, mine, other, own_att, own_lse, att, lse, pieces, bias, stats, weights, out, doc_sum
 ):
     row = Row(lengths)
-    for group in range(KV_HEADS):
-        columns = slice(group * GROUP_W, (group + 1) * GROUP_W)
-        low_total = part_attention(row, row.low, group, q, (mine, other), held, out)
-        own_total = own_lse[0:1, columns]
+    fill_bias(row, row.low, bias)
+    member = jnp.concatenate([row.member, jnp.zeros((TOK - 8, TOK), jnp.float32)], axis=0)
+    member = member.astype(jnp.bfloat16)
+    part_attention(row.low, q, (mine, other), bias, stats, weights, out)
+    for h in range(HEADS):
+        at = head(h)
+        low_total, inverse = part_result(h, stats)
+        own_total = own_lse[0:1, at]
         top = jnp.maximum(low_total, own_total)
         log_total = top + jnp.log(jnp.exp(low_total - top) + jnp.exp(own_total - top))
-        att[:, columns] = own_att[:, columns] * jnp.exp(own_total - log_total) + out[
-            ...
-        ] * jnp.exp(low_total - log_total)
-        lse[:, columns] = jnp.broadcast_to(log_total, (8, GROUP_W))
-        for h in range(PER_GROUP):
-            at = head_columns(group, h)
-            doc_sum[:, at] = mm(row.member, att[:, at], NT, FULL_ACCURACY)
+        own_scale = jnp.exp(own_total - log_total)
+        low_scale = jnp.exp(low_total - log_total) * inverse
+        lse[:, at] = jnp.broadcast_to(log_total, (8, TOK))
+        merged = own_att[:, at] * own_scale + out[:, at] * low_scale
+        att[:, at] = merged
+        big, small = halves(merged)
+        doc_sum[:, at] = (mm(big, member, NT) + mm(small, member, NT)).T[:8]
     mean = doc_sum[...] / row.length_column()
     for d in range(DOCS):
         for c in range(2):
@@ -239,22 +257,28 @@
     query_grad[:, PIECE:] = query_inv * (u_right - q_right * inner)
 
 
-def back_part(row, part, group, q, kv, log_total, out_rows, delta, dq, d_kv):
-    base, low, high = part
-    q_rows = head_rows(q, group)
+def back_part(part, q, kv, bias, lse, out_low, delta, dq, d_kv, grads, weights):
+    _, low, high = part
 
     def step(chunk, carry):
-        k_rows = chunk_of(kv, chunk, group)
-        v_rows = chunk_of(kv, chunk, KV_HEADS + group)
-        scores = mm(k_rows, q_rows, NT) * FACTOR + row.bias(base, chunk, len(kv) > 1)
-        probs = jnp.exp(scores - log_total)
-        flow = mm(v_rows, out_rows, NT)
-        score_grad = (probs * (flow - delta)).astype(jnp.bfloat16)
-        dq[...] += mm(k_rows, score_grad, TN)
-        k_part = (mm(score_grad, q_rows, NN) * FACTOR).astype(jnp.bfloat16)
-        v_part = mm(probs.astype(jnp.bfloat16), out_rows, NN).astype(jnp.bfloat16)
-        put_chunk(d_kv, chunk, group, k_part)
-        put_chunk(d_kv, chunk, KV_HEADS + group, v_part)
+        blocked = bias[chunk]
+        for group in range(KV_HEADS):
+            k_rows = chunk_of(kv, chunk, group)
+            v_rows = chunk_of(kv, chunk, KV_HEADS + group)
+            for h in range(group * PER_GROUP, (group + 1) * PER_GROUP):
+                at = head(h)
+                scores = mm(k_rows, q[:, at], NT) * FACTOR + blocked
+                probs = jnp.exp(scores - lse[0:1, at])
+                flow = mm(v_rows, out_low[:, at], NT)
+                grads[:, at] = (probs * (flow - delta[0:1, at])).astype(jnp.bfloat16)
+                weights[:, at] = probs.astype(jnp.bfloat16)
+            columns = slice(group * GROUP_W, (group + 1) * GROUP_W)
+            score_grad = grads[:, columns]
+            dq[:, columns] += mm(k_rows, score_grad, TN)
+            k_part = mm(score_grad, head_rows(q, group), NN) * FACTOR
+            v_part = mm(weights[:, columns], head_rows(out_low, group), NN)
+            put_chunk(d_kv, chunk, group, k_part.astype(jnp.bfloat16))
+            put_chunk(d_kv, chunk, KV_HEADS + group, v_part.astype(jnp.bfloat16))
         return carry
 
     lax.fori_loop(low, high, step, 0)
@@ -274,11 +298,14 @@
     dq_low,
     d_mine,
     d_other,
-    dq,
+    bias,
+    grads,
+    weights,
 ):
     row = Row(lengths)
     d_mine[...] = jnp.zeros(d_mine.shape, d_mine.dtype)
     d_other[...] = jnp.zeros(d_other.shape, d_other.dtype)
+    fill_bias(row, row.low, bias)
     w = jnp.concatenate(
         [
             jnp.concatenate([upstream[2 * d + c] for d in range(DOCS)] * 2, axis=0)
@@ -291,56 +318,46 @@
     unit = docs * doc_inv
     inner = jnp.sum(unit * w, axis=1, keepdims=True)
     doc_grad = doc_inv * (w - unit * inner) / row.length_column()
-    low_grad = doc_grad.astype(jnp.bfloat16)
-    member_low = row.member.astype(jnp.bfloat16)
-    out_low[...] = mm(member_low, low_grad, TN).astype(jnp.bfloat16)
-    for group in range(KV_HEADS):
-        columns = slice(group * GROUP_W, (group + 1) * GROUP_W)
-        for h in range(PER_GROUP):
-            at = head_columns(group, h)
-            by_doc = mm(doc_grad[:, at], att[:, at], NN, FULL_ACCURACY)
-            one = jnp.sum(row.member * by_doc, axis=0, keepdims=True)
-            delta[:, at] = jnp.broadcast_to(one, (8, TOK))
-        dq[...] = jnp.zeros(dq.shape, jnp.float32)
-        back_part(
-            row,
-            row.low,
-            group,
-            q,
-            (mine, other),
-            lse[0:1, columns],
-            head_rows(out_low, group),
-            delta[0:1, columns],
-            dq,
-            (d_mine, d_other),
-        )
-        dq_low[:, columns] = dq[...]
+    big, small = halves(doc_grad)
+    member = row.member.astype(jnp.bfloat16)
+    out_low[...] = mm(member, big, TN).astype(jnp.bfloat16)
+    both = jnp.concatenate([big, small], axis=0)
+    twice = jnp.concatenate([member, member], axis=0)
+    for h in range(HEADS):
+        at = head(h)
+        one = jnp.sum(mm(both[:, at], twice, TN) * att[:, at], axis=0, keepdims=True)
+        delta[:, at] = jnp.broadcast_to(one, (8, TOK))
+    dq_low[...] = jnp.zeros(dq_low.shape, jnp.float32)
+    kv, d_kv = (mine, other), (d_mine, d_other)
+    back_part(row.low, q, kv, bias, lse, out_low, delta, dq_low, d_kv, grads, weights)
 
 
 def back_own_kernel(
-    lengths, q, mine, other, lse, out_low, delta, dq_low, grad_q, d_mine, d_other, dq
+    lengths,
+    q,
+    mine,
+    other,
+    lse,
+    out_low,
+    delta,
+    dq_low,
+    grad_q,
+    d_mine,
+    d_other,
+    bias,
+    dq,
+    grads,
+    weights,
 ):
     row = Row(lengths)
     d_mine[...] = jnp.zeros(d_mine.shape, d_mine.dtype)
     d_other[...] = jnp.zeros(d_other.shape, d_other.dtype)
-    for group in range(KV_HEADS):
-        columns = slice(group * GROUP_W, (group + 1) * GROUP_W)
-        dq[...] = dq_low[:, columns]
-        back_part(
-            row,
-            row.own,
-            group,
-            q,
-            (mine, other),
-            lse[0:1, columns],
-            head_rows(out_low, group),
-            delta[0:1, columns],
-            dq,
-            (d_mine, d_other),
-        )
-        for h in range(PER_GROUP):
-            block = dq[:, h * TOK : (h + 1) * TOK]
-            grad_q[:, head_columns(group, h)] = (block.T * FACTOR).astype(jnp.bfloat16)
+    fill_bias(row, row.own, bias)
+    dq[...] = dq_low[...]
+    kv, d_kv = (mine, other), (d_mine, d_other)
+    back_part(row.own, q, kv, bias, lse, out_low, delta, dq, d_kv, grads, weights)
+    for h in range(HEADS):
+        grad_q[:, head(h)] = (dq[:, head(h)].T * FACTOR).astype(jnp.bfloat16)
 
 
 F32, BF16 = jnp.float32, jnp.bfloat16
@@ -367,18 +384,20 @@
 
 
 TERMS = shape((CHUNKS, TOK, 2 * KVW), BF16)
-HELD = pltpu.VMEM((CHUNKS, CHUNK, GROUP_W), F32)
-WIDE = pltpu.VMEM((HEAD_DIM, GROUP_W), F32)
+WIDE = pltpu.VMEM((HEAD_DIM, EMB), F32)
+BIAS = pltpu.VMEM((CHUNKS, CHUNK, TOK), F32)
+STATS = pltpu.VMEM((2, HEADS, TOK), F32)
+ROUNDED = pltpu.VMEM((CHUNK, EMB), BF16)
 
 
 def attend_own(lengths, *arrays):
     outs = (shape((HEAD_DIM, EMB), F32), shape((8, EMB), F32))
-    return run(attend_own_kernel, "attend_own", outs, [HELD, WIDE], lengths, *arrays)
+    return run(attend_own_kernel, "attend_own", outs, [BIAS, STATS, ROUNDED, WIDE], lengths, *arrays)
 
 
 def attend_low(lengths, *arrays):
     outs = (shape((HEAD_DIM, EMB), F32), shape((8, EMB), F32), shape((8, 1, PIECE), F32))
-    scratch = [HELD, WIDE, pltpu.VMEM((8, EMB), F32)]
+    scratch = [BIAS, STATS, ROUNDED, WIDE, pltpu.VMEM((8, EMB), F32)]
     return run(attend_low_kernel, "attend_low", outs, scratch, lengths, *arrays)
 
 
@@ -399,12 +418,12 @@
         TERMS,
         TERMS,
     )
-    return run(back_low_kernel, "back_low", outs, [WIDE], lengths, *arrays)
+    return run(back_low_kernel, "back_low", outs, [BIAS, ROUNDED, ROUNDED], lengths, *arrays)
 
 
 def back_own(lengths, *arrays):
     outs = (shape((TOK, EMB), BF16), TERMS, TERMS)
-    return run(back_own_kernel, "back_own", outs, [WIDE], lengths, *arrays)
+    return run(back_own_kernel, "back_own", outs, [BIAS, WIDE, ROUNDED, ROUNDED], lengths, *arrays)
 
 
 def to_all(block, axes, count):
@@ -454,10 +473,12 @@
     out_low, delta, dq_low, d_mine, d_other = back_low(
         lengths, q, low_mine, low_other, att, lse, own_docs, upstream
     )
+    paired = pair_terms(d_mine, d_other)
+    paired, dq_low = lax.optimization_barrier((paired, dq_low))
     grad_q, own_d_mine, own_d_other = back_own(
         lengths, q, own_mine, own_other, lse, out_low, delta, dq_low
     )
-    low_terms = lax.all_to_all(pair_terms(d_mine, d_other), "x", 0, 0)
+    low_terms = lax.all_to_all(paired, "x", 0, 0)
     low_sum = added(low_terms).astype(BF16)
     own_paired = pair_terms(own_d_mine, own_d_other)
     low_sum, own_paired = lax.optimization_barrier((low_sum, own_paired))

time: 195 us -> 195 us (level)
  the two profiles are of different devices: /device:TPU:42 before, /device:TPU:34 now
where the time goes in v4:
time: 195 us; the launch traced here: 194 us
  blocking collectives  78.4 us (40%)
  starting transfers between devices  49 us (25%)
  waiting for transfers between devices  40.7 us (21%)
  Pallas kernels  14.3 us (7%)
  local copies, waits for them, and re-layouts  6.37 us (3%)
  other arithmetic  4.13 us (2%)
    all_to_all x3, blocking collectives, to_all(): lax.all_to_all(jnp.broadcast_to(block[None], (count,) + block.shape), axe...  51.5 us
    ppermute x1, waiting for transfers between devices, per_device(): from_high = lax.ppermute(low_sum, 'zhi', [(1, 0)])  20.5 us
    all_to_all x1, blocking collectives, per_device(): terms = added(lax.all_to_all(terms, ('y', 'zlo'), 0, 0))  16.7 us
    ppermute x1, starting transfers between devices, per_device(): kv_low = lax.ppermute(kv, 'zhi', [(0, 1)])  14.8 us
    pallas_call x6, Pallas kernels, run(): pl.pallas_call(kernel, out_shape=outs, in_specs=[smem] * len(first) + [vm...  14.3 us
    ppermute x1, waiting for transfers between devices, per_device(): kv_low = lax.ppermute(kv, 'zhi', [(0, 1)])  10.6 us
    all_to_all x1, blocking collectives, per_device(): part = added(lax.all_to_all(pieces, NEAR, 0, 0))  10.2 us
    ppermute x5, starting transfers between devices, swap_cores(): return lax.ppermute(block, 'core', [(0, 1), (1, 0)])  9.81 us
  transfers between devices with their start and end apart: 11, of which 6 were waited for; matrix products, arithmetic and copies ran while one was open for 1% of the time, Pallas kernels for 5%

profile of v4, /device:TPU:34, one launch (start us, length us, event | category | flops | bytes accessed | tf_op | source)
XLA Modules:
  0.0 193.7 jit_solution(2671689134986436298)
XLA Ops:
  0.6 0.9 pad_maximum_fusion
  1.5 0.8 broadcast_in_dim.44
  2.4 4.8 %all-to-all-start = ((bf16[4,128,512]{2,1,0:T(8,128)(2,1)}), bf16[4,128,512]{2,1,0:T(8,128)(2,1)S(1)}, u32[]{:S(2)}, u32[]{:S(2)}) async-start(bf16[4,128,512]{2,1,0:T(8,128)(2,1)} %broadcast_in_dim.44), calls=%async_computation | async-start | bytes 1048576 | tf_op jit(solution)/shard_map/all_to_all | solution.py:430
  7.2 14.8 %collective-permute-start = (bf16[128,512]{1,0:T(8,128)(2,1)S(1)}, bf16[128,512]{1,0:T(8,128)(2,1)S(1)}, u32[]{:S(2)}, u32[]{:S(2)}) collective-permute-start(bf16[128,512]{1,0:T(8,128)(2,1)S(1)} %pad_maximum_fusion), channel_id=1, source_target_pairs={{0,8},{1,9},{2,10},{3,11},{4,12},{5,13},{6,14},{7,15},{16,24},{17,... | collective-permute-start | bytes 393224 | tf_op jit(solution)/shard_map/ppermute | solution.py:452
  22.0 10.6 %collective-permute-done = bf16[128,512]{1,0:T(8,128)(2,1)S(1)} collective-permute-done((bf16[128,512]{1,0:T(8,128)(2,1)S(1)}, bf16[128,512]{1,0:T(8,128)(2,1)S(1)}, u32[]{:S(2)}, u32[]{:S(2)}) %collective-permute-start) | collective-permute-done | bytes 131104 | tf_op jit(solution)/shard_map/ppermute | solution.py:452
  32.6 0.0 all-to-all-done.mine
  32.6 0.8 broadcast_in_dim.45
  33.4 4.9 %all-to-all-start.1 = ((bf16[4,128,512]{2,1,0:T(8,128)(2,1)}), bf16[4,128,512]{2,1,0:T(8,128)(2,1)S(1)}, u32[]{:S(2)}, u32[]{:S(2)}) async-start(bf16[4,128,512]{2,1,0:T(8,128)(2,1)} %broadcast_in_dim.45), calls=%async_computation.1 | async-start | bytes 1048576 | tf_op jit(solution)/shard_map/all_to_all | solution.py:430
  38.4 2.0 %collective-permute-start.2 = (bf16[4,128,512]{2,1,0:T(8,128)(2,1)S(1)}, bf16[4,128,512]{2,1,0:T(8,128)(2,1)S(1)}, u32[]{:S(2)}, u32[]{:S(2)}) collective-permute-start(bf16[4,128,512]{2,1,0:T(8,128)(2,1)S(1)} %all-to-all-done.mine), channel_id=1, source_target_pairs={{0,1},{1,0},{2,3},{3,2},{4,5},{5,4},{6,7},{7,6},{8,9},{9,8},{10,11... | collective-permute-start | bytes 1572872 | tf_op jit(solution)/shard_map/ppermute | solution.py:434
  40.4 5.0 %all-to-all-done.1.mine = bf16[4,128,512]{2,1,0:T(8,128)(2,1)S(1)} async-done(((bf16[4,128,512]{2,1,0:T(8,128)(2,1)}), bf16[4,128,512]{2,1,0:T(8,128)(2,1)S(1)}, u32[]{:S(2)}, u32[]{:S(2)}) %all-to-all-start.1) | async-done | bytes 524320 | tf_op jit(solution)/shard_map/all_to_all | solution.py:430
  45.4 1.9 collective-permute-start.1
  47.4 0.0 collective-permute-done.2.other
  47.4 3.1 %attend_own.1 = (f32[128,1792]{1,0:T(8,128)S(1)}, f32[8,1792]{1,0:T(8,128)S(1)}) custom-call(s32[1,4]{1,0:T(1,128)S(1)} %copy-done.8, bf16[128,1792]{1,0:T(8,128)(2,1)S(1)} %bitcast.19, bf16[4,128,512]{2,1,0:T(8,128)(2,1)S(1)} %all-to-all-done.mine, bf16[4,128,512]{2,1,0:T(8,128)(2,1)S(1)} %collective-permute-done.2.other), custom_call_target="tpu_custom_call" | custom-call | tf_op jit(solution)/shard_map/attend_own/pallas_call | solution.py:374
  50.5 0.0 collective-permute-done.1.other
  50.5 1.1 attend_low.1
  51.6 10.2 %all_to_all.45 = f32[8,1,896]{2,1,0:T(1,128)S(1)} all-to-all(f32[8,1,896]{2,1,0:T(1,128)S(1)} %get-tuple-element.33), channel_id=1, replica_groups=mesh['zlo'=8,'y'=4,'zhi'=2,'x'=4,'core'=2] {'x','core'}, dimensions={0} | all-to-all | bytes 57344 | tf_op jit(solution)/shard_map/all_to_all | solution.py:461
  61.9 27.0 %all_to_all.46 = f32[16,1,896]{2,1,0:T(1,128)S(1)} all-to-all(f32[16,1,896]{2,1,0:T(1,128)S(1)} %broadcast_in_dim.47), channel_id=1, replica_groups=mesh['zlo'=8,'y'=4,'zhi'=2,'x'=4,'core'=2] {'zlo','zhi'}, dimensions={0} | all-to-all | bytes 114688 | tf_op jit(solution)/shard_map/all_to_all | solution.py:430
  89.0 0.0 copy-start.1
  89.0 16.7 %all_to_all.47 = f32[16,8,896]{2,1,0:T(8,128)S(1)} all-to-all(f32[16,8,896]{2,1,0:T(8,128)S(1)} %broadcast_in_dim.49), channel_id=1, replica_groups=mesh['zlo'=8,'y'=4,'zhi'=2,'x'=4,'core'=2] {'y','x'}, dimensions={0} | all-to-all | bytes 917504 | tf_op jit(solution)/shard_map/all_to_all | solution.py:430
  105.7 2.0 %collective-permute-start.3 = (f32[128,896]{1,0:T(8,128)S(1)}, f32[128,896]{1,0:T(8,128)S(1)}, u32[]{:S(2)}, u32[]{:S(2)}) collective-permute-start(f32[128,896]{1,0:T(8,128)S(1)} %bitcast.23), channel_id=1, source_target_pairs={{0,1},{1,0},{2,3},{3,2},{4,5},{5,4},{6,7},{7,6},{8,9},{9,8},{10,11... | collective-permute-start | bytes 1376264 | tf_op jit(solution)/shard_map/ppermute | solution.py:434
  107.8 1.8 collective-permute-done.3.docs_other
  109.5 1.6 contrast.1
  111.2 16.7 %all_to_all.48 = f32[32,1,896]{2,1,0:T(1,128)S(1)} all-to-all(f32[32,1,896]{2,1,0:T(1,128)S(1)} %get-tuple-element.38), channel_id=1, replica_groups=mesh['zlo'=8,'y'=4,'zhi'=2,'x'=4,'core'=2] {'y','zlo'}, dimensions={0} | all-to-all | bytes 229376 | tf_op jit(solution)/shard_map/all_to_all | solution.py:470
  127.9 0.1 fusion.2
  128.0 7.8 %all_to_all.49.upstream = f32[8,1,896]{2,1,0:T(1,128)S(1)} all-to-all(f32[8,1,896]{2,1,0:T(1,128)S(1)} %broadcast_in_dim.51), channel_id=1, replica_groups=mesh['zlo'=8,'y'=4,'zhi'=2,'x'=4,'core'=2] {'x','core'}, dimensions={0} | all-to-all | bytes 57344 | tf_op jit(solution)/shard_map/all_to_all | solution.py:430
  135.7 1.2 back_low.1
  136.9 0.0 copy-start.2
  137.0 0.9 copy-done.2
  137.9 1.9 collective-permute-start.4
  139.8 1.9 collective-permute-done.4
  141.7 0.9 add_convert_fusion.1
  142.6 5.5 %all-to-all-start.7 = ((bf16[4,128,512]{2,1,0:T(8,128)(2,1)}), bf16[4,128,512]{2,1,0:T(8,128)(2,1)}, u32[]{:S(2)}, u32[]{:S(2)}) async-start(bf16[4,128,512]{2,1,0:T(8,128)(2,1)} %add_convert_fusion.1), calls=%async_computation.7 | async-start | bytes 1048576 | tf_op jit(solution)/shard_map/all_to_all | solution.py:481
  148.2 1.2 copy-done.3
  149.3 1.0 copy-done.5
  150.3 0.8 copy-done.7
  151.2 5.0 %back_own.1 = (bf16[128,1792]{1,0:T(8,128)(2,1)}, bf16[4,128,512]{2,1,0:T(8,128)(2,1)S(1)}, bf16[4,128,512]{2,1,0:T(8,128)(2,1)}) custom-call(s32[1,4]{1,0:T(1,128)S(1)} %copy-done.8, bf16[128,1792]{1,0:T(8,128)(2,1)S(1)} %bitcast.22, bf16[4,128,512]{2,1,0:T(8,128)(2,1)S(1)} %all-to-all-done.mine, bf16[4,128,512]{2,1,0:T(8,128)(2,1)S(1)} %collective-permute-done.2.other, ...), custom_call_target="tpu_custom_call" | custom-call | tf_op jit(solution)/shard_map/back_own/pallas_call | solution.py:374
  156.2 1.9 collective-permute-start.5
  158.1 0.0 all-to-all-done.7
  158.1 1.2 fusion.1
  159.3 0.9 collective-permute-done.5
  160.2 0.9 add_convert_fusion
  161.2 7.8 %all-to-all-start.8 = ((bf16[4,128,512]{2,1,0:T(8,128)(2,1)}), bf16[4,128,512]{2,1,0:T(8,128)(2,1)S(1)}, u32[]{:S(2)}, u32[]{:S(2)}) async-start(bf16[4,128,512]{2,1,0:T(8,128)(2,1)} %add_convert_fusion), calls=%async_computation.8 | async-start | bytes 1048576 | tf_op jit(solution)/shard_map/all_to_all | solution.py:486
  169.0 1.3 collective-permute-start.6
  170.3 2.2 %query_back.1 = f32[128,1792]{1,0:T(8,128)} custom-call(bf16[128,1792]{1,0:T(8,128)(2,1)S(1)} %copy-done.1, f32[128,896]{1,0:T(8,128)S(1)} %bitcast.25, f32[128,896]{1,0:T(8,128)S(1)} %collective-permute-done.3.docs_other, f32[128,128]{1,0:T(8,128)S(1)} %get-tuple-element.49.coefficient), custom_call_target="tpu_custom_call" | custom-call | tf_op jit(solution)/shard_map/query_back/pallas_call | solution.py:374
  172.4 20.5 %collective-permute-done.6 = bf16[128,512]{1,0:T(8,128)(2,1)S(1)} collective-permute-done((bf16[128,512]{1,0:T(8,128)(2,1)S(1)}, bf16[128,512]{1,0:T(8,128)(2,1)S(1)}, u32[]{:S(2)}, u32[]{:S(2)}) %collective-permute-start.6) | collective-permute-done | bytes 131104 | tf_op jit(solution)/shard_map/ppermute | solution.py:485
  193.0 0.0 all-to-all-done.8
  193.0 0.1 fusion
  193.1 0.7 slice_bitcast_fusion
  (20 shorter events, 0.2 us)
Async XLA Ops:
  2.4 30.2 %all-to-all-start = ((bf16[4,128,512]{2,1,0:T(8,128)(2,1)}), bf16[4,128,512]{2,1,0:T(8,128)(2,1)S(1)}, u32[]{:S(2)}, u32[]{:S(2)}) async-start(bf16[4,128,512]{2,1,0:T(8,128)(2,1)} %broadcast_in_dim.44), calls=%async_computation | async-start | bytes 1048576 | tf_op jit(solution)/shard_map/all_to_all | solution.py:430
  7.2 25.4 %collective-permute-start = (bf16[128,512]{1,0:T(8,128)(2,1)S(1)}, bf16[128,512]{1,0:T(8,128)(2,1)S(1)}, u32[]{:S(2)}, u32[]{:S(2)}) collective-permute-start(bf16[128,512]{1,0:T(8,128)(2,1)S(1)} %pad_maximum_fusion), channel_id=1, source_target_pairs={{0,8},{1,9},{2,10},{3,11},{4,12},{5,13},{6,14},{7,15},{16,24},{17,... | collective-permute-start | bytes 393224 | tf_op jit(solution)/shard_map/ppermute | solution.py:452
  33.4 13.9 %copy-start = (bf16[1,128,1792]{2,1,0:T(8,128)(2,1)S(1)}, bf16[1,128,1792]{2,1,0:T(8,128)(2,1)}, u32[]{:S(2)}) copy-start(bf16[1,128,1792]{2,1,0:T(8,128)(2,1)} %param.6) | copy-start | bytes 1376260
  33.4 12.0 %all-to-all-start.1 = ((bf16[4,128,512]{2,1,0:T(8,128)(2,1)}), bf16[4,128,512]{2,1,0:T(8,128)(2,1)S(1)}, u32[]{:S(2)}, u32[]{:S(2)}) async-start(bf16[4,128,512]{2,1,0:T(8,128)(2,1)} %broadcast_in_dim.45), calls=%async_computation.1 | async-start | bytes 1048576 | tf_op jit(solution)/shard_map/all_to_all | solution.py:430
  38.4 9.0 %copy-start.8 = (s32[1,4]{1,0:T(1,128)S(1)}, s32[1,4]{1,0:T(1,128)}, u32[]{:S(2)}) copy-start(s32[1,4]{1,0:T(1,128)} %lengths.7) | copy-start | bytes 52
  38.4 9.0 %collective-permute-start.2 = (bf16[4,128,512]{2,1,0:T(8,128)(2,1)S(1)}, bf16[4,128,512]{2,1,0:T(8,128)(2,1)S(1)}, u32[]{:S(2)}, u32[]{:S(2)}) collective-permute-start(bf16[4,128,512]{2,1,0:T(8,128)(2,1)S(1)} %all-to-all-done.mine), channel_id=1, source_target_pairs={{0,1},{1,0},{2,3},{3,2},{4,5},{5,4},{6,7},{7,6},{8,9},{9,8},{10,11... | collective-permute-start | bytes 1572872 | tf_op jit(solution)/shard_map/ppermute | solution.py:434
  45.4 5.1 %collective-permute-start.1 = (bf16[4,128,512]{2,1,0:T(8,128)(2,1)S(1)}, bf16[4,128,512]{2,1,0:T(8,128)(2,1)S(1)}, u32[]{:S(2)}, u32[]{:S(2)}) collective-permute-start(bf16[4,128,512]{2,1,0:T(8,128)(2,1)S(1)} %all-to-all-done.1.mine), channel_id=1, source_target_pairs={{0,1},{1,0},{2,3},{3,2},{4,5},{5,4},{6,7},{7,6},{8,9},{9,8},{10,11... | collective-permute-start | bytes 1572872 | tf_op jit(solution)/shard_map/ppermute | solution.py:434
  89.0 20.5 %copy-start.1 = (bf16[128,1792]{1,0:T(8,128)(2,1)S(1)}, bf16[128,1792]{1,0:T(8,128)(2,1)}, u32[]{:S(2)}) copy-start(bf16[128,1792]{1,0:T(8,128)(2,1)} %q.3) | copy-start | bytes 1376260
  105.7 3.8 %copy-start.9 = (s32[128]{0:T(128)S(1)}, s32[128]{0:T(128)}, u32[]{:S(2)}) copy-start(s32[128]{0:T(128)} %param.11) | copy-start | bytes 1540
  105.7 3.8 %collective-permute-start.3 = (f32[128,896]{1,0:T(8,128)S(1)}, f32[128,896]{1,0:T(8,128)S(1)}, u32[]{:S(2)}, u32[]{:S(2)}) collective-permute-start(f32[128,896]{1,0:T(8,128)S(1)} %bitcast.23), channel_id=1, source_target_pairs={{0,1},{1,0},{2,3},{3,2},{4,5},{5,4},{6,7},{7,6},{8,9},{9,8},{10,11... | collective-permute-start | bytes 1376264 | tf_op jit(solution)/shard_map/ppermute | solution.py:434
  136.9 0.9 copy-start.2
  137.9 4.7 %copy-start.4 = (bf16[128,1792]{1,0:T(8,128)(2,1)}, bf16[128,1792]{1,0:T(8,128)(2,1)S(1)}, u32[]{:S(2)}) copy-start(bf16[128,1792]{1,0:T(8,128)(2,1)S(1)} %get-tuple-element.43.out_low) | copy-start | bytes 1376260
  137.9 4.7 %copy-start.6 = (f32[8,1792]{1,0:T(8,128)}, f32[8,1792]{1,0:T(8,128)S(1)}, u32[]{:S(2)}) copy-start(f32[8,1792]{1,0:T(8,128)S(1)} %get-tuple-element.44.delta) | copy-start | bytes 172036
  137.9 3.8 %collective-permute-start.4 = (bf16[4,128,512]{2,1,0:T(8,128)(2,1)S(1)}, bf16[4,128,512]{2,1,0:T(8,128)(2,1)S(1)}, u32[]{:S(2)}, u32[]{:S(2)}) collective-permute-start(bf16[4,128,512]{2,1,0:T(8,128)(2,1)S(1)} %get-tuple-element.40), channel_id=1, source_target_pairs={{0,1},{1,0},{2,3},{3,2},{4,5},{5,4},{6,7},{7,6},{8,9},{9,8},{10,11... | collective-permute-start | bytes 1572872 | tf_op jit(solution)/shard_map/ppermute | solution.py:434
  142.6 15.5 %all-to-all-start.7 = ((bf16[4,128,512]{2,1,0:T(8,128)(2,1)}), bf16[4,128,512]{2,1,0:T(8,128)(2,1)}, u32[]{:S(2)}, u32[]{:S(2)}) async-start(bf16[4,128,512]{2,1,0:T(8,128)(2,1)} %add_convert_fusion.1), calls=%async_computation.7 | async-start | bytes 1048576 | tf_op jit(solution)/shard_map/all_to_all | solution.py:481
  148.1 1.2 copy-start.3
  149.3 1.0 copy-start.5
  150.3 0.8 copy-start.7
  156.2 4.0 %collective-permute-start.5 = (bf16[4,128,512]{2,1,0:T(8,128)(2,1)}, bf16[4,128,512]{2,1,0:T(8,128)(2,1)S(1)}, u32[]{:S(2)}, u32[]{:S(2)}) collective-permute-start(bf16[4,128,512]{2,1,0:T(8,128)(2,1)} %get-tuple-element.47), channel_id=1, source_target_pairs={{0,1},{1,0},{2,3},{3,2},{4,5},{5,4},{6,7},{7,6},{8,9},{9,8},{10,11... | collective-permute-start | bytes 1572872 | tf_op jit(solution)/shard_map/ppermute | solution.py:434
  161.2 31.8 %all-to-all-start.8 = ((bf16[4,128,512]{2,1,0:T(8,128)(2,1)}), bf16[4,128,512]{2,1,0:T(8,128)(2,1)S(1)}, u32[]{:S(2)}, u32[]{:S(2)}) async-start(bf16[4,128,512]{2,1,0:T(8,128)(2,1)} %add_convert_fusion), calls=%async_computation.8 | async-start | bytes 1048576 | tf_op jit(solution)/shard_map/all_to_all | solution.py:486
  169.0 24.0 %collective-permute-start.6 = (bf16[128,512]{1,0:T(8,128)(2,1)S(1)}, bf16[128,512]{1,0:T(8,128)(2,1)S(1)}, u32[]{:S(2)}, u32[]{:S(2)}) collective-permute-start(bf16[128,512]{1,0:T(8,128)(2,1)S(1)} %fusion.1), channel_id=1, source_target_pairs={{8,0},{9,1},{10,2},{11,3},{12,4},{13,5},{14,6},{15,7},{24,16},{25,... | collective-permute-start | bytes 393224 | tf_op jit(solution)/shard_map/ppermute | solution.py:485

commit v5 on v4

--- a/solution.py
+++ b/solution.py
@@ -21,6 +21,9 @@
 CHUNKS = HALF // CHUNK
 PIECE = EMB // 2
 NDOC = 128
+SHARE = 32
+SHARED = 8 * SHARE
+SHARE_W = 2048
 
 FACTOR = HEAD_DIM ** (-0.5)
 INVERSE_TEMPER = 0.05
@@ -199,41 +202,78 @@
             pieces[2 * d + c] = mean[d : d + 1, c * PIECE : (c + 1) * PIECE]
 
 
-def contrast_kernel(q, positive, docs_mine, docs_other, coefficient, terms, own_docs):
-    z_lo, y, _, x, core = place()
+def own_rows(core, left_or_mine, right_or_other):
+    return jnp.where(core == 1, right_or_other, left_or_mine)
+
+
+def share_kernel(q, positive, out):
+    _, _, _, x, _ = place()
+    first = x * SHARE
+    rows = q[pl.ds(pl.multiple_of(first, SHARE), SHARE), :]
+    out[:, :EMB] = rows
+    values = rows.astype(jnp.float32)
+    inverse = lax.rsqrt(jnp.sum(values * values, axis=1, keepdims=True) + EPSILON)
+    lane = lax.broadcasted_iota(jnp.int32, (SHARE, 128), 1)
+    row = lax.broadcasted_iota(jnp.int32, (SHARE, 128), 0)
+    doc = jnp.sum(
+        jnp.where(lane == first + row, positive[...].astype(jnp.float32), 0.0),
+        axis=1,
+        keepdims=True,
+    )
+    extra = jnp.where(lane == 0, doc, 0.0)
+    rest = inverse
+    for i in range(1, 4):
+        piece = rest.astype(jnp.bfloat16).astype(jnp.float32)
+        extra = jnp.where(lane == i, piece, extra)
+        rest = rest - piece
+    out[:, EMB : EMB + 128] = extra.astype(jnp.bfloat16)
+    out[:, EMB + 128 :] = jnp.zeros((SHARE, SHARE_W - EMB - 128), jnp.bfloat16)
+
+
+def contrast_kernel(shared, docs_mine, docs_other, terms, own_docs, coefficient):
+    z_lo, y, _, _, core = place()
     d_mine, d_other = docs_mine[...], docs_other[...]
     doc_inv = lax.rsqrt(
         jnp.sum(d_mine * d_mine, axis=1, keepdims=True)
         + jnp.sum(d_other * d_other, axis=1, keepdims=True)
         + EPSILON
     )
-    q_all = q[...].astype(jnp.float32)
-    query_inv = lax.rsqrt(jnp.sum(q_all * q_all, axis=1, keepdims=True) + EPSILON)
-    q_unit = q_all * query_inv
-    q_mine = jnp.where(core == 1, q_unit[:, PIECE:], q_unit[:, :PIECE])
-    q_other = jnp.where(core == 1, q_unit[:, :PIECE], q_unit[:, PIECE:])
-    logits = mm(d_mine * doc_inv, q_mine, NT, FULL_ACCURACY)
-    logits = (logits + mm(d_other * doc_inv, q_other, NT, FULL_ACCURACY)) / INVERSE_TEMPER
-    exps = jnp.exp(logits)
-    at = lax.broadcasted_iota(jnp.int32, (NDOC, 128), 0)
+    extra = shared[:, EMB : EMB + 128].astype(jnp.float32).T
+    target_doc = extra[0:1]
+    query_inv = extra[1:2] + extra[2:3] + extra[3:4]
+    left = own_rows(core, d_mine, d_other) * doc_inv
+    right = own_rows(core, d_other, d_mine) * doc_inv
+    logits = jnp.zeros((NDOC, SHARED), jnp.float32)
+    for part, at in ((left, slice(0, PIECE)), (right, slice(PIECE, EMB))):
+        for piece in halves(part):
+            logits = logits + mm(piece, shared[:, at], NT)
+    exps = jnp.exp(logits * query_inv / INVERSE_TEMPER)
+    at = lax.broadcasted_iota(jnp.int32, (NDOC, SHARED), 0)
     doc = ((at % 8) * 4 + at // 32) * DOCS + (at // 8) % 4
-    target = (doc == positive[...]).astype(jnp.float32)
-    coefficient[...] = exps / jnp.sum(exps, axis=0, keepdims=True) - target
-    near = jnp.concatenate(
-        [coefficient[pl.ds(pl.multiple_of(b * 32 + x * 8, 8), 8), :] for b in range(4)], axis=0
-    )
-    near_terms = mm(near, q_mine, NN, FULL_ACCURACY) / INVERSE_TEMPER
-    for r in range(32):
-        terms[r] = near_terms[r : r + 1]
+    target = (doc.astype(jnp.float32) == target_doc).astype(jnp.float32)
+    share = exps / jnp.sum(exps, axis=0, keepdims=True) - target
+    coefficient[...] = share * query_inv / INVERSE_TEMPER
     own_docs[...] = jnp.zeros((8, EMB), jnp.float32)
+    near = []
     for d in range(DOCS):
         r = y * 32 + d * 8 + z_lo
         a, b = docs_mine[pl.ds(r, 1), :], docs_other[pl.ds(r, 1), :]
-        own_docs[d : d + 1, :PIECE] = jnp.where(core == 1, b, a)
-        own_docs[d : d + 1, PIECE:] = jnp.where(core == 1, a, b)
-
-
-def query_kernel(q, docs_mine, docs_other, coefficient, query_grad):
+        own_docs[d : d + 1, :PIECE] = own_rows(core, a, b)
+        own_docs[d : d + 1, PIECE:] = own_rows(core, b, a)
+        for other_y in range(4):
+            near.append(coefficient[pl.ds(other_y * 32 + d * 8 + z_lo, 1), :])
+    big, small = halves(jnp.concatenate(near, axis=0))
+    sums = mm(jnp.concatenate([big, small], axis=0), shared[:, :EMB], NN)
+    for d in range(DOCS):
+        for other_y in range(4):
+            r = d * 4 + other_y
+            one = sums[r : r + 1] + sums[16 + r : 17 + r]
+            for c in range(2):
+                row = 2 * d + c
+                terms[other_y, row : row + 1, :] = one[:, c * PIECE : (c + 1) * PIECE]
+
+
+def query_kernel(q, positive, docs_mine, docs_other, query_grad):
     _, _, _, _, core = place()
     d_mine, d_other = docs_mine[...], docs_other[...]
     doc_inv = lax.rsqrt(
@@ -241,15 +281,20 @@
         + jnp.sum(d_other * d_other, axis=1, keepdims=True)
         + EPSILON
     )
-    scaled = coefficient[...] * doc_inv
-    u_mine = mm(scaled, d_mine, TN, FULL_ACCURACY) / INVERSE_TEMPER
-    u_other = mm(scaled, d_other, TN, FULL_ACCURACY) / INVERSE_TEMPER
-    u_left = jnp.where(core == 1, u_other, u_mine)
-    u_right = jnp.where(core == 1, u_mine, u_other)
+    left = own_rows(core, d_mine, d_other) * doc_inv
+    right = own_rows(core, d_other, d_mine) * doc_inv
     q_all = q[...].astype(jnp.float32)
     query_inv = lax.rsqrt(jnp.sum(q_all * q_all, axis=1, keepdims=True) + EPSILON)
     q_unit = q_all * query_inv
     q_left, q_right = q_unit[:, :PIECE], q_unit[:, PIECE:]
+    logits = mm(left, q_left, NT, FULL_ACCURACY) + mm(right, q_right, NT, FULL_ACCURACY)
+    exps = jnp.exp(logits / INVERSE_TEMPER)
+    at = lax.broadcasted_iota(jnp.int32, (NDOC, 128), 0)
+    doc = ((at % 8) * 4 + at // 32) * DOCS + (at // 8) % 4
+    target = (doc == positive[...]).astype(jnp.float32)
+    coefficient = exps / jnp.sum(exps, axis=0, keepdims=True) - target
+    u_left = mm(coefficient, left, TN, FULL_ACCURACY) / INVERSE_TEMPER
+    u_right = mm(coefficient, right, TN, FULL_ACCURACY) / INVERSE_TEMPER
     inner = jnp.sum(q_left * u_left, axis=1, keepdims=True) + jnp.sum(
         q_right * u_right, axis=1, keepdims=True
     )
@@ -308,7 +353,7 @@
     fill_bias(row, row.low, bias)
     w = jnp.concatenate(
         [
-            jnp.concatenate([upstream[2 * d + c] for d in range(DOCS)] * 2, axis=0)
+            jnp.concatenate([upstream[2 * d + c : 2 * d + c + 1] for d in range(DOCS)] * 2, axis=0)
             for c in range(2)
         ],
         axis=1,
@@ -401,9 +446,15 @@
     return run(attend_low_kernel, "attend_low", outs, scratch, lengths, *arrays)
 
 
+def share(*arrays):
+    outs = (shape((SHARE, SHARE_W), BF16),)
+    return run(share_kernel, "share", outs, [], None, *arrays)[0]
+
+
 def contrast(*arrays):
-    outs = (shape((NDOC, 128), F32), shape((32, 1, PIECE), F32), shape((8, EMB), F32))
-    return run(contrast_kernel, "contrast", outs, [], None, *arrays)
+    outs = (shape((4, 8, PIECE), F32), shape((8, EMB), F32))
+    scratch = [pltpu.VMEM((NDOC, SHARED), F32)]
+    return run(contrast_kernel, "contrast", outs, scratch, None, *arrays)
 
 
 def query_back(*arrays):
@@ -451,6 +502,8 @@
     kv = jnp.concatenate([keys[0], values[0]], axis=1)
     kv_low = lax.ppermute(kv, "zhi", [(0, 1)])
     own_mine = to_all(kv, "x", 4)
+    positive = positive.reshape(1, 128)
+    shared = lax.all_gather(share(query_emb, positive), "zlo", axis=0, tiled=True)
     kv_low, own_mine = lax.optimization_barrier((kv_low, own_mine))
     own_other = swap_cores(own_mine)
     own_att, own_lse = attend_own(lengths, q, own_mine, own_other)
@@ -464,11 +517,9 @@
     docs_mine = to_all(column, ("y", "x"), 16).reshape(NDOC, PIECE)
     docs_other = swap_cores(docs_mine)
 
-    coefficient, terms, own_docs = contrast(
-        query_emb, positive.reshape(1, 128), docs_mine, docs_other
-    )
-    terms = added(lax.all_to_all(terms, ("y", "zlo"), 0, 0))
-    upstream = to_all(terms, NEAR, 8)
+    terms, own_docs = contrast(shared, docs_mine, docs_other)
+    terms = jnp.broadcast_to(terms[:, None], (4, 4, 8, PIECE)).reshape(16, 8, PIECE)
+    upstream = added(lax.all_to_all(terms, ("y", "x"), 0, 0))
 
     out_low, delta, dq_low, d_mine, d_other = back_low(
         lengths, q, low_mine, low_other, att, lse, own_docs, upstream
@@ -485,8 +536,8 @@
     from_high = lax.ppermute(low_sum, "zhi", [(1, 0)])
     own_terms = lax.all_to_all(own_paired, "x", 0, 0)
     own_sum = added(own_terms)
-    coefficient, low_sum = lax.optimization_barrier((coefficient, low_sum))
-    query_grad = query_back(query_emb, docs_mine, docs_other, coefficient)
+    docs_mine, low_sum = lax.optimization_barrier((docs_mine, low_sum))
+    query_grad = query_back(query_emb, positive, docs_mine, docs_other)
     query_grad, from_high = lax.optimization_barrier((query_grad, from_high))
     total = (own_sum + from_high.astype(F32)).astype(BF16)
     return (query_grad, grad_q[None], total[None, :, :KVW], total[None, :, KVW:])

time: 195 us -> 199 us (1.021)
  the two profiles are of different devices: /device:TPU:34 before, /device:TPU:2 now
where the time goes in v5:
time: 199 us; the launch traced here: 198 us
  blocking collectives  78.4 us (39%)
  starting transfers between devices  49.9 us (25%)
  waiting for transfers between devices  27 us (14%)
  Pallas kernels  17.9 us (9%)
  between operations  14.3 us (7%)
  local copies, waits for them, and re-layouts  6.41 us (3%)
  other arithmetic  4.08 us (2%)
    all_to_all x2, blocking collectives, to_all(): lax.all_to_all(jnp.broadcast_to(block[None], (count,) + block.shape), axe...  51.8 us
    pallas_call x7, Pallas kernels, run(): pl.pallas_call(kernel, out_shape=outs, in_specs=[smem] * len(first) + [vm...  17.9 us
    all_to_all x1, blocking collectives, per_device(): upstream = added(lax.all_to_all(terms, ('y', 'x'), 0, 0))  16.3 us
    all_to_all x2, starting transfers between devices, to_all(): lax.all_to_all(jnp.broadcast_to(block[None], (count,) + block.shape), axe...  14.3 us
    ppermute x1, starting transfers between devices, per_device(): kv_low = lax.ppermute(kv, 'zhi', [(0, 1)])  11.2 us
    all_to_all x1, blocking collectives, per_device(): part = added(lax.all_to_all(pieces, NEAR, 0, 0))  10.2 us
    ppermute x1, waiting for transfers between devices, per_device(): from_high = lax.ppermute(low_sum, 'zhi', [(1, 0)])  9.9 us
    ppermute x5, starting transfers between devices, swap_cores(): return lax.ppermute(block, 'core', [(0, 1), (1, 0)])  9.68 us
  transfers between devices with their start and end apart: 12, of which 7 were waited for; matrix products, arithmetic and copies ran while one was open for 1% of the time, Pallas kernels for 7%

profile of v5, /device:TPU:2, one launch (start us, length us, event | category | flops | bytes accessed | tf_op | source)
XLA Modules:
  0.0 197.9 jit_solution(14018281197017498949)
XLA Ops:
  7.2 0.9 pad_maximum_fusion
  8.1 0.8 broadcast_in_dim.20
  8.9 9.3 %all-to-all-start = ((bf16[4,128,512]{2,1,0:T(8,128)(2,1)}), bf16[4,128,512]{2,1,0:T(8,128)(2,1)S(1)}, u32[]{:S(2)}, u32[]{:S(2)}) async-start(bf16[4,128,512]{2,1,0:T(8,128)(2,1)} %broadcast_in_dim.20), calls=%async_computation | async-start | bytes 1048576 | tf_op jit(solution)/shard_map/all_to_all | solution.py:481
  18.2 11.2 %collective-permute-start = (bf16[128,512]{1,0:T(8,128)(2,1)S(1)}, bf16[128,512]{1,0:T(8,128)(2,1)S(1)}, u32[]{:S(2)}, u32[]{:S(2)}) collective-permute-start(bf16[128,512]{1,0:T(8,128)(2,1)S(1)} %pad_maximum_fusion), channel_id=1, source_target_pairs={{0,8},{1,9},{2,10},{3,11},{4,12},{5,13},{6,14},{7,15},{16,24},{17,... | collective-permute-start | bytes 393224 | tf_op jit(solution)/shard_map/ppermute | solution.py:503
  29.4 2.5 %collective-permute-done = bf16[128,512]{1,0:T(8,128)(2,1)S(1)} collective-permute-done((bf16[128,512]{1,0:T(8,128)(2,1)S(1)}, bf16[128,512]{1,0:T(8,128)(2,1)S(1)}, u32[]{:S(2)}, u32[]{:S(2)}) %collective-permute-start) | collective-permute-done | bytes 131104 | tf_op jit(solution)/shard_map/ppermute | solution.py:503
  31.9 0.8 broadcast_in_dim.21
  32.8 4.9 %all-to-all-start.1 = ((bf16[4,128,512]{2,1,0:T(8,128)(2,1)}), bf16[4,128,512]{2,1,0:T(8,128)(2,1)S(1)}, u32[]{:S(2)}, u32[]{:S(2)}) async-start(bf16[4,128,512]{2,1,0:T(8,128)(2,1)} %broadcast_in_dim.21), calls=%async_computation.1 | async-start | bytes 1048576 | tf_op jit(solution)/shard_map/all_to_all | solution.py:481
  37.7 2.0 %collective-permute-start.2 = (bf16[4,128,512]{2,1,0:T(8,128)(2,1)S(1)}, bf16[4,128,512]{2,1,0:T(8,128)(2,1)S(1)}, u32[]{:S(2)}, u32[]{:S(2)}) collective-permute-start(bf16[4,128,512]{2,1,0:T(8,128)(2,1)S(1)} %all-to-all-done.mine), channel_id=1, source_target_pairs={{0,1},{1,0},{2,3},{3,2},{4,5},{5,4},{6,7},{7,6},{8,9},{9,8},{10,11... | collective-permute-start | bytes 1572872 | tf_op jit(solution)/shard_map/ppermute | solution.py:485
  39.8 4.6 %all-to-all-done.1.mine = bf16[4,128,512]{2,1,0:T(8,128)(2,1)S(1)} async-done(((bf16[4,128,512]{2,1,0:T(8,128)(2,1)}), bf16[4,128,512]{2,1,0:T(8,128)(2,1)S(1)}, u32[]{:S(2)}, u32[]{:S(2)}) %all-to-all-start.1) | async-done | bytes 524320 | tf_op jit(solution)/shard_map/all_to_all | solution.py:481
  44.3 1.9 collective-permute-start.1
  46.3 0.8 share.1
  47.0 0.0 all-gather.2.cloned.1.call-update
  47.1 0.0 copy-start.11
  47.1 0.0 collective-permute-done.2.other
  47.1 0.6 copy-done.11
  47.7 3.1 %attend_own.1 = (f32[128,1792]{1,0:T(8,128)S(1)}, f32[8,1792]{1,0:T(8,128)S(1)}) custom-call(s32[1,4]{1,0:T(1,128)S(1)} %copy-done.11, bf16[128,1792]{1,0:T(8,128)(2,1)S(1)} %bitcast.22, bf16[4,128,512]{2,1,0:T(8,128)(2,1)S(1)} %all-to-all-done.mine, bf16[4,128,512]{2,1,0:T(8,128)(2,1)S(1)} %collective-permute-done.2.other), custom_call_target="tpu_custom_call" | custom-call | tf_op jit(solution)/shard_map/attend_own/pallas_call | solution.py:419
  50.8 0.0 collective-permute-done.1.other
  50.8 1.1 attend_low.1
  52.0 10.2 %all_to_all.40 = f32[8,1,896]{2,1,0:T(1,128)S(1)} all-to-all(f32[8,1,896]{2,1,0:T(1,128)S(1)} %get-tuple-element.32), channel_id=1, replica_groups=mesh['zlo'=8,'y'=4,'zhi'=2,'x'=4,'core'=2] {'x','core'}, dimensions={0} | all-to-all | bytes 57344 | tf_op jit(solution)/shard_map/all_to_all | solution.py:514
  62.3 37.4 %all_to_all.41 = f32[16,1,896]{2,1,0:T(1,128)S(1)} all-to-all(f32[16,1,896]{2,1,0:T(1,128)S(1)} %broadcast_in_dim.45), channel_id=1, replica_groups=mesh['zlo'=8,'y'=4,'zhi'=2,'x'=4,'core'=2] {'zlo','zhi'}, dimensions={0} | all-to-all | bytes 114688 | tf_op jit(solution)/shard_map/all_to_all | solution.py:481
  99.8 14.4 %all_to_all.42 = f32[16,8,896]{2,1,0:T(8,128)S(1)} all-to-all(f32[16,8,896]{2,1,0:T(8,128)S(1)} %broadcast_in_dim.47), channel_id=1, replica_groups=mesh['zlo'=8,'y'=4,'zhi'=2,'x'=4,'core'=2] {'y','x'}, dimensions={0} | all-to-all | bytes 917504 | tf_op jit(solution)/shard_map/all_to_all | solution.py:481
  114.2 1.9 collective-permute-start.3
  116.1 7.2 %all-gather.2.cloned.1.call-done.shared = bf16[256,2048]{1,0:T(8,128)(2,1)} async-done(((bf16[32,2048]{1,0:T(8,128)(2,1)}), bf16[256,2048]{1,0:T(8,128)(2,1)}) %all-gather.2.cloned.1.call-update) | async-done | bytes 1048592 | tf_op jit(solution)/shard_map/all_gather | solution.py:506
  123.3 0.0 collective-permute-done.3.docs_other
  123.3 1.2 copy-done.2
  124.5 2.2 %contrast.1 = (f32[4,8,896]{2,1,0:T(8,128)S(1)}, f32[8,1792]{1,0:T(8,128)S(1)}) custom-call(bf16[256,2048]{1,0:T(8,128)(2,1)S(1)} %copy-done.2, f32[128,896]{1,0:T(8,128)S(1)} %bitcast.27, f32[128,896]{1,0:T(8,128)} %collective-permute-done.3.docs_other), custom_call_target="tpu_custom_call" | custom-call | tf_op jit(solution)/shard_map/contrast/pallas_call | solution.py:419
  126.8 0.0 copy-start.4
  126.9 16.3 %all_to_all.43 = f32[16,8,896]{2,1,0:T(8,128)S(1)} all-to-all(f32[16,8,896]{2,1,0:T(8,128)S(1)} %bitcast.31), channel_id=1, replica_groups=mesh['zlo'=8,'y'=4,'zhi'=2,'x'=4,'core'=2] {'y','x'}, dimensions={0} | all-to-all | bytes 917504 | tf_op jit(solution)/shard_map/all_to_all | solution.py:522
  143.2 1.2 back_low.1
  144.4 0.0 copy-start.5
  144.4 0.9 copy-done.5
  145.3 1.9 collective-permute-start.4
  147.3 1.9 collective-permute-done.4
  149.1 0.9 add_convert_fusion.1
  150.1 5.7 %all-to-all-start.6 = ((bf16[4,128,512]{2,1,0:T(8,128)(2,1)}), bf16[4,128,512]{2,1,0:T(8,128)(2,1)}, u32[]{:S(2)}, u32[]{:S(2)}) async-start(bf16[4,128,512]{2,1,0:T(8,128)(2,1)} %add_convert_fusion.1), calls=%async_computation.6 | async-start | bytes 1048576 | tf_op jit(solution)/shard_map/all_to_all | solution.py:532
  155.8 1.2 copy-done.6
  157.0 5.0 %back_own.1 = (bf16[128,1792]{1,0:T(8,128)(2,1)}, bf16[4,128,512]{2,1,0:T(8,128)(2,1)S(1)}, bf16[4,128,512]{2,1,0:T(8,128)(2,1)}) custom-call(s32[1,4]{1,0:T(1,128)S(1)} %copy-done.11, bf16[128,1792]{1,0:T(8,128)(2,1)S(1)} %bitcast.25, bf16[4,128,512]{2,1,0:T(8,128)(2,1)S(1)} %all-to-all-done.mine, bf16[4,128,512]{2,1,0:T(8,128)(2,1)S(1)} %collective-permute-done.2.other, ...), custom_call_target="tpu_custom_call" | custom-call | tf_op jit(solution)/shard_map/back_own/pallas_call | solution.py:419
  162.0 1.9 collective-permute-start.5
  163.9 0.6 all-to-all-done.6
  164.5 1.2 fusion.1
  165.6 0.3 collective-permute-done.5
  166.0 0.9 add_convert_fusion
  166.9 7.8 %all-to-all-start.7 = ((bf16[4,128,512]{2,1,0:T(8,128)(2,1)}), bf16[4,128,512]{2,1,0:T(8,128)(2,1)S(1)}, u32[]{:S(2)}, u32[]{:S(2)}) async-start(bf16[4,128,512]{2,1,0:T(8,128)(2,1)} %add_convert_fusion), calls=%async_computation.7 | async-start | bytes 1048576 | tf_op jit(solution)/shard_map/all_to_all | solution.py:537
  174.7 1.3 collective-permute-start.6
  176.0 4.4 %query_back.1 = f32[128,1792]{1,0:T(8,128)} custom-call(bf16[128,1792]{1,0:T(8,128)(2,1)S(1)} %copy-done.1, s32[1,128]{1,0:T(1,128)S(1)} %bitcast.30, f32[128,896]{1,0:T(8,128)S(1)} %bitcast.28, f32[128,896]{1,0:T(8,128)} %collective-permute-done.3.docs_other), custom_call_target="tpu_custom_call" | custom-call | tf_op jit(solution)/shard_map/query_back/pallas_call | solution.py:419
  180.4 9.9 %collective-permute-done.6 = bf16[128,512]{1,0:T(8,128)(2,1)S(1)} collective-permute-done((bf16[128,512]{1,0:T(8,128)(2,1)S(1)}, bf16[128,512]{1,0:T(8,128)(2,1)S(1)}, u32[]{:S(2)}, u32[]{:S(2)}) %collective-permute-start.6) | collective-permute-done | bytes 131104 | tf_op jit(solution)/shard_map/ppermute | solution.py:536
  190.3 0.1 fusion
  190.4 0.7 slice_bitcast_fusion
  (29 shorter events, 0.2 us)
Async XLA Ops:
  8.9 23.0 %all-to-all-start = ((bf16[4,128,512]{2,1,0:T(8,128)(2,1)}), bf16[4,128,512]{2,1,0:T(8,128)(2,1)S(1)}, u32[]{:S(2)}, u32[]{:S(2)}) async-start(bf16[4,128,512]{2,1,0:T(8,128)(2,1)} %broadcast_in_dim.20), calls=%async_computation | async-start | bytes 1048576 | tf_op jit(solution)/shard_map/all_to_all | solution.py:481
  18.2 13.7 %collective-permute-start = (bf16[128,512]{1,0:T(8,128)(2,1)S(1)}, bf16[128,512]{1,0:T(8,128)(2,1)S(1)}, u32[]{:S(2)}, u32[]{:S(2)}) collective-permute-start(bf16[128,512]{1,0:T(8,128)(2,1)S(1)} %pad_maximum_fusion), channel_id=1, source_target_pairs={{0,8},{1,9},{2,10},{3,11},{4,12},{5,13},{6,14},{7,15},{16,24},{17,... | collective-permute-start | bytes 393224 | tf_op jit(solution)/shard_map/ppermute | solution.py:503
  32.8 13.5 %copy-start.1 = (bf16[128,1792]{1,0:T(8,128)(2,1)S(1)}, bf16[128,1792]{1,0:T(8,128)(2,1)}, u32[]{:S(2)}) copy-start(bf16[128,1792]{1,0:T(8,128)(2,1)} %q.3) | copy-start | bytes 1376260
  32.8 13.5 %copy-start.12 = (s32[128]{0:T(128)S(1)}, s32[128]{0:T(128)}, u32[]{:S(2)}) copy-start(s32[128]{0:T(128)} %param.11) | copy-start | bytes 1540
  32.8 11.6 %all-to-all-start.1 = ((bf16[4,128,512]{2,1,0:T(8,128)(2,1)}), bf16[4,128,512]{2,1,0:T(8,128)(2,1)S(1)}, u32[]{:S(2)}, u32[]{:S(2)}) async-start(bf16[4,128,512]{2,1,0:T(8,128)(2,1)} %broadcast_in_dim.21), calls=%async_computation.1 | async-start | bytes 1048576 | tf_op jit(solution)/shard_map/all_to_all | solution.py:481
  37.7 9.4 %copy-start = (bf16[1,128,1792]{2,1,0:T(8,128)(2,1)S(1)}, bf16[1,128,1792]{2,1,0:T(8,128)(2,1)}, u32[]{:S(2)}) copy-start(bf16[1,128,1792]{2,1,0:T(8,128)(2,1)} %param.6) | copy-start | bytes 1376260
  37.7 85.6 %all-gather.2.cloned.1.call-start = ((), (), s32[]{:S(2)}) async-start(), calls=%async_computation.8 | async-start | bytes 1179648 | tf_op jit(solution)/shard_map/all_gather | solution.py:506
  37.7 9.4 %collective-permute-start.2 = (bf16[4,128,512]{2,1,0:T(8,128)(2,1)S(1)}, bf16[4,128,512]{2,1,0:T(8,128)(2,1)S(1)}, u32[]{:S(2)}, u32[]{:S(2)}) collective-permute-start(bf16[4,128,512]{2,1,0:T(8,128)(2,1)S(1)} %all-to-all-done.mine), channel_id=1, source_target_pairs={{0,1},{1,0},{2,3},{3,2},{4,5},{5,4},{6,7},{7,6},{8,9},{9,8},{10,11... | collective-permute-start | bytes 1572872 | tf_op jit(solution)/shard_map/ppermute | solution.py:485
  44.3 6.5 %collective-permute-start.1 = (bf16[4,128,512]{2,1,0:T(8,128)(2,1)S(1)}, bf16[4,128,512]{2,1,0:T(8,128)(2,1)S(1)}, u32[]{:S(2)}, u32[]{:S(2)}) collective-permute-start(bf16[4,128,512]{2,1,0:T(8,128)(2,1)S(1)} %all-to-all-done.1.mine), channel_id=1, source_target_pairs={{0,1},{1,0},{2,3},{3,2},{4,5},{5,4},{6,7},{7,6},{8,9},{9,8},{10,11... | collective-permute-start | bytes 1572872 | tf_op jit(solution)/shard_map/ppermute | solution.py:485
  47.1 0.7 copy-start.11
  52.0 62.2 %copy-start.3 = (f32[128,1792]{1,0:T(8,128)}, f32[128,1792]{1,0:T(8,128)S(1)}, u32[]{:S(2)}) copy-start(f32[128,1792]{1,0:T(8,128)S(1)} %get-tuple-element.33.att) | copy-start | bytes 2752516
  114.2 9.1 %collective-permute-start.3 = (f32[128,896]{1,0:T(8,128)S(1)}, f32[128,896]{1,0:T(8,128)}, u32[]{:S(2)}, u32[]{:S(2)}) collective-permute-start(f32[128,896]{1,0:T(8,128)S(1)} %bitcast.26), channel_id=1, source_target_pairs={{0,1},{1,0},{2,3},{3,2},{4,5},{5,4},{6,7},{7,6},{8,9},{9,8},{10,11... | collective-permute-start | bytes 1376264 | tf_op jit(solution)/shard_map/ppermute | solution.py:485
  123.3 1.2 copy-start.2
  126.8 16.4 %copy-start.4 = (f32[128,1792]{1,0:T(8,128)S(1)}, f32[128,1792]{1,0:T(8,128)}, u32[]{:S(2)}) copy-start(f32[128,1792]{1,0:T(8,128)} %copy-done.3) | copy-start | bytes 2752516
  144.4 0.9 copy-start.5
  145.3 4.7 %copy-start.7 = (bf16[128,1792]{1,0:T(8,128)(2,1)}, bf16[128,1792]{1,0:T(8,128)(2,1)S(1)}, u32[]{:S(2)}) copy-start(bf16[128,1792]{1,0:T(8,128)(2,1)S(1)} %get-tuple-element.41.out_low) | copy-start | bytes 1376260
  145.3 4.7 %copy-start.9 = (f32[8,1792]{1,0:T(8,128)}, f32[8,1792]{1,0:T(8,128)S(1)}, u32[]{:S(2)}) copy-start(f32[8,1792]{1,0:T(8,128)S(1)} %get-tuple-element.42.delta) | copy-start | bytes 172036
  145.3 3.8 %collective-permute-start.4 = (bf16[4,128,512]{2,1,0:T(8,128)(2,1)S(1)}, bf16[4,128,512]{2,1,0:T(8,128)(2,1)S(1)}, u32[]{:S(2)}, u32[]{:S(2)}) collective-permute-start(bf16[4,128,512]{2,1,0:T(8,128)(2,1)S(1)} %get-tuple-element.38), channel_id=1, source_target_pairs={{0,1},{1,0},{2,3},{3,2},{4,5},{5,4},{6,7},{7,6},{8,9},{9,8},{10,11... | collective-permute-start | bytes 1572872 | tf_op jit(solution)/shard_map/ppermute | solution.py:485
  150.1 5.7 %copy-start.8 = (bf16[128,1792]{1,0:T(8,128)(2,1)S(1)}, bf16[128,1792]{1,0:T(8,128)(2,1)}, u32[]{:S(2)}) copy-start(bf16[128,1792]{1,0:T(8,128)(2,1)} %copy-done.7) | copy-start | bytes 1376260
  150.1 5.7 %copy-start.10 = (f32[8,1792]{1,0:T(8,128)S(1)}, f32[8,1792]{1,0:T(8,128)}, u32[]{:S(2)}) copy-start(f32[8,1792]{1,0:T(8,128)} %copy-done.9) | copy-start | bytes 172036
  150.1 14.4 %all-to-all-start.6 = ((bf16[4,128,512]{2,1,0:T(8,128)(2,1)}), bf16[4,128,512]{2,1,0:T(8,128)(2,1)}, u32[]{:S(2)}, u32[]{:S(2)}) async-start(bf16[4,128,512]{2,1,0:T(8,128)(2,1)} %add_convert_fusion.1), calls=%async_computation.6 | async-start | bytes 1048576 | tf_op jit(solution)/shard_map/all_to_all | solution.py:532
  155.8 1.2 copy-start.6
  162.0 4.0 %collective-permute-start.5 = (bf16[4,128,512]{2,1,0:T(8,128)(2,1)}, bf16[4,128,512]{2,1,0:T(8,128)(2,1)S(1)}, u32[]{:S(2)}, u32[]{:S(2)}) collective-permute-start(bf16[4,128,512]{2,1,0:T(8,128)(2,1)} %get-tuple-element.45), channel_id=1, source_target_pairs={{0,1},{1,0},{2,3},{3,2},{4,5},{5,4},{6,7},{7,6},{8,9},{9,8},{10,11... | collective-permute-start | bytes 1572872 | tf_op jit(solution)/shard_map/ppermute | solution.py:485
  166.9 23.4 %all-to-all-start.7 = ((bf16[4,128,512]{2,1,0:T(8,128)(2,1)}), bf16[4,128,512]{2,1,0:T(8,128)(2,1)S(1)}, u32[]{:S(2)}, u32[]{:S(2)}) async-start(bf16[4,128,512]{2,1,0:T(8,128)(2,1)} %add_convert_fusion), calls=%async_computation.7 | async-start | bytes 1048576 | tf_op jit(solution)/shard_map/all_to_all | solution.py:537
  174.7 15.6 %collective-permute-start.6 = (bf16[128,512]{1,0:T(8,128)(2,1)S(1)}, bf16[128,512]{1,0:T(8,128)(2,1)S(1)}, u32[]{:S(2)}, u32[]{:S(2)}) collective-permute-start(bf16[128,512]{1,0:T(8,128)(2,1)S(1)} %fusion.1), channel_id=1, source_target_pairs={{8,0},{9,1},{10,2},{11,3},{12,4},{13,5},{14,6},{15,7},{24,16},{25,... | collective-permute-start | bytes 393224 | tf_op jit(solution)/shard_map/ppermute | solution.py:536
Sparse Core Ops, SparseCore 0:
  47.2 76.0 all-gather.1

commit v6 on v4

--- a/solution.py
+++ b/solution.py
@@ -28,6 +28,7 @@
 FULL_ACCURACY = lax.Precision.HIGHEST
 MASKED = -1e30
 TINY = 1e-30
+FILLS_A_WAIT = 10**12
 NT = (((1,), (1,)), ((), ()))
 TN = (((0,), (0,)), ((), ()))
 NN = (((1,), (0,)), ((), ()))
@@ -199,7 +200,17 @@
             pieces[2 * d + c] = mean[d : d + 1, c * PIECE : (c + 1) * PIECE]
 
 
-def contrast_kernel(q, positive, docs_mine, docs_other, coefficient, terms, own_docs):
+def inverse_kernel(q, inverse):
+    values = q[...].astype(jnp.float32)
+    query_inv = lax.rsqrt(jnp.sum(values * values, axis=1, keepdims=True) + EPSILON)
+    inverse[...] = jnp.broadcast_to(query_inv, (128, 128))
+
+
+def unit_kernel(q, inverse, unit):
+    unit[...] = q[...].astype(jnp.float32) * inverse[:, :1]
+
+
+def contrast_kernel(unit, positive, docs_mine, docs_other, coefficient, terms, own_docs):
     z_lo, y, _, x, core = place()
     d_mine, d_other = docs_mine[...], docs_other[...]
     doc_inv = lax.rsqrt(
@@ -207,11 +218,9 @@
         + jnp.sum(d_other * d_other, axis=1, keepdims=True)
         + EPSILON
     )
-    q_all = q[...].astype(jnp.float32)
-    query_inv = lax.rsqrt(jnp.sum(q_all * q_all, axis=1, keepdims=True) + EPSILON)
-    q_unit = q_all * query_inv
-    q_mine = jnp.where(core == 1, q_unit[:, PIECE:], q_unit[:, :PIECE])
-    q_other = jnp.where(core == 1, q_unit[:, :PIECE], q_unit[:, PIECE:])
+    q_left, q_right = unit[:, :PIECE], unit[:, PIECE:]
+    q_mine = jnp.where(core == 1, q_right, q_left)
+    q_other = jnp.where(core == 1, q_left, q_right)
     logits = mm(d_mine * doc_inv, q_mine, NT, FULL_ACCURACY)
     logits = (logits + mm(d_other * doc_inv, q_other, NT, FULL_ACCURACY)) / INVERSE_TEMPER
     exps = jnp.exp(logits)
@@ -233,7 +242,7 @@
         own_docs[d : d + 1, PIECE:] = jnp.where(core == 1, a, b)
 
 
-def query_kernel(q, docs_mine, docs_other, coefficient, query_grad):
+def query_kernel(unit, inverse, docs_mine, docs_other, coefficient, query_grad):
     _, _, _, _, core = place()
     d_mine, d_other = docs_mine[...], docs_other[...]
     doc_inv = lax.rsqrt(
@@ -246,10 +255,8 @@
     u_other = mm(scaled, d_other, TN, FULL_ACCURACY) / INVERSE_TEMPER
     u_left = jnp.where(core == 1, u_other, u_mine)
     u_right = jnp.where(core == 1, u_mine, u_other)
-    q_all = q[...].astype(jnp.float32)
-    query_inv = lax.rsqrt(jnp.sum(q_all * q_all, axis=1, keepdims=True) + EPSILON)
-    q_unit = q_all * query_inv
-    q_left, q_right = q_unit[:, :PIECE], q_unit[:, PIECE:]
+    query_inv = inverse[:, :1]
+    q_left, q_right = unit[:, :PIECE], unit[:, PIECE:]
     inner = jnp.sum(q_left * u_left, axis=1, keepdims=True) + jnp.sum(
         q_right * u_right, axis=1, keepdims=True
     )
@@ -392,7 +399,10 @@
 
 def attend_own(lengths, *arrays):
     outs = (shape((HEAD_DIM, EMB), F32), shape((8, EMB), F32))
-    return run(attend_own_kernel, "attend_own", outs, [BIAS, STATS, ROUNDED, WIDE], lengths, *arrays)
+    scratch = [BIAS, STATS, ROUNDED, WIDE]
+    return run(
+        attend_own_kernel, "attend_own", outs, scratch, lengths, *arrays, flops=FILLS_A_WAIT
+    )
 
 
 def attend_low(lengths, *arrays):
@@ -401,13 +411,24 @@
     return run(attend_low_kernel, "attend_low", outs, scratch, lengths, *arrays)
 
 
+def query_inverses(q):
+    outs = (shape((128, 128), F32),)
+    return run(inverse_kernel, "query_inverses", outs, [], None, q, flops=FILLS_A_WAIT)[0]
+
+
+def query_units(*arrays):
+    outs = (shape((128, EMB), F32),)
+    return run(unit_kernel, "query_units", outs, [], None, *arrays, flops=FILLS_A_WAIT)[0]
+
+
 def contrast(*arrays):
     outs = (shape((NDOC, 128), F32), shape((32, 1, PIECE), F32), shape((8, EMB), F32))
     return run(contrast_kernel, "contrast", outs, [], None, *arrays)
 
 
 def query_back(*arrays):
-    return run(query_kernel, "query_back", (shape((128, EMB), F32),), [], None, *arrays)[0]
+    outs = (shape((128, EMB), F32),)
+    return run(query_kernel, "query_back", outs, [], None, *arrays, flops=FILLS_A_WAIT)[0]
 
 
 def back_low(lengths, *arrays):
@@ -451,9 +472,12 @@
     kv = jnp.concatenate([keys[0], values[0]], axis=1)
     kv_low = lax.ppermute(kv, "zhi", [(0, 1)])
     own_mine = to_all(kv, "x", 4)
-    kv_low, own_mine = lax.optimization_barrier((kv_low, own_mine))
+    inverse = query_inverses(query_emb)
+    own_mine, inverse = lax.optimization_barrier((own_mine, inverse))
+    unit = query_units(query_emb, inverse)
     own_other = swap_cores(own_mine)
     own_att, own_lse = attend_own(lengths, q, own_mine, own_other)
+    kv_low, own_att, unit = lax.optimization_barrier((kv_low, own_att, unit))
     low_mine = to_all(kv_low, "x", 4)
     low_other = swap_cores(low_mine)
     att, lse, pieces = attend_low(lengths, q, low_mine, low_other, own_att, own_lse)
@@ -465,7 +489,7 @@
     docs_other = swap_cores(docs_mine)
 
     coefficient, terms, own_docs = contrast(
-        query_emb, positive.reshape(1, 128), docs_mine, docs_other
+        unit, positive.reshape(1, 128), docs_mine, docs_other
     )
     terms = added(lax.all_to_all(terms, ("y", "zlo"), 0, 0))
     upstream = to_all(terms, NEAR, 8)
@@ -481,12 +505,12 @@
     low_terms = lax.all_to_all(paired, "x", 0, 0)
     low_sum = added(low_terms).astype(BF16)
     own_paired = pair_terms(own_d_mine, own_d_other)
+    from_high = lax.ppermute(low_sum, "zhi", [(1, 0)])
     low_sum, own_paired = lax.optimization_barrier((low_sum, own_paired))
-    from_high = lax.ppermute(low_sum, "zhi", [(1, 0)])
     own_terms = lax.all_to_all(own_paired, "x", 0, 0)
     own_sum = added(own_terms)
     coefficient, low_sum = lax.optimization_barrier((coefficient, low_sum))
-    query_grad = query_back(query_emb, docs_mine, docs_other, coefficient)
+    query_grad = query_back(unit, inverse, docs_mine, docs_other, coefficient)
     query_grad, from_high = lax.optimization_barrier((query_grad, from_high))
     total = (own_sum + from_high.astype(F32)).astype(BF16)
     return (query_grad, grad_q[None], total[None, :, :KVW], total[None, :, KVW:])

time: 195 us -> 185 us (0.949)
  the two profiles are of different devices: /device:TPU:34 before, /device:TPU:37 now
where the time goes in v6:
time: 185 us; the launch traced here: 184 us
  blocking collectives  73.5 us (40%)
  starting transfers between devices  51.2 us (28%)
  waiting for transfers between devices  28.5 us (15%)
  Pallas kernels  18.7 us (10%)
  other arithmetic  6.6 us (4%)
  local copies, waits for them, and re-layouts  4.48 us (2%)
    all_to_all x4, blocking collectives, to_all(): lax.all_to_all(jnp.broadcast_to(block[None], (count,) + block.shape), axe...  51 us
    pallas_call x8, Pallas kernels, run(): pl.pallas_call(kernel, out_shape=outs, in_specs=[smem] * len(first) + [vm...  18.7 us
    ppermute x5, starting transfers between devices, swap_cores(): return lax.ppermute(block, 'core', [(0, 1), (1, 0)])  18.3 us
    ppermute x1, waiting for transfers between devices, per_device(): from_high = lax.ppermute(low_sum, 'zhi', [(1, 0)])  16.6 us
    ppermute x1, starting transfers between devices, per_device(): kv_low = lax.ppermute(kv, 'zhi', [(0, 1)])  15.2 us
    all_to_all x1, blocking collectives, per_device(): terms = added(lax.all_to_all(terms, ('y', 'zlo'), 0, 0))  14.8 us
    all_to_all x1, blocking collectives, per_device(): part = added(lax.all_to_all(pieces, NEAR, 0, 0))  7.71 us
    all_to_all x1, starting transfers between devices, per_device(): low_terms = lax.all_to_all(paired, 'x', 0, 0)  6.25 us
  transfers between devices with their start and end apart: 10, of which 6 were waited for; matrix products, arithmetic and copies ran while one was open for 2% of the time, Pallas kernels for 8%

profile of v6, /device:TPU:37, one launch (start us, length us, event | category | flops | bytes accessed | tf_op | source)
XLA Modules:
  0.0 183.8 jit_solution(18068366278315596007)
XLA Ops:
  0.6 1.5 pad_maximum_fusion
  2.2 15.2 %collective-permute-start = (bf16[128,512]{1,0:T(8,128)(2,1)}, bf16[128,512]{1,0:T(8,128)(2,1)}, u32[]{:S(2)}, u32[]{:S(2)}) collective-permute-start(bf16[128,512]{1,0:T(8,128)(2,1)} %pad_maximum_fusion), channel_id=1, source_target_pairs={{0,8},{1,9},{2,10},{3,11},{4,12},{5,13},{6,14},{7,15},{16,24},{17,... | collective-permute-start | bytes 393224 | tf_op jit(solution)/shard_map/ppermute | solution.py:473
  17.4 1.7 broadcast_in_dim.44
  19.1 4.5 %all-to-all-start = ((bf16[4,128,512]{2,1,0:T(8,128)(2,1)}), bf16[4,128,512]{2,1,0:T(8,128)(2,1)}, u32[]{:S(2)}, u32[]{:S(2)}) async-start(bf16[4,128,512]{2,1,0:T(8,128)(2,1)} %broadcast_in_dim.44), calls=%async_computation | async-start | bytes 1048576 | tf_op jit(solution)/shard_map/all_to_all | solution.py:451
  23.6 0.2 query_inverses.1.inverse
  23.7 5.7 %all-to-all-done.mine = bf16[4,128,512]{2,1,0:T(8,128)(2,1)} async-done(((bf16[4,128,512]{2,1,0:T(8,128)(2,1)}), bf16[4,128,512]{2,1,0:T(8,128)(2,1)}, u32[]{:S(2)}, u32[]{:S(2)}) %all-to-all-start) | async-done | bytes 524320 | tf_op jit(solution)/shard_map/all_to_all | solution.py:451
  29.4 3.9 %collective-permute-start.1 = (bf16[4,128,512]{2,1,0:T(8,128)(2,1)}, bf16[4,128,512]{2,1,0:T(8,128)(2,1)}, u32[]{:S(2)}, u32[]{:S(2)}) collective-permute-start(bf16[4,128,512]{2,1,0:T(8,128)(2,1)} %all-to-all-done.mine), channel_id=1, source_target_pairs={{0,1},{1,0},{2,3},{3,2},{4,5},{5,4},{6,7},{7,6},{8,9},{9,8},{10,11... | collective-permute-start | bytes 1572872 | tf_op jit(solution)/shard_map/ppermute | solution.py:455
  33.3 0.0 copy-start
  33.3 0.1 query_units.1.unit
  33.5 0.0 copy-start.5
  33.5 1.7 collective-permute-done.1.other
  35.2 0.0 copy-done
  35.2 5.0 %attend_own.1 = (f32[128,1792]{1,0:T(8,128)S(1)}, f32[8,1792]{1,0:T(8,128)S(1)}) custom-call(s32[1,4]{1,0:T(1,128)S(1)} %copy-done.5, bf16[128,1792]{1,0:T(8,128)(2,1)S(1)} %bitcast.19, bf16[4,128,512]{2,1,0:T(8,128)(2,1)} %all-to-all-done.mine, bf16[4,128,512]{2,1,0:T(8,128)(2,1)} %collective-permute-done.1.other), custom_call_target="tpu_custom_call" | custom-call | flops 999999995904 | tf_op jit(solution)/shard_map/attend_own/pallas_call | solution.py:381
  40.2 0.0 collective-permute-done
  40.2 0.9 broadcast_in_dim.45
  41.1 12.1 %all_to_all.45.mine = bf16[4,128,512]{2,1,0:T(8,128)(2,1)S(1)} all-to-all(bf16[4,128,512]{2,1,0:T(8,128)(2,1)S(1)} %broadcast_in_dim.45), channel_id=1, replica_groups=mesh['zlo'=8,'y'=4,'zhi'=2,'x'=4,'core'=2] {'x'}, dimensions={0} | all-to-all | bytes 1048576 | tf_op jit(solution)/shard_map/all_to_all | solution.py:451
  53.3 3.6 %collective-permute-start.2 = (bf16[4,128,512]{2,1,0:T(8,128)(2,1)S(1)}, bf16[4,128,512]{2,1,0:T(8,128)(2,1)S(1)}, u32[]{:S(2)}, u32[]{:S(2)}) collective-permute-start(bf16[4,128,512]{2,1,0:T(8,128)(2,1)S(1)} %all_to_all.45.mine), channel_id=1, source_target_pairs={{0,1},{1,0},{2,3},{3,2},{4,5},{5,4},{6,7},{7,6},{8,9},{9,8},{10,11... | collective-permute-start | bytes 1572872 | tf_op jit(solution)/shard_map/ppermute | solution.py:455
  56.9 1.5 collective-permute-done.2.other
  58.4 1.1 attend_low.1
  59.5 7.7 %all_to_all.46 = f32[8,1,896]{2,1,0:T(1,128)S(1)} all-to-all(f32[8,1,896]{2,1,0:T(1,128)S(1)} %get-tuple-element.37), channel_id=1, replica_groups=mesh['zlo'=8,'y'=4,'zhi'=2,'x'=4,'core'=2] {'x','core'}, dimensions={0} | all-to-all | bytes 57344 | tf_op jit(solution)/shard_map/all_to_all | solution.py:485
  67.3 16.6 %all_to_all.47 = f32[16,1,896]{2,1,0:T(1,128)S(1)} all-to-all(f32[16,1,896]{2,1,0:T(1,128)S(1)} %broadcast_in_dim.47), channel_id=1, replica_groups=mesh['zlo'=8,'y'=4,'zhi'=2,'x'=4,'core'=2] {'zlo','zhi'}, dimensions={0} | all-to-all | bytes 114688 | tf_op jit(solution)/shard_map/all_to_all | solution.py:451
  84.0 12.6 %all_to_all.48 = f32[16,8,896]{2,1,0:T(8,128)S(1)} all-to-all(f32[16,8,896]{2,1,0:T(8,128)S(1)} %broadcast_in_dim.49), channel_id=1, replica_groups=mesh['zlo'=8,'y'=4,'zhi'=2,'x'=4,'core'=2] {'y','x'}, dimensions={0} | all-to-all | bytes 917504 | tf_op jit(solution)/shard_map/all_to_all | solution.py:451
  96.6 5.6 %collective-permute-start.3 = (f32[128,896]{1,0:T(8,128)S(1)}, f32[128,896]{1,0:T(8,128)S(1)}, u32[]{:S(2)}, u32[]{:S(2)}) collective-permute-start(f32[128,896]{1,0:T(8,128)S(1)} %bitcast.23), channel_id=1, source_target_pairs={{0,1},{1,0},{2,3},{3,2},{4,5},{5,4},{6,7},{7,6},{8,9},{9,8},{10,11... | collective-permute-start | bytes 1376264 | tf_op jit(solution)/shard_map/ppermute | solution.py:455
  102.3 1.4 collective-permute-done.3.docs_other
  103.7 1.6 contrast.1
  105.3 14.8 %all_to_all.49 = f32[32,1,896]{2,1,0:T(1,128)S(1)} all-to-all(f32[32,1,896]{2,1,0:T(1,128)S(1)} %get-tuple-element.42), channel_id=1, replica_groups=mesh['zlo'=8,'y'=4,'zhi'=2,'x'=4,'core'=2] {'y','zlo'}, dimensions={0} | all-to-all | bytes 229376 | tf_op jit(solution)/shard_map/all_to_all | solution.py:494
  120.0 0.1 fusion.2
  120.1 9.6 %all_to_all.50.upstream = f32[8,1,896]{2,1,0:T(1,128)S(1)} all-to-all(f32[8,1,896]{2,1,0:T(1,128)S(1)} %broadcast_in_dim.51), channel_id=1, replica_groups=mesh['zlo'=8,'y'=4,'zhi'=2,'x'=4,'core'=2] {'x','core'}, dimensions={0} | all-to-all | bytes 57344 | tf_op jit(solution)/shard_map/all_to_all | solution.py:451
  129.7 1.2 back_low.1
  130.9 0.0 copy-start.1
  130.9 2.6 %collective-permute-start.4 = (bf16[4,128,512]{2,1,0:T(8,128)(2,1)S(1)}, bf16[4,128,512]{2,1,0:T(8,128)(2,1)S(1)}, u32[]{:S(2)}, u32[]{:S(2)}) collective-permute-start(bf16[4,128,512]{2,1,0:T(8,128)(2,1)S(1)} %get-tuple-element.44), channel_id=1, source_target_pairs={{0,1},{1,0},{2,3},{3,2},{4,5},{5,4},{6,7},{7,6},{8,9},{9,8},{10,11... | collective-permute-start | bytes 1572872 | tf_op jit(solution)/shard_map/ppermute | solution.py:455
  133.6 1.5 collective-permute-done.4
  135.1 0.9 add_convert_fusion.1
  136.0 6.3 %all-to-all-start.7 = ((bf16[4,128,512]{2,1,0:T(8,128)(2,1)}), bf16[4,128,512]{2,1,0:T(8,128)(2,1)}, u32[]{:S(2)}, u32[]{:S(2)}) async-start(bf16[4,128,512]{2,1,0:T(8,128)(2,1)} %add_convert_fusion.1), calls=%async_computation.7 | async-start | bytes 1048576 | tf_op jit(solution)/shard_map/all_to_all | solution.py:505
  142.3 1.0 copy-done.2
  143.3 7.4 %back_own.1 = (bf16[128,1792]{1,0:T(8,128)(2,1)}, bf16[4,128,512]{2,1,0:T(8,128)(2,1)S(1)}, bf16[4,128,512]{2,1,0:T(8,128)(2,1)}) custom-call(s32[1,4]{1,0:T(1,128)S(1)} %copy-done.5, bf16[128,1792]{1,0:T(8,128)(2,1)S(1)} %bitcast.22, bf16[4,128,512]{2,1,0:T(8,128)(2,1)} %all-to-all-done.mine, bf16[4,128,512]{2,1,0:T(8,128)(2,1)} %collective-permute-done.1.other, ...), custom_call_target="tpu_custom_call" | custom-call | tf_op jit(solution)/shard_map/back_own/pallas_call | solution.py:381
  150.7 2.6 %collective-permute-start.6 = (bf16[4,128,512]{2,1,0:T(8,128)(2,1)}, bf16[4,128,512]{2,1,0:T(8,128)(2,1)S(1)}, u32[]{:S(2)}, u32[]{:S(2)}) collective-permute-start(bf16[4,128,512]{2,1,0:T(8,128)(2,1)} %get-tuple-element.53), channel_id=1, source_target_pairs={{0,1},{1,0},{2,3},{3,2},{4,5},{5,4},{6,7},{7,6},{8,9},{9,8},{10,11... | collective-permute-start | bytes 1572872 | tf_op jit(solution)/shard_map/ppermute | solution.py:455
  153.2 0.0 all-to-all-done.7
  153.2 1.8 fusion.1
  155.1 1.3 collective-permute-start.5
  156.3 0.0 collective-permute-done.6
  156.4 0.9 add_convert_fusion
  157.3 5.7 %all-to-all-start.8 = ((bf16[4,128,512]{2,1,0:T(8,128)(2,1)}), bf16[4,128,512]{2,1,0:T(8,128)(2,1)}, u32[]{:S(2)}, u32[]{:S(2)}) async-start(bf16[4,128,512]{2,1,0:T(8,128)(2,1)} %add_convert_fusion), calls=%async_computation.8 | async-start | bytes 1048576 | tf_op jit(solution)/shard_map/all_to_all | solution.py:510
  163.0 2.2 %query_back.1 = f32[128,1792]{1,0:T(8,128)} custom-call(f32[128,1792]{1,0:T(8,128)S(1)} %query_units.1.unit, f32[128,128]{1,0:T(8,128)S(1)} %copy-done.9, f32[128,896]{1,0:T(8,128)S(1)} %bitcast.25, f32[128,896]{1,0:T(8,128)S(1)} %copy-done.4, f32[128,128]{1,0:T(8,128)S(1)} %get-tuple-element.38.coefficient), custom_call_target="tpu_custom_call" | custom-call | flops 999999995904 | tf_op jit(solution)/shard_map/query_back/pallas_call | solution.py:381
  165.2 16.6 %collective-permute-done.5 = bf16[128,512]{1,0:T(8,128)(2,1)} collective-permute-done((bf16[128,512]{1,0:T(8,128)(2,1)}, bf16[128,512]{1,0:T(8,128)(2,1)}, u32[]{:S(2)}, u32[]{:S(2)}) %collective-permute-start.5) | collective-permute-done | bytes 131104 | tf_op jit(solution)/shard_map/ppermute | solution.py:508
  181.9 0.0 all-to-all-done.8
  181.9 1.2 fusion
  183.1 0.7 slice_bitcast_fusion
  (21 shorter events, 0.2 us)
Async XLA Ops:
  2.2 38.0 %collective-permute-start = (bf16[128,512]{1,0:T(8,128)(2,1)}, bf16[128,512]{1,0:T(8,128)(2,1)}, u32[]{:S(2)}, u32[]{:S(2)}) collective-permute-start(bf16[128,512]{1,0:T(8,128)(2,1)} %pad_maximum_fusion), channel_id=1, source_target_pairs={{0,8},{1,9},{2,10},{3,11},{4,12},{5,13},{6,14},{7,15},{16,24},{17,... | collective-permute-start | bytes 393224 | tf_op jit(solution)/shard_map/ppermute | solution.py:473
  19.1 4.5 %copy-start.7 = (bf16[128,1792]{1,0:T(8,128)(2,1)S(1)}, bf16[128,1792]{1,0:T(8,128)(2,1)}, u32[]{:S(2)}) copy-start(bf16[128,1792]{1,0:T(8,128)(2,1)} %q.3) | copy-start | bytes 1376260
  19.1 10.3 %all-to-all-start = ((bf16[4,128,512]{2,1,0:T(8,128)(2,1)}), bf16[4,128,512]{2,1,0:T(8,128)(2,1)}, u32[]{:S(2)}, u32[]{:S(2)}) async-start(bf16[4,128,512]{2,1,0:T(8,128)(2,1)} %broadcast_in_dim.44), calls=%async_computation | async-start | bytes 1048576 | tf_op jit(solution)/shard_map/all_to_all | solution.py:451
  23.7 9.7 %copy-start.8 = (f32[128,128]{1,0:T(8,128)}, f32[128,128]{1,0:T(8,128)S(1)}, u32[]{:S(2)}) copy-start(f32[128,128]{1,0:T(8,128)S(1)} %query_inverses.1.inverse) | copy-start | bytes 196612
  29.4 5.8 %collective-permute-start.1 = (bf16[4,128,512]{2,1,0:T(8,128)(2,1)}, bf16[4,128,512]{2,1,0:T(8,128)(2,1)}, u32[]{:S(2)}, u32[]{:S(2)}) collective-permute-start(bf16[4,128,512]{2,1,0:T(8,128)(2,1)} %all-to-all-done.mine), channel_id=1, source_target_pairs={{0,1},{1,0},{2,3},{3,2},{4,5},{5,4},{6,7},{7,6},{8,9},{9,8},{10,11... | collective-permute-start | bytes 1572872 | tf_op jit(solution)/shard_map/ppermute | solution.py:455
  33.3 1.9 %copy-start = (bf16[1,128,1792]{2,1,0:T(8,128)(2,1)S(1)}, bf16[1,128,1792]{2,1,0:T(8,128)(2,1)}, u32[]{:S(2)}) copy-start(bf16[1,128,1792]{2,1,0:T(8,128)(2,1)} %param.6) | copy-start | bytes 1376260
  33.5 1.7 copy-start.5
  53.3 5.1 %collective-permute-start.2 = (bf16[4,128,512]{2,1,0:T(8,128)(2,1)S(1)}, bf16[4,128,512]{2,1,0:T(8,128)(2,1)S(1)}, u32[]{:S(2)}, u32[]{:S(2)}) collective-permute-start(bf16[4,128,512]{2,1,0:T(8,128)(2,1)S(1)} %all_to_all.45.mine), channel_id=1, source_target_pairs={{0,1},{1,0},{2,3},{3,2},{4,5},{5,4},{6,7},{7,6},{8,9},{9,8},{10,11... | collective-permute-start | bytes 1572872 | tf_op jit(solution)/shard_map/ppermute | solution.py:455
  96.6 7.1 %copy-start.6 = (s32[128]{0:T(128)S(1)}, s32[128]{0:T(128)}, u32[]{:S(2)}) copy-start(s32[128]{0:T(128)} %param.11) | copy-start | bytes 1540
  96.6 7.0 %collective-permute-start.3 = (f32[128,896]{1,0:T(8,128)S(1)}, f32[128,896]{1,0:T(8,128)S(1)}, u32[]{:S(2)}, u32[]{:S(2)}) collective-permute-start(f32[128,896]{1,0:T(8,128)S(1)} %bitcast.23), channel_id=1, source_target_pairs={{0,1},{1,0},{2,3},{3,2},{4,5},{5,4},{6,7},{7,6},{8,9},{9,8},{10,11... | collective-permute-start | bytes 1376264 | tf_op jit(solution)/shard_map/ppermute | solution.py:455
  103.7 1.6 copy-start.3
  130.9 5.1 %copy-start.1 = (bf16[128,1792]{1,0:T(8,128)(2,1)}, bf16[128,1792]{1,0:T(8,128)(2,1)S(1)}, u32[]{:S(2)}) copy-start(bf16[128,1792]{1,0:T(8,128)(2,1)S(1)} %get-tuple-element.48.out_low) | copy-start | bytes 1376260
  130.9 4.2 %collective-permute-start.4 = (bf16[4,128,512]{2,1,0:T(8,128)(2,1)S(1)}, bf16[4,128,512]{2,1,0:T(8,128)(2,1)S(1)}, u32[]{:S(2)}, u32[]{:S(2)}) collective-permute-start(bf16[4,128,512]{2,1,0:T(8,128)(2,1)S(1)} %get-tuple-element.44), channel_id=1, source_target_pairs={{0,1},{1,0},{2,3},{3,2},{4,5},{5,4},{6,7},{7,6},{8,9},{9,8},{10,11... | collective-permute-start | bytes 1572872 | tf_op jit(solution)/shard_map/ppermute | solution.py:455
  136.0 17.2 %all-to-all-start.7 = ((bf16[4,128,512]{2,1,0:T(8,128)(2,1)}), bf16[4,128,512]{2,1,0:T(8,128)(2,1)}, u32[]{:S(2)}, u32[]{:S(2)}) async-start(bf16[4,128,512]{2,1,0:T(8,128)(2,1)} %add_convert_fusion.1), calls=%async_computation.7 | async-start | bytes 1048576 | tf_op jit(solution)/shard_map/all_to_all | solution.py:505
  142.3 1.0 copy-start.2
  150.7 5.7 %collective-permute-start.6 = (bf16[4,128,512]{2,1,0:T(8,128)(2,1)}, bf16[4,128,512]{2,1,0:T(8,128)(2,1)S(1)}, u32[]{:S(2)}, u32[]{:S(2)}) collective-permute-start(bf16[4,128,512]{2,1,0:T(8,128)(2,1)} %get-tuple-element.53), channel_id=1, source_target_pairs={{0,1},{1,0},{2,3},{3,2},{4,5},{5,4},{6,7},{7,6},{8,9},{9,8},{10,11... | collective-permute-start | bytes 1572872 | tf_op jit(solution)/shard_map/ppermute | solution.py:455
  155.1 26.8 %collective-permute-start.5 = (bf16[128,512]{1,0:T(8,128)(2,1)}, bf16[128,512]{1,0:T(8,128)(2,1)}, u32[]{:S(2)}, u32[]{:S(2)}) collective-permute-start(bf16[128,512]{1,0:T(8,128)(2,1)} %fusion.1), channel_id=1, source_target_pairs={{8,0},{9,1},{10,2},{11,3},{12,4},{13,5},{14,6},{15,7},{24,16},{25,... | collective-permute-start | bytes 393224 | tf_op jit(solution)/shard_map/ppermute | solution.py:508
  157.3 5.7 %copy-start.4 = (f32[128,896]{1,0:T(8,128)S(1)}, f32[128,896]{1,0:T(8,128)}, u32[]{:S(2)}) copy-start(f32[128,896]{1,0:T(8,128)} %copy-done.3) | copy-start | bytes 1376260
  157.3 5.7 %copy-start.9 = (f32[128,128]{1,0:T(8,128)S(1)}, f32[128,128]{1,0:T(8,128)}, u32[]{:S(2)}) copy-start(f32[128,128]{1,0:T(8,128)} %copy-done.8) | copy-start | bytes 196612
  157.3 24.6 %all-to-all-start.8 = ((bf16[4,128,512]{2,1,0:T(8,128)(2,1)}), bf16[4,128,512]{2,1,0:T(8,128)(2,1)}, u32[]{:S(2)}, u32[]{:S(2)}) async-start(bf16[4,128,512]{2,1,0:T(8,128)(2,1)} %add_convert_fusion), calls=%async_computation.8 | async-start | bytes 1048576 | tf_op jit(solution)/shard_map/all_to_all | solution.py:510

commit v7 on v6

--- a/solution.py
+++ b/solution.py
@@ -125,6 +125,16 @@
     return slice(h * HEAD_DIM, (h + 1) * HEAD_DIM)
 
 
+def join_kernel(keys, values, kv):
+    kv[:, :KVW] = keys[...]
+    kv[:, KVW:] = values[...]
+
+
+def spread_kernel(kv, spread):
+    for i in range(4):
+        spread[i] = kv[...]
+
+
 def part_attention(part, q, kv, bias, stats, weights, out):
     _, low, high = part
     stats[0] = jnp.full((HEADS, TOK), MASKED, jnp.float32)
@@ -163,9 +173,13 @@
     return stats[0, h : h + 1] * FACTOR + jnp.log(total), 1.0 / total
 
 
-def attend_own_kernel(lengths, q, mine, other, att, lse, bias, stats, weights, out):
+def bias_kernel(lengths, bias):
     row = Row(lengths)
     fill_bias(row, row.own, bias)
+
+
+def attend_own_kernel(lengths, q, mine, other, bias, att, lse, stats, weights, out):
+    row = Row(lengths)
     part_attention(row.own, q, (mine, other), bias, stats, weights, out)
     for h in range(HEADS):
         log_total, inverse = part_result(h, stats)
@@ -397,9 +411,22 @@
 ROUNDED = pltpu.VMEM((CHUNK, EMB), BF16)
 
 
+def join(*arrays):
+    return run(join_kernel, "join", (shape((TOK, 2 * KVW), BF16),), [], None, *arrays)[0]
+
+
+def spread(kv):
+    return run(spread_kernel, "spread", (shape((4, TOK, 2 * KVW), BF16),), [], None, kv)[0]
+
+
+def near_bias(lengths):
+    outs = (shape((CHUNKS, CHUNK, TOK), F32),)
+    return run(bias_kernel, "near_bias", outs, [], lengths, flops=FILLS_A_WAIT)[0]
+
+
 def attend_own(lengths, *arrays):
     outs = (shape((HEAD_DIM, EMB), F32), shape((8, EMB), F32))
-    scratch = [BIAS, STATS, ROUNDED, WIDE]
+    scratch = [STATS, ROUNDED, WIDE]
     return run(
         attend_own_kernel, "attend_own", outs, scratch, lengths, *arrays, flops=FILLS_A_WAIT
     )
@@ -469,16 +496,19 @@
 
 def per_device(queries_q, keys, values, lengths, query_emb, positive):
     q = queries_q[0]
-    kv = jnp.concatenate([keys[0], values[0]], axis=1)
+    kv = join(keys[0], values[0])
     kv_low = lax.ppermute(kv, "zhi", [(0, 1)])
-    own_mine = to_all(kv, "x", 4)
+    own_mine = lax.all_to_all(spread(kv), "x", 0, 0)
     inverse = query_inverses(query_emb)
-    own_mine, inverse = lax.optimization_barrier((own_mine, inverse))
+    own_mine, inverse, after = lax.optimization_barrier((own_mine, inverse, lengths))
+    own_other = swap_cores(own_mine)
+    own_bias = near_bias(after)
+    own_other, inverse, own_bias = lax.optimization_barrier((own_other, inverse, own_bias))
     unit = query_units(query_emb, inverse)
-    own_other = swap_cores(own_mine)
-    own_att, own_lse = attend_own(lengths, q, own_mine, own_other)
-    kv_low, own_att, unit = lax.optimization_barrier((kv_low, own_att, unit))
-    low_mine = to_all(kv_low, "x", 4)
+    kv_low, own_other, unit = lax.optimization_barrier((kv_low, own_other, unit))
+    own_att, own_lse = attend_own(lengths, q, own_mine, own_other, own_bias)
+    low_mine = lax.all_to_all(spread(kv_low), "x", 0, 0)
+    low_mine, own_att = lax.optimization_barrier((low_mine, own_att))
     low_other = swap_cores(low_mine)
     att, lse, pieces = attend_low(lengths, q, low_mine, low_other, own_att, own_lse)
 
@@ -512,8 +542,9 @@
     coefficient, low_sum = lax.optimization_barrier((coefficient, low_sum))
     query_grad = query_back(unit, inverse, docs_mine, docs_other, coefficient)
     query_grad, from_high = lax.optimization_barrier((query_grad, from_high))
-    total = (own_sum + from_high.astype(F32)).astype(BF16)
-    return (query_grad, grad_q[None], total[None, :, :KVW], total[None, :, KVW:])
+    grad_k = (own_sum[:, :KVW] + from_high[:, :KVW].astype(F32)).astype(BF16)
+    grad_v = (own_sum[:, KVW:] + from_high[:, KVW:].astype(F32)).astype(BF16)
+    return (query_grad, grad_q[None], grad_k[None], grad_v[None])
 
 
 def solution(mesh):

time: 185 us -> 186 us (level)
  the two profiles are of different devices: /device:TPU:37 before, /device:TPU:39 now
where the time goes in v7:
time: 186 us; the launch traced here: 185 us
  blocking collectives  63.2 us (34%)
  starting transfers between devices  55.2 us (30%)
  waiting for transfers between devices  28.6 us (15%)
  Pallas kernels  27.2 us (15%)
  other arithmetic  6.55 us (4%)
  local copies, waits for them, and re-layouts  3.46 us (2%)
    all_to_all x3, blocking collectives, to_all(): lax.all_to_all(jnp.broadcast_to(block[None], (count,) + block.shape), axe...  40.8 us
    pallas_call x12, Pallas kernels, run(): pl.pallas_call(kernel, out_shape=outs, in_specs=[smem] * len(first) + [vm...  27.2 us
    ppermute x5, starting transfers between devices, swap_cores(): return lax.ppermute(block, 'core', [(0, 1), (1, 0)])  18.2 us
    ppermute x1, waiting for transfers between devices, per_device(): from_high = lax.ppermute(low_sum, 'zhi', [(1, 0)])  15.7 us
    ppermute x1, starting transfers between devices, per_device(): kv_low = lax.ppermute(kv, 'zhi', [(0, 1)])  15.2 us
    all_to_all x1, blocking collectives, per_device(): terms = added(lax.all_to_all(terms, ('y', 'zlo'), 0, 0))  15.1 us
    all_to_all x1, blocking collectives, per_device(): part = added(lax.all_to_all(pieces, NEAR, 0, 0))  7.42 us
    all_to_all x1, waiting for transfers between devices, per_device(): own_mine = lax.all_to_all(spread(kv), 'x', 0, 0)  6.21 us
  transfers between devices with their start and end apart: 11, of which 7 were waited for; matrix products, arithmetic and copies ran while one was open for 2% of the time, Pallas kernels for 11%

profile of v7, /device:TPU:39, one launch (start us, length us, event | category | flops | bytes accessed | tf_op | source)
XLA Modules:
  0.0 185.2 jit_solution(17224324078109707409)
XLA Ops:
  0.6 0.8 copy-done.5
  1.5 0.8 copy-done.6
  2.3 0.7 join.1.kv
  3.0 15.2 %collective-permute-start = (bf16[128,512]{1,0:T(8,128)(2,1)}, bf16[128,512]{1,0:T(8,128)(2,1)}, u32[]{:S(2)}, u32[]{:S(2)}) collective-permute-start(bf16[128,512]{1,0:T(8,128)(2,1)} %join.1.kv), channel_id=1, source_target_pairs={{0,8},{1,9},{2,10},{3,11},{4,12},{5,13},{6,14},{7,15},{16,24},{17,... | collective-permute-start | bytes 393224 | tf_op jit(solution)/shard_map/ppermute | solution.py:500
  18.2 1.7 spread.2
  19.9 4.4 %all-to-all-start = ((bf16[4,128,512]{2,1,0:T(8,128)(2,1)}), bf16[4,128,512]{2,1,0:T(8,128)(2,1)}, u32[]{:S(2)}, u32[]{:S(2)}) async-start(bf16[4,128,512]{2,1,0:T(8,128)(2,1)} %spread.2), calls=%async_computation | async-start | bytes 1048576 | tf_op jit(solution)/shard_map/all_to_all | solution.py:501
  24.3 0.2 query_inverses.1.inverse
  24.5 6.2 %all-to-all-done.mine = bf16[4,128,512]{2,1,0:T(8,128)(2,1)} async-done(((bf16[4,128,512]{2,1,0:T(8,128)(2,1)}), bf16[4,128,512]{2,1,0:T(8,128)(2,1)}, u32[]{:S(2)}, u32[]{:S(2)}) %all-to-all-start) | async-done | bytes 524320 | tf_op jit(solution)/shard_map/all_to_all | solution.py:501
  30.7 4.2 %collective-permute-start.1 = (bf16[4,128,512]{2,1,0:T(8,128)(2,1)}, bf16[4,128,512]{2,1,0:T(8,128)(2,1)}, u32[]{:S(2)}, u32[]{:S(2)}) collective-permute-start(bf16[4,128,512]{2,1,0:T(8,128)(2,1)} %all-to-all-done.mine), channel_id=1, source_target_pairs={{0,1},{1,0},{2,3},{3,2},{4,5},{5,4},{6,7},{7,6},{8,9},{9,8},{10,11... | collective-permute-start | bytes 1572872 | tf_op jit(solution)/shard_map/ppermute | solution.py:482
  35.0 0.8 near_bias.1.bias
  35.8 1.0 collective-permute-done.1.other
  36.8 0.1 query_units.1.unit
  37.0 0.0 collective-permute-done.kv
  37.0 1.7 spread.3
  38.7 6.0 %all-to-all-start.1 = ((bf16[4,128,512]{2,1,0:T(8,128)(2,1)}), bf16[4,128,512]{2,1,0:T(8,128)(2,1)}, u32[]{:S(2)}, u32[]{:S(2)}) async-start(bf16[4,128,512]{2,1,0:T(8,128)(2,1)} %spread.3), calls=%async_computation.1 | async-start | bytes 1048576 | tf_op jit(solution)/shard_map/all_to_all | solution.py:510
  44.8 0.7 copy-done.8
  45.4 5.9 %attend_own.1 = (f32[128,1792]{1,0:T(8,128)S(1)}, f32[8,1792]{1,0:T(8,128)S(1)}) custom-call(s32[1,4]{1,0:T(1,128)S(1)} %copy-done.8, bf16[128,1792]{1,0:T(8,128)(2,1)S(1)} %bitcast.17, bf16[4,128,512]{2,1,0:T(8,128)(2,1)} %all-to-all-done.mine, bf16[4,128,512]{2,1,0:T(8,128)(2,1)} %collective-permute-done.1.other, f32[4,256,128]{2,1,0:T(8,128)S(1)} %near_bias.1.bias), custom_call_target="tpu_custom_call" | custom-call | flops 999999995904 | tf_op jit(solution)/shard_map/attend_own/pallas_call | solution.py:395
  51.3 1.0 all-to-all-done.1.mine
  52.3 3.1 %collective-permute-start.2 = (bf16[4,128,512]{2,1,0:T(8,128)(2,1)}, bf16[4,128,512]{2,1,0:T(8,128)(2,1)S(1)}, u32[]{:S(2)}, u32[]{:S(2)}) collective-permute-start(bf16[4,128,512]{2,1,0:T(8,128)(2,1)} %all-to-all-done.1.mine), channel_id=1, source_target_pairs={{0,1},{1,0},{2,3},{3,2},{4,5},{5,4},{6,7},{7,6},{8,9},{9,8},{10,11... | collective-permute-start | bytes 1572872 | tf_op jit(solution)/shard_map/ppermute | solution.py:482
  55.4 1.7 collective-permute-done.2.other
  57.1 1.6 attend_low.1
  58.8 7.4 %all_to_all.45 = f32[8,1,896]{2,1,0:T(1,128)S(1)} all-to-all(f32[8,1,896]{2,1,0:T(1,128)S(1)} %get-tuple-element.49), channel_id=1, replica_groups=mesh['zlo'=8,'y'=4,'zhi'=2,'x'=4,'core'=2] {'x','core'}, dimensions={0} | all-to-all | bytes 57344 | tf_op jit(solution)/shard_map/all_to_all | solution.py:515
  66.2 18.4 %all_to_all.46 = f32[16,1,896]{2,1,0:T(1,128)S(1)} all-to-all(f32[16,1,896]{2,1,0:T(1,128)S(1)} %broadcast_in_dim.33), channel_id=1, replica_groups=mesh['zlo'=8,'y'=4,'zhi'=2,'x'=4,'core'=2] {'zlo','zhi'}, dimensions={0} | all-to-all | bytes 114688 | tf_op jit(solution)/shard_map/all_to_all | solution.py:478
  84.8 12.7 %all_to_all.47 = f32[16,8,896]{2,1,0:T(8,128)S(1)} all-to-all(f32[16,8,896]{2,1,0:T(8,128)S(1)} %broadcast_in_dim.35), channel_id=1, replica_groups=mesh['zlo'=8,'y'=4,'zhi'=2,'x'=4,'core'=2] {'y','x'}, dimensions={0} | all-to-all | bytes 917504 | tf_op jit(solution)/shard_map/all_to_all | solution.py:478
  97.4 5.6 %collective-permute-start.3 = (f32[128,896]{1,0:T(8,128)S(1)}, f32[128,896]{1,0:T(8,128)S(1)}, u32[]{:S(2)}, u32[]{:S(2)}) collective-permute-start(f32[128,896]{1,0:T(8,128)S(1)} %bitcast.21), channel_id=1, source_target_pairs={{0,1},{1,0},{2,3},{3,2},{4,5},{5,4},{6,7},{7,6},{8,9},{9,8},{10,11... | collective-permute-start | bytes 1376264 | tf_op jit(solution)/shard_map/ppermute | solution.py:482
  103.1 1.4 collective-permute-done.3.docs_other
  104.5 1.6 contrast.1
  106.1 15.1 %all_to_all.48 = f32[32,1,896]{2,1,0:T(1,128)S(1)} all-to-all(f32[32,1,896]{2,1,0:T(1,128)S(1)} %get-tuple-element.54), channel_id=1, replica_groups=mesh['zlo'=8,'y'=4,'zhi'=2,'x'=4,'core'=2] {'y','zlo'}, dimensions={0} | all-to-all | bytes 229376 | tf_op jit(solution)/shard_map/all_to_all | solution.py:524
  121.1 0.1 fusion.5
  121.2 9.6 %all_to_all.49.upstream = f32[8,1,896]{2,1,0:T(1,128)S(1)} all-to-all(f32[8,1,896]{2,1,0:T(1,128)S(1)} %broadcast_in_dim.37), channel_id=1, replica_groups=mesh['zlo'=8,'y'=4,'zhi'=2,'x'=4,'core'=2] {'x','core'}, dimensions={0} | all-to-all | bytes 57344 | tf_op jit(solution)/shard_map/all_to_all | solution.py:478
  130.9 1.7 back_low.1
  132.6 0.0 copy-start.1
  132.6 2.6 %collective-permute-start.4 = (bf16[4,128,512]{2,1,0:T(8,128)(2,1)S(1)}, bf16[4,128,512]{2,1,0:T(8,128)(2,1)S(1)}, u32[]{:S(2)}, u32[]{:S(2)}) collective-permute-start(bf16[4,128,512]{2,1,0:T(8,128)(2,1)S(1)} %get-tuple-element.56), channel_id=1, source_target_pairs={{0,1},{1,0},{2,3},{3,2},{4,5},{5,4},{6,7},{7,6},{8,9},{9,8},{10,11... | collective-permute-start | bytes 1572872 | tf_op jit(solution)/shard_map/ppermute | solution.py:482
  135.2 1.5 collective-permute-done.4
  136.7 0.9 add_convert_fusion.1
  137.7 5.9 %all-to-all-start.7 = ((bf16[4,128,512]{2,1,0:T(8,128)(2,1)}), bf16[4,128,512]{2,1,0:T(8,128)(2,1)}, u32[]{:S(2)}, u32[]{:S(2)}) async-start(bf16[4,128,512]{2,1,0:T(8,128)(2,1)} %add_convert_fusion.1), calls=%async_computation.7 | async-start | bytes 1048576 | tf_op jit(solution)/shard_map/all_to_all | solution.py:535
  143.6 1.0 copy-done.2
  144.6 9.0 %back_own.1 = (bf16[128,1792]{1,0:T(8,128)(2,1)}, bf16[4,128,512]{2,1,0:T(8,128)(2,1)S(1)}, bf16[4,128,512]{2,1,0:T(8,128)(2,1)}) custom-call(s32[1,4]{1,0:T(1,128)S(1)} %copy-done.8, bf16[128,1792]{1,0:T(8,128)(2,1)S(1)} %bitcast.20, bf16[4,128,512]{2,1,0:T(8,128)(2,1)} %all-to-all-done.mine, bf16[4,128,512]{2,1,0:T(8,128)(2,1)} %collective-permute-done.1.other, ...), custom_call_target="tpu_custom_call" | custom-call | tf_op jit(solution)/shard_map/back_own/pallas_call | solution.py:395
  153.6 2.5 %collective-permute-start.6 = (bf16[4,128,512]{2,1,0:T(8,128)(2,1)}, bf16[4,128,512]{2,1,0:T(8,128)(2,1)S(1)}, u32[]{:S(2)}, u32[]{:S(2)}) collective-permute-start(bf16[4,128,512]{2,1,0:T(8,128)(2,1)} %get-tuple-element.65), channel_id=1, source_target_pairs={{0,1},{1,0},{2,3},{3,2},{4,5},{5,4},{6,7},{7,6},{8,9},{9,8},{10,11... | collective-permute-start | bytes 1572872 | tf_op jit(solution)/shard_map/ppermute | solution.py:482
  156.2 1.8 fusion
  158.0 1.3 collective-permute-start.5
  159.3 0.0 collective-permute-done.6
  159.3 1.0 add_convert_fusion
  160.2 4.3 %all-to-all-start.8 = ((bf16[4,128,512]{2,1,0:T(8,128)(2,1)}), bf16[4,128,512]{2,1,0:T(8,128)(2,1)}, u32[]{:S(2)}, u32[]{:S(2)}) async-start(bf16[4,128,512]{2,1,0:T(8,128)(2,1)} %add_convert_fusion), calls=%async_computation.8 | async-start | bytes 1048576 | tf_op jit(solution)/shard_map/all_to_all | solution.py:540
  164.5 2.2 %query_back.1 = f32[128,1792]{1,0:T(8,128)} custom-call(f32[128,1792]{1,0:T(8,128)S(1)} %query_units.1.unit, f32[128,128]{1,0:T(8,128)S(1)} %copy-done.12, f32[128,896]{1,0:T(8,128)S(1)} %bitcast.23, f32[128,896]{1,0:T(8,128)S(1)} %copy-done.4, f32[128,128]{1,0:T(8,128)S(1)} %get-tuple-element.50.coefficient), custom_call_target="tpu_custom_call" | custom-call | flops 999999995904 | tf_op jit(solution)/shard_map/query_back/pallas_call | solution.py:395
  166.7 15.7 %collective-permute-done.5 = bf16[128,512]{1,0:T(8,128)(2,1)} collective-permute-done((bf16[128,512]{1,0:T(8,128)(2,1)}, bf16[128,512]{1,0:T(8,128)(2,1)}, u32[]{:S(2)}, u32[]{:S(2)}) %collective-permute-start.5) | collective-permute-done | bytes 131104 | tf_op jit(solution)/shard_map/ppermute | solution.py:538
  182.4 1.2 add_bitcast_fusion
  183.6 1.6 fusion.4
  (29 shorter events, 0.2 us)
Async XLA Ops:
  0.6 0.8 copy-start.5
  1.5 0.8 copy-start.6
  3.0 34.0 %collective-permute-start = (bf16[128,512]{1,0:T(8,128)(2,1)}, bf16[128,512]{1,0:T(8,128)(2,1)}, u32[]{:S(2)}, u32[]{:S(2)}) collective-permute-start(bf16[128,512]{1,0:T(8,128)(2,1)} %join.1.kv), channel_id=1, source_target_pairs={{0,8},{1,9},{2,10},{3,11},{4,12},{5,13},{6,14},{7,15},{16,24},{17,... | collective-permute-start | bytes 393224 | tf_op jit(solution)/shard_map/ppermute | solution.py:500
  19.9 4.5 %copy-start.10 = (bf16[128,1792]{1,0:T(8,128)(2,1)S(1)}, bf16[128,1792]{1,0:T(8,128)(2,1)}, u32[]{:S(2)}) copy-start(bf16[128,1792]{1,0:T(8,128)(2,1)} %q.3) | copy-start | bytes 1376260
  19.9 10.8 %all-to-all-start = ((bf16[4,128,512]{2,1,0:T(8,128)(2,1)}), bf16[4,128,512]{2,1,0:T(8,128)(2,1)}, u32[]{:S(2)}, u32[]{:S(2)}) async-start(bf16[4,128,512]{2,1,0:T(8,128)(2,1)} %spread.2), calls=%async_computation | async-start | bytes 1048576 | tf_op jit(solution)/shard_map/all_to_all | solution.py:501
  24.3 10.7 %copy-start.7 = (s32[1,4]{1,0:T(1,128)S(1)}, s32[1,4]{1,0:T(1,128)}, u32[]{:S(2)}) copy-start(s32[1,4]{1,0:T(1,128)} %lengths.8) | copy-start | bytes 52
  24.5 12.3 %copy-start.11 = (f32[128,128]{1,0:T(8,128)}, f32[128,128]{1,0:T(8,128)S(1)}, u32[]{:S(2)}) copy-start(f32[128,128]{1,0:T(8,128)S(1)} %query_inverses.1.inverse) | copy-start | bytes 196612
  30.7 6.1 %collective-permute-start.1 = (bf16[4,128,512]{2,1,0:T(8,128)(2,1)}, bf16[4,128,512]{2,1,0:T(8,128)(2,1)}, u32[]{:S(2)}, u32[]{:S(2)}) collective-permute-start(bf16[4,128,512]{2,1,0:T(8,128)(2,1)} %all-to-all-done.mine), channel_id=1, source_target_pairs={{0,1},{1,0},{2,3},{3,2},{4,5},{5,4},{6,7},{7,6},{8,9},{9,8},{10,11... | collective-permute-start | bytes 1572872 | tf_op jit(solution)/shard_map/ppermute | solution.py:482
  38.7 6.0 %copy-start = (bf16[1,128,1792]{2,1,0:T(8,128)(2,1)S(1)}, bf16[1,128,1792]{2,1,0:T(8,128)(2,1)}, u32[]{:S(2)}) copy-start(bf16[1,128,1792]{2,1,0:T(8,128)(2,1)} %param.6) | copy-start | bytes 1376260
  38.7 13.6 %all-to-all-start.1 = ((bf16[4,128,512]{2,1,0:T(8,128)(2,1)}), bf16[4,128,512]{2,1,0:T(8,128)(2,1)}, u32[]{:S(2)}, u32[]{:S(2)}) async-start(bf16[4,128,512]{2,1,0:T(8,128)(2,1)} %spread.3), calls=%async_computation.1 | async-start | bytes 1048576 | tf_op jit(solution)/shard_map/all_to_all | solution.py:510
  44.7 0.7 copy-start.8
  52.3 4.8 %collective-permute-start.2 = (bf16[4,128,512]{2,1,0:T(8,128)(2,1)}, bf16[4,128,512]{2,1,0:T(8,128)(2,1)S(1)}, u32[]{:S(2)}, u32[]{:S(2)}) collective-permute-start(bf16[4,128,512]{2,1,0:T(8,128)(2,1)} %all-to-all-done.1.mine), channel_id=1, source_target_pairs={{0,1},{1,0},{2,3},{3,2},{4,5},{5,4},{6,7},{7,6},{8,9},{9,8},{10,11... | collective-permute-start | bytes 1572872 | tf_op jit(solution)/shard_map/ppermute | solution.py:482
  97.4 7.1 %copy-start.9 = (s32[128]{0:T(128)S(1)}, s32[128]{0:T(128)}, u32[]{:S(2)}) copy-start(s32[128]{0:T(128)} %param.11) | copy-start | bytes 1540
  97.4 7.1 %collective-permute-start.3 = (f32[128,896]{1,0:T(8,128)S(1)}, f32[128,896]{1,0:T(8,128)S(1)}, u32[]{:S(2)}, u32[]{:S(2)}) collective-permute-start(f32[128,896]{1,0:T(8,128)S(1)} %bitcast.21), channel_id=1, source_target_pairs={{0,1},{1,0},{2,3},{3,2},{4,5},{5,4},{6,7},{7,6},{8,9},{9,8},{10,11... | collective-permute-start | bytes 1376264 | tf_op jit(solution)/shard_map/ppermute | solution.py:482
  104.5 1.6 copy-start.3
  132.6 5.1 %copy-start.1 = (bf16[128,1792]{1,0:T(8,128)(2,1)}, bf16[128,1792]{1,0:T(8,128)(2,1)S(1)}, u32[]{:S(2)}) copy-start(bf16[128,1792]{1,0:T(8,128)(2,1)S(1)} %get-tuple-element.60.out_low) | copy-start | bytes 1376260
  132.6 4.2 %collective-permute-start.4 = (bf16[4,128,512]{2,1,0:T(8,128)(2,1)S(1)}, bf16[4,128,512]{2,1,0:T(8,128)(2,1)S(1)}, u32[]{:S(2)}, u32[]{:S(2)}) collective-permute-start(bf16[4,128,512]{2,1,0:T(8,128)(2,1)S(1)} %get-tuple-element.56), channel_id=1, source_target_pairs={{0,1},{1,0},{2,3},{3,2},{4,5},{5,4},{6,7},{7,6},{8,9},{9,8},{10,11... | collective-permute-start | bytes 1572872 | tf_op jit(solution)/shard_map/ppermute | solution.py:482
  137.7 18.5 %all-to-all-start.7 = ((bf16[4,128,512]{2,1,0:T(8,128)(2,1)}), bf16[4,128,512]{2,1,0:T(8,128)(2,1)}, u32[]{:S(2)}, u32[]{:S(2)}) async-start(bf16[4,128,512]{2,1,0:T(8,128)(2,1)} %add_convert_fusion.1), calls=%async_computation.7 | async-start | bytes 1048576 | tf_op jit(solution)/shard_map/all_to_all | solution.py:535
  143.6 1.0 copy-start.2
  153.6 5.7 %collective-permute-start.6 = (bf16[4,128,512]{2,1,0:T(8,128)(2,1)}, bf16[4,128,512]{2,1,0:T(8,128)(2,1)S(1)}, u32[]{:S(2)}, u32[]{:S(2)}) collective-permute-start(bf16[4,128,512]{2,1,0:T(8,128)(2,1)} %get-tuple-element.65), channel_id=1, source_target_pairs={{0,1},{1,0},{2,3},{3,2},{4,5},{5,4},{6,7},{7,6},{8,9},{9,8},{10,11... | collective-permute-start | bytes 1572872 | tf_op jit(solution)/shard_map/ppermute | solution.py:482
  158.0 24.5 %collective-permute-start.5 = (bf16[128,512]{1,0:T(8,128)(2,1)}, bf16[128,512]{1,0:T(8,128)(2,1)}, u32[]{:S(2)}, u32[]{:S(2)}) collective-permute-start(bf16[128,512]{1,0:T(8,128)(2,1)} %fusion), channel_id=1, source_target_pairs={{8,0},{9,1},{10,2},{11,3},{12,4},{13,5},{14,6},{15,7},{24,16},{25,... | collective-permute-start | bytes 393224 | tf_op jit(solution)/shard_map/ppermute | solution.py:538
  160.2 4.3 %copy-start.4 = (f32[128,896]{1,0:T(8,128)S(1)}, f32[128,896]{1,0:T(8,128)}, u32[]{:S(2)}) copy-start(f32[128,896]{1,0:T(8,128)} %copy-done.3) | copy-start | bytes 1376260
  160.2 4.3 %copy-start.12 = (f32[128,128]{1,0:T(8,128)S(1)}, f32[128,128]{1,0:T(8,128)}, u32[]{:S(2)}) copy-start(f32[128,128]{1,0:T(8,128)} %copy-done.11) | copy-start | bytes 196612
  160.2 22.2 %all-to-all-start.8 = ((bf16[4,128,512]{2,1,0:T(8,128)(2,1)}), bf16[4,128,512]{2,1,0:T(8,128)(2,1)}, u32[]{:S(2)}, u32[]{:S(2)}) async-start(bf16[4,128,512]{2,1,0:T(8,128)(2,1)} %add_convert_fusion), calls=%async_computation.8 | async-start | bytes 1048576 | tf_op jit(solution)/shard_map/all_to_all | solution.py:540

commit v8 on v7

--- a/solution.py
+++ b/solution.py
@@ -123,16 +123,6 @@
 
 def head(h):
     return slice(h * HEAD_DIM, (h + 1) * HEAD_DIM)
-
-
-def join_kernel(keys, values, kv):
-    kv[:, :KVW] = keys[...]
-    kv[:, KVW:] = values[...]
-
-
-def spread_kernel(kv, spread):
-    for i in range(4):
-        spread[i] = kv[...]
 
 
 def part_attention(part, q, kv, bias, stats, weights, out):
@@ -381,6 +371,16 @@
         grad_q[:, head(h)] = (dq[:, head(h)].T * FACTOR).astype(jnp.bfloat16)
 
 
+def total_kernel(terms, total):
+    total[...] = added(terms)
+
+
+def finish_kernel(near, far, grad_k, grad_v):
+    total = (near[...] + far[...].astype(jnp.float32)).astype(jnp.bfloat16)
+    grad_k[...] = total[:, :KVW]
+    grad_v[...] = total[:, KVW:]
+
+
 F32, BF16 = jnp.float32, jnp.bfloat16
 
 
@@ -411,14 +411,6 @@
 ROUNDED = pltpu.VMEM((CHUNK, EMB), BF16)
 
 
-def join(*arrays):
-    return run(join_kernel, "join", (shape((TOK, 2 * KVW), BF16),), [], None, *arrays)[0]
-
-
-def spread(kv):
-    return run(spread_kernel, "spread", (shape((4, TOK, 2 * KVW), BF16),), [], None, kv)[0]
-
-
 def near_bias(lengths):
     outs = (shape((CHUNKS, CHUNK, TOK), F32),)
     return run(bias_kernel, "near_bias", outs, [], lengths, flops=FILLS_A_WAIT)[0]
@@ -456,6 +448,16 @@
 def query_back(*arrays):
     outs = (shape((128, EMB), F32),)
     return run(query_kernel, "query_back", outs, [], None, *arrays, flops=FILLS_A_WAIT)[0]
+
+
+def total_of(terms):
+    outs = (shape((TOK, 2 * KVW), F32),)
+    return run(total_kernel, "total_of", outs, [], None, terms)[0]
+
+
+def finish(*arrays):
+    outs = (shape((TOK, KVW), BF16), shape((TOK, KVW), BF16))
+    return run(finish_kernel, "finish", outs, [], None, *arrays)
 
 
 def back_low(lengths, *arrays):
@@ -496,9 +498,9 @@
 
 def per_device(queries_q, keys, values, lengths, query_emb, positive):
     q = queries_q[0]
-    kv = join(keys[0], values[0])
+    kv = jnp.concatenate([keys[0], values[0]], axis=1)
     kv_low = lax.ppermute(kv, "zhi", [(0, 1)])
-    own_mine = lax.all_to_all(spread(kv), "x", 0, 0)
+    own_mine = to_all(kv, "x", 4)
     inverse = query_inverses(query_emb)
     own_mine, inverse, after = lax.optimization_barrier((own_mine, inverse, lengths))
     own_other = swap_cores(own_mine)
@@ -507,7 +509,7 @@
     unit = query_units(query_emb, inverse)
     kv_low, own_other, unit = lax.optimization_barrier((kv_low, own_other, unit))
     own_att, own_lse = attend_own(lengths, q, own_mine, own_other, own_bias)
-    low_mine = lax.all_to_all(spread(kv_low), "x", 0, 0)
+    low_mine = to_all(kv_low, "x", 4)
     low_mine, own_att = lax.optimization_barrier((low_mine, own_att))
     low_other = swap_cores(low_mine)
     att, lse, pieces = attend_low(lengths, q, low_mine, low_other, own_att, own_lse)
@@ -538,12 +540,10 @@
     from_high = lax.ppermute(low_sum, "zhi", [(1, 0)])
     low_sum, own_paired = lax.optimization_barrier((low_sum, own_paired))
     own_terms = lax.all_to_all(own_paired, "x", 0, 0)
-    own_sum = added(own_terms)
     coefficient, low_sum = lax.optimization_barrier((coefficient, low_sum))
     query_grad = query_back(unit, inverse, docs_mine, docs_other, coefficient)
-    query_grad, from_high = lax.optimization_barrier((query_grad, from_high))
-    grad_k = (own_sum[:, :KVW] + from_high[:, :KVW].astype(F32)).astype(BF16)
-    grad_v = (own_sum[:, KVW:] + from_high[:, KVW:].astype(F32)).astype(BF16)
+    query_grad, own_terms = lax.optimization_barrier((query_grad, own_terms))
+    grad_k, grad_v = finish(total_of(own_terms), from_high)
     return (query_grad, grad_q[None], grad_k[None], grad_v[None])
 
 

time: 186 us -> 183 us (0.984)
  Pallas kernels: 27.2 us -> 20.1 us
  waiting for transfers between devices: 28.6 us -> 32.8 us
    pallas_call x12 -> x11, Pallas kernels: 27.2 us -> 20.1 us  [run(): pl.pallas_call(kernel, out_shape=outs, in_specs=[smem] * len(first) + [vm...]
    all_to_all x1, waiting for transfers between devices: 0.01 us -> 4.13 us  [per_device(): own_terms = lax.all_to_all(own_paired, 'x', 0, 0)]
    broadcast_in_dim x3 -> x5, local copies, waits for them, and re-layouts: 0.08 us -> 3.55 us  [to_all(): jnp.broadcast_to(block[None], (count,) + block.shape)]
    ppermute x1, waiting for transfers between devices: 15.7 us -> 13.4 us  [per_device(): from_high = lax.ppermute(low_sum, 'zhi', [(1, 0)])]
    all_to_all x2, waiting for transfers between devices: 7.18 us -> 9.44 us  [to_all(): lax.all_to_all(jnp.broadcast_to(block[None], (count,) + block.shape), axe...]
  transfers between devices with their start and end apart: 11 -> 11, of which waited for: 7 -> 8; matrix products, arithmetic and copies ran while one was open for 2% -> 2% of each run, Pallas kernels for 11% -> 8%
where the time goes in v8:
time: 183 us; the launch traced here: 182 us
  blocking collectives  62 us (34%)
  starting transfers between devices  55.2 us (30%)
  waiting for transfers between devices  32.8 us (18%)
  Pallas kernels  20.1 us (11%)
  other arithmetic  5.35 us (3%)
  local copies, waits for them, and re-layouts  5.26 us (3%)
    all_to_all x3, blocking collectives, to_all(): lax.all_to_all(jnp.broadcast_to(block[None], (count,) + block.shape), axe...  39.6 us
    pallas_call x11, Pallas kernels, run(): pl.pallas_call(kernel, out_shape=outs, in_specs=[smem] * len(first) + [vm...  20.1 us
    ppermute x5, starting transfers between devices, swap_cores(): return lax.ppermute(block, 'core', [(0, 1), (1, 0)])  18.2 us
    ppermute x1, starting transfers between devices, per_device(): kv_low = lax.ppermute(kv, 'zhi', [(0, 1)])  15.2 us
    all_to_all x1, blocking collectives, per_device(): terms = added(lax.all_to_all(terms, ('y', 'zlo'), 0, 0))  15.1 us
    ppermute x1, waiting for transfers between devices, per_device(): from_high = lax.ppermute(low_sum, 'zhi', [(1, 0)])  13.4 us
    all_to_all x2, starting transfers between devices, to_all(): lax.all_to_all(jnp.broadcast_to(block[None], (count,) + block.shape), axe...  10.4 us
    all_to_all x2, waiting for transfers between devices, to_all(): lax.all_to_all(jnp.broadcast_to(block[None], (count,) + block.shape), axe...  9.44 us
  transfers between devices with their start and end apart: 11, of which 8 were waited for; matrix products, arithmetic and copies ran while one was open for 2% of the time, Pallas kernels for 8%

profile of v8, /device:TPU:39, one launch (start us, length us, event | category | flops | bytes accessed | tf_op | source)
XLA Modules:
  0.0 181.6 jit_solution(7358373240428732929)
XLA Ops:
  0.6 1.5 pad_maximum_fusion
  2.2 15.2 %collective-permute-start = (bf16[128,512]{1,0:T(8,128)(2,1)}, bf16[128,512]{1,0:T(8,128)(2,1)}, u32[]{:S(2)}, u32[]{:S(2)}) collective-permute-start(bf16[128,512]{1,0:T(8,128)(2,1)} %pad_maximum_fusion), channel_id=1, source_target_pairs={{0,8},{1,9},{2,10},{3,11},{4,12},{5,13},{6,14},{7,15},{16,24},{17,... | collective-permute-start | bytes 393224 | tf_op jit(solution)/shard_map/ppermute | solution.py:502
  17.3 1.7 broadcast_in_dim.44
  19.1 4.4 %all-to-all-start = ((bf16[4,128,512]{2,1,0:T(8,128)(2,1)}), bf16[4,128,512]{2,1,0:T(8,128)(2,1)}, u32[]{:S(2)}, u32[]{:S(2)}) async-start(bf16[4,128,512]{2,1,0:T(8,128)(2,1)} %broadcast_in_dim.44), calls=%async_computation | async-start | bytes 1048576 | tf_op jit(solution)/shard_map/all_to_all | solution.py:480
  23.5 0.2 query_inverses.1.inverse
  23.7 6.2 %all-to-all-done.mine = bf16[4,128,512]{2,1,0:T(8,128)(2,1)} async-done(((bf16[4,128,512]{2,1,0:T(8,128)(2,1)}), bf16[4,128,512]{2,1,0:T(8,128)(2,1)}, u32[]{:S(2)}, u32[]{:S(2)}) %all-to-all-start) | async-done | bytes 524320 | tf_op jit(solution)/shard_map/all_to_all | solution.py:480
  29.9 4.3 %collective-permute-start.1 = (bf16[4,128,512]{2,1,0:T(8,128)(2,1)}, bf16[4,128,512]{2,1,0:T(8,128)(2,1)}, u32[]{:S(2)}, u32[]{:S(2)}) collective-permute-start(bf16[4,128,512]{2,1,0:T(8,128)(2,1)} %all-to-all-done.mine), channel_id=1, source_target_pairs={{0,1},{1,0},{2,3},{3,2},{4,5},{5,4},{6,7},{7,6},{8,9},{9,8},{10,11... | collective-permute-start | bytes 1572872 | tf_op jit(solution)/shard_map/ppermute | solution.py:484
  34.2 0.7 near_bias.1.bias
  34.9 1.2 collective-permute-done.1.other
  36.0 0.1 query_units.1.unit
  36.2 0.0 collective-permute-done
  36.2 1.7 broadcast_in_dim.45
  37.9 6.0 %all-to-all-start.1 = ((bf16[4,128,512]{2,1,0:T(8,128)(2,1)}), bf16[4,128,512]{2,1,0:T(8,128)(2,1)}, u32[]{:S(2)}, u32[]{:S(2)}) async-start(bf16[4,128,512]{2,1,0:T(8,128)(2,1)} %broadcast_in_dim.45), calls=%async_computation.1 | async-start | bytes 1048576 | tf_op jit(solution)/shard_map/all_to_all | solution.py:480
  43.9 0.7 copy-done.6
  44.6 3.6 %attend_own.1 = (f32[128,1792]{1,0:T(8,128)S(1)}, f32[8,1792]{1,0:T(8,128)S(1)}) custom-call(s32[1,4]{1,0:T(1,128)S(1)} %copy-done.6, bf16[128,1792]{1,0:T(8,128)(2,1)S(1)} %bitcast.13, bf16[4,128,512]{2,1,0:T(8,128)(2,1)} %all-to-all-done.mine, bf16[4,128,512]{2,1,0:T(8,128)(2,1)} %collective-permute-done.1.other, f32[4,256,128]{2,1,0:T(8,128)S(1)} %near_bias.1.bias), custom_call_target="tpu_custom_call" | custom-call | flops 999999995904 | tf_op jit(solution)/shard_map/attend_own/pallas_call | solution.py:395
  48.2 3.2 %all-to-all-done.1.mine = bf16[4,128,512]{2,1,0:T(8,128)(2,1)} async-done(((bf16[4,128,512]{2,1,0:T(8,128)(2,1)}), bf16[4,128,512]{2,1,0:T(8,128)(2,1)}, u32[]{:S(2)}, u32[]{:S(2)}) %all-to-all-start.1) | async-done | bytes 524320 | tf_op jit(solution)/shard_map/all_to_all | solution.py:480
  51.5 3.1 %collective-permute-start.2 = (bf16[4,128,512]{2,1,0:T(8,128)(2,1)}, bf16[4,128,512]{2,1,0:T(8,128)(2,1)S(1)}, u32[]{:S(2)}, u32[]{:S(2)}) collective-permute-start(bf16[4,128,512]{2,1,0:T(8,128)(2,1)} %all-to-all-done.1.mine), channel_id=1, source_target_pairs={{0,1},{1,0},{2,3},{3,2},{4,5},{5,4},{6,7},{7,6},{8,9},{9,8},{10,11... | collective-permute-start | bytes 1572872 | tf_op jit(solution)/shard_map/ppermute | solution.py:484
  54.6 1.7 collective-permute-done.2.other
  56.3 1.6 attend_low.1
  57.9 7.4 %all_to_all.45 = f32[8,1,896]{2,1,0:T(1,128)S(1)} all-to-all(f32[8,1,896]{2,1,0:T(1,128)S(1)} %get-tuple-element.51), channel_id=1, replica_groups=mesh['zlo'=8,'y'=4,'zhi'=2,'x'=4,'core'=2] {'x','core'}, dimensions={0} | all-to-all | bytes 57344 | tf_op jit(solution)/shard_map/all_to_all | solution.py:517
  65.4 16.7 %all_to_all.46 = f32[16,1,896]{2,1,0:T(1,128)S(1)} all-to-all(f32[16,1,896]{2,1,0:T(1,128)S(1)} %broadcast_in_dim.47), channel_id=1, replica_groups=mesh['zlo'=8,'y'=4,'zhi'=2,'x'=4,'core'=2] {'zlo','zhi'}, dimensions={0} | all-to-all | bytes 114688 | tf_op jit(solution)/shard_map/all_to_all | solution.py:480
  82.2 13.3 %all_to_all.47 = f32[16,8,896]{2,1,0:T(8,128)S(1)} all-to-all(f32[16,8,896]{2,1,0:T(8,128)S(1)} %broadcast_in_dim.49), channel_id=1, replica_groups=mesh['zlo'=8,'y'=4,'zhi'=2,'x'=4,'core'=2] {'y','x'}, dimensions={0} | all-to-all | bytes 917504 | tf_op jit(solution)/shard_map/all_to_all | solution.py:480
  95.4 5.6 %collective-permute-start.3 = (f32[128,896]{1,0:T(8,128)S(1)}, f32[128,896]{1,0:T(8,128)S(1)}, u32[]{:S(2)}, u32[]{:S(2)}) collective-permute-start(f32[128,896]{1,0:T(8,128)S(1)} %bitcast.17), channel_id=1, source_target_pairs={{0,1},{1,0},{2,3},{3,2},{4,5},{5,4},{6,7},{7,6},{8,9},{9,8},{10,11... | collective-permute-start | bytes 1376264 | tf_op jit(solution)/shard_map/ppermute | solution.py:484
  101.1 1.4 collective-permute-done.3.docs_other
  102.5 1.6 contrast.1
  104.1 15.1 %all_to_all.48 = f32[32,1,896]{2,1,0:T(1,128)S(1)} all-to-all(f32[32,1,896]{2,1,0:T(1,128)S(1)} %get-tuple-element.56), channel_id=1, replica_groups=mesh['zlo'=8,'y'=4,'zhi'=2,'x'=4,'core'=2] {'y','zlo'}, dimensions={0} | all-to-all | bytes 229376 | tf_op jit(solution)/shard_map/all_to_all | solution.py:526
  119.1 0.1 fusion.1
  119.2 9.6 %all_to_all.49.upstream = f32[8,1,896]{2,1,0:T(1,128)S(1)} all-to-all(f32[8,1,896]{2,1,0:T(1,128)S(1)} %broadcast_in_dim.51), channel_id=1, replica_groups=mesh['zlo'=8,'y'=4,'zhi'=2,'x'=4,'core'=2] {'x','core'}, dimensions={0} | all-to-all | bytes 57344 | tf_op jit(solution)/shard_map/all_to_all | solution.py:480
  128.9 1.7 back_low.1
  130.6 0.0 copy-start.1
  130.6 2.6 %collective-permute-start.4 = (bf16[4,128,512]{2,1,0:T(8,128)(2,1)S(1)}, bf16[4,128,512]{2,1,0:T(8,128)(2,1)S(1)}, u32[]{:S(2)}, u32[]{:S(2)}) collective-permute-start(bf16[4,128,512]{2,1,0:T(8,128)(2,1)S(1)} %get-tuple-element.58), channel_id=1, source_target_pairs={{0,1},{1,0},{2,3},{3,2},{4,5},{5,4},{6,7},{7,6},{8,9},{9,8},{10,11... | collective-permute-start | bytes 1572872 | tf_op jit(solution)/shard_map/ppermute | solution.py:484
  133.2 1.5 collective-permute-done.4
  134.7 0.9 add_convert_fusion.1
  135.7 5.9 %all-to-all-start.7 = ((bf16[4,128,512]{2,1,0:T(8,128)(2,1)}), bf16[4,128,512]{2,1,0:T(8,128)(2,1)}, u32[]{:S(2)}, u32[]{:S(2)}) async-start(bf16[4,128,512]{2,1,0:T(8,128)(2,1)} %add_convert_fusion.1), calls=%async_computation.7 | async-start | bytes 1048576 | tf_op jit(solution)/shard_map/all_to_all | solution.py:537
  141.6 1.0 copy-done.2
  142.6 5.7 %back_own.1 = (bf16[128,1792]{1,0:T(8,128)(2,1)}, bf16[4,128,512]{2,1,0:T(8,128)(2,1)S(1)}, bf16[4,128,512]{2,1,0:T(8,128)(2,1)}) custom-call(s32[1,4]{1,0:T(1,128)S(1)} %copy-done.6, bf16[128,1792]{1,0:T(8,128)(2,1)S(1)} %bitcast.16, bf16[4,128,512]{2,1,0:T(8,128)(2,1)} %all-to-all-done.mine, bf16[4,128,512]{2,1,0:T(8,128)(2,1)} %collective-permute-done.1.other, ...), custom_call_target="tpu_custom_call" | custom-call | tf_op jit(solution)/shard_map/back_own/pallas_call | solution.py:395
  148.3 2.5 %collective-permute-start.5 = (bf16[4,128,512]{2,1,0:T(8,128)(2,1)}, bf16[4,128,512]{2,1,0:T(8,128)(2,1)S(1)}, u32[]{:S(2)}, u32[]{:S(2)}) collective-permute-start(bf16[4,128,512]{2,1,0:T(8,128)(2,1)} %get-tuple-element.65), channel_id=1, source_target_pairs={{0,1},{1,0},{2,3},{3,2},{4,5},{5,4},{6,7},{7,6},{8,9},{9,8},{10,11... | collective-permute-start | bytes 1572872 | tf_op jit(solution)/shard_map/ppermute | solution.py:484
  150.8 0.0 all-to-all-done.7
  150.8 1.8 fusion
  152.7 1.3 collective-permute-start.6
  153.9 0.0 collective-permute-done.5
  154.0 0.9 add_convert_fusion
  154.9 4.3 %all-to-all-start.8 = ((bf16[4,128,512]{2,1,0:T(8,128)(2,1)}), bf16[4,128,512]{2,1,0:T(8,128)(2,1)}, u32[]{:S(2)}, u32[]{:S(2)}) async-start(bf16[4,128,512]{2,1,0:T(8,128)(2,1)} %add_convert_fusion), calls=%async_computation.8 | async-start | bytes 1048576 | tf_op jit(solution)/shard_map/all_to_all | solution.py:542
  159.2 2.2 %query_back.1 = f32[128,1792]{1,0:T(8,128)} custom-call(f32[128,1792]{1,0:T(8,128)S(1)} %query_units.1.unit, f32[128,128]{1,0:T(8,128)S(1)} %copy-done.10, f32[128,896]{1,0:T(8,128)S(1)} %bitcast.19, f32[128,896]{1,0:T(8,128)S(1)} %copy-done.4, f32[128,128]{1,0:T(8,128)S(1)} %get-tuple-element.52.coefficient), custom_call_target="tpu_custom_call" | custom-call | flops 999999995904 | tf_op jit(solution)/shard_map/query_back/pallas_call | solution.py:395
  161.4 4.1 %all-to-all-done.8.terms = bf16[4,128,512]{2,1,0:T(8,128)(2,1)} async-done(((bf16[4,128,512]{2,1,0:T(8,128)(2,1)}), bf16[4,128,512]{2,1,0:T(8,128)(2,1)}, u32[]{:S(2)}, u32[]{:S(2)}) %all-to-all-start.8) | async-done | bytes 524320 | tf_op jit(solution)/shard_map/all_to_all | solution.py:542
  165.5 1.1 total_of.1.near
  166.6 13.4 %collective-permute-done.6.far = bf16[128,512]{1,0:T(8,128)(2,1)} collective-permute-done((bf16[128,512]{1,0:T(8,128)(2,1)}, bf16[128,512]{1,0:T(8,128)(2,1)}, u32[]{:S(2)}, u32[]{:S(2)}) %collective-permute-start.6) | collective-permute-done | bytes 131104 | tf_op jit(solution)/shard_map/ppermute | solution.py:540
  180.0 1.6 finish.1
  (25 shorter events, 0.2 us)
Async XLA Ops:
  2.2 34.0 %collective-permute-start = (bf16[128,512]{1,0:T(8,128)(2,1)}, bf16[128,512]{1,0:T(8,128)(2,1)}, u32[]{:S(2)}, u32[]{:S(2)}) collective-permute-start(bf16[128,512]{1,0:T(8,128)(2,1)} %pad_maximum_fusion), channel_id=1, source_target_pairs={{0,8},{1,9},{2,10},{3,11},{4,12},{5,13},{6,14},{7,15},{16,24},{17,... | collective-permute-start | bytes 393224 | tf_op jit(solution)/shard_map/ppermute | solution.py:502
  19.1 4.4 %copy-start.8 = (bf16[128,1792]{1,0:T(8,128)(2,1)S(1)}, bf16[128,1792]{1,0:T(8,128)(2,1)}, u32[]{:S(2)}) copy-start(bf16[128,1792]{1,0:T(8,128)(2,1)} %q.3) | copy-start | bytes 1376260
  19.1 10.8 %all-to-all-start = ((bf16[4,128,512]{2,1,0:T(8,128)(2,1)}), bf16[4,128,512]{2,1,0:T(8,128)(2,1)}, u32[]{:S(2)}, u32[]{:S(2)}) async-start(bf16[4,128,512]{2,1,0:T(8,128)(2,1)} %broadcast_in_dim.44), calls=%async_computation | async-start | bytes 1048576 | tf_op jit(solution)/shard_map/all_to_all | solution.py:480
  23.5 10.7 %copy-start.5 = (s32[1,4]{1,0:T(1,128)S(1)}, s32[1,4]{1,0:T(1,128)}, u32[]{:S(2)}) copy-start(s32[1,4]{1,0:T(1,128)} %lengths.8) | copy-start | bytes 52
  23.7 12.3 %copy-start.9 = (f32[128,128]{1,0:T(8,128)}, f32[128,128]{1,0:T(8,128)S(1)}, u32[]{:S(2)}) copy-start(f32[128,128]{1,0:T(8,128)S(1)} %query_inverses.1.inverse) | copy-start | bytes 196612
  29.9 6.1 %collective-permute-start.1 = (bf16[4,128,512]{2,1,0:T(8,128)(2,1)}, bf16[4,128,512]{2,1,0:T(8,128)(2,1)}, u32[]{:S(2)}, u32[]{:S(2)}) collective-permute-start(bf16[4,128,512]{2,1,0:T(8,128)(2,1)} %all-to-all-done.mine), channel_id=1, source_target_pairs={{0,1},{1,0},{2,3},{3,2},{4,5},{5,4},{6,7},{7,6},{8,9},{9,8},{10,11... | collective-permute-start | bytes 1572872 | tf_op jit(solution)/shard_map/ppermute | solution.py:484
  37.9 6.0 %copy-start = (bf16[1,128,1792]{2,1,0:T(8,128)(2,1)S(1)}, bf16[1,128,1792]{2,1,0:T(8,128)(2,1)}, u32[]{:S(2)}) copy-start(bf16[1,128,1792]{2,1,0:T(8,128)(2,1)} %param.6) | copy-start | bytes 1376260
  37.9 13.6 %all-to-all-start.1 = ((bf16[4,128,512]{2,1,0:T(8,128)(2,1)}), bf16[4,128,512]{2,1,0:T(8,128)(2,1)}, u32[]{:S(2)}, u32[]{:S(2)}) async-start(bf16[4,128,512]{2,1,0:T(8,128)(2,1)} %broadcast_in_dim.45), calls=%async_computation.1 | async-start | bytes 1048576 | tf_op jit(solution)/shard_map/all_to_all | solution.py:480
  43.9 0.7 copy-start.6
  51.5 4.8 %collective-permute-start.2 = (bf16[4,128,512]{2,1,0:T(8,128)(2,1)}, bf16[4,128,512]{2,1,0:T(8,128)(2,1)S(1)}, u32[]{:S(2)}, u32[]{:S(2)}) collective-permute-start(bf16[4,128,512]{2,1,0:T(8,128)(2,1)} %all-to-all-done.1.mine), channel_id=1, source_target_pairs={{0,1},{1,0},{2,3},{3,2},{4,5},{5,4},{6,7},{7,6},{8,9},{9,8},{10,11... | collective-permute-start | bytes 1572872 | tf_op jit(solution)/shard_map/ppermute | solution.py:484
  95.4 7.1 %copy-start.7 = (s32[128]{0:T(128)S(1)}, s32[128]{0:T(128)}, u32[]{:S(2)}) copy-start(s32[128]{0:T(128)} %param.11) | copy-start | bytes 1540
  95.4 7.1 %collective-permute-start.3 = (f32[128,896]{1,0:T(8,128)S(1)}, f32[128,896]{1,0:T(8,128)S(1)}, u32[]{:S(2)}, u32[]{:S(2)}) collective-permute-start(f32[128,896]{1,0:T(8,128)S(1)} %bitcast.17), channel_id=1, source_target_pairs={{0,1},{1,0},{2,3},{3,2},{4,5},{5,4},{6,7},{7,6},{8,9},{9,8},{10,11... | collective-permute-start | bytes 1376264 | tf_op jit(solution)/shard_map/ppermute | solution.py:484
  102.5 1.6 copy-start.3
  130.6 5.1 %copy-start.1 = (bf16[128,1792]{1,0:T(8,128)(2,1)}, bf16[128,1792]{1,0:T(8,128)(2,1)S(1)}, u32[]{:S(2)}) copy-start(bf16[128,1792]{1,0:T(8,128)(2,1)S(1)} %get-tuple-element.61.out_low) | copy-start | bytes 1376260
  130.6 4.2 %collective-permute-start.4 = (bf16[4,128,512]{2,1,0:T(8,128)(2,1)S(1)}, bf16[4,128,512]{2,1,0:T(8,128)(2,1)S(1)}, u32[]{:S(2)}, u32[]{:S(2)}) collective-permute-start(bf16[4,128,512]{2,1,0:T(8,128)(2,1)S(1)} %get-tuple-element.58), channel_id=1, source_target_pairs={{0,1},{1,0},{2,3},{3,2},{4,5},{5,4},{6,7},{7,6},{8,9},{9,8},{10,11... | collective-permute-start | bytes 1572872 | tf_op jit(solution)/shard_map/ppermute | solution.py:484
  135.7 15.2 %all-to-all-start.7 = ((bf16[4,128,512]{2,1,0:T(8,128)(2,1)}), bf16[4,128,512]{2,1,0:T(8,128)(2,1)}, u32[]{:S(2)}, u32[]{:S(2)}) async-start(bf16[4,128,512]{2,1,0:T(8,128)(2,1)} %add_convert_fusion.1), calls=%async_computation.7 | async-start | bytes 1048576 | tf_op jit(solution)/shard_map/all_to_all | solution.py:537
  141.6 1.0 copy-start.2
  148.3 5.7 %collective-permute-start.5 = (bf16[4,128,512]{2,1,0:T(8,128)(2,1)}, bf16[4,128,512]{2,1,0:T(8,128)(2,1)S(1)}, u32[]{:S(2)}, u32[]{:S(2)}) collective-permute-start(bf16[4,128,512]{2,1,0:T(8,128)(2,1)} %get-tuple-element.65), channel_id=1, source_target_pairs={{0,1},{1,0},{2,3},{3,2},{4,5},{5,4},{6,7},{7,6},{8,9},{9,8},{10,11... | collective-permute-start | bytes 1572872 | tf_op jit(solution)/shard_map/ppermute | solution.py:484
  152.7 27.4 %collective-permute-start.6 = (bf16[128,512]{1,0:T(8,128)(2,1)}, bf16[128,512]{1,0:T(8,128)(2,1)}, u32[]{:S(2)}, u32[]{:S(2)}) collective-permute-start(bf16[128,512]{1,0:T(8,128)(2,1)} %fusion), channel_id=1, source_target_pairs={{8,0},{9,1},{10,2},{11,3},{12,4},{13,5},{14,6},{15,7},{24,16},{25,... | collective-permute-start | bytes 393224 | tf_op jit(solution)/shard_map/ppermute | solution.py:540
  154.9 4.3 %copy-start.4 = (f32[128,896]{1,0:T(8,128)S(1)}, f32[128,896]{1,0:T(8,128)}, u32[]{:S(2)}) copy-start(f32[128,896]{1,0:T(8,128)} %copy-done.3) | copy-start | bytes 1376260
  154.9 4.3 %copy-start.10 = (f32[128,128]{1,0:T(8,128)S(1)}, f32[128,128]{1,0:T(8,128)}, u32[]{:S(2)}) copy-start(f32[128,128]{1,0:T(8,128)} %copy-done.9) | copy-start | bytes 196612
  154.9 10.6 %all-to-all-start.8 = ((bf16[4,128,512]{2,1,0:T(8,128)(2,1)}), bf16[4,128,512]{2,1,0:T(8,128)(2,1)}, u32[]{:S(2)}, u32[]{:S(2)}) async-start(bf16[4,128,512]{2,1,0:T(8,128)(2,1)} %add_convert_fusion), calls=%async_computation.8 | async-start | bytes 1048576 | tf_op jit(solution)/shard_map/all_to_all | solution.py:542

commit v9 on v8

--- a/solution.py
+++ b/solution.py
@@ -25,6 +25,7 @@
 FACTOR = HEAD_DIM ** (-0.5)
 INVERSE_TEMPER = 0.05
 EPSILON = 1e-06
+LOG2_E = 1.4426950408889634
 FULL_ACCURACY = lax.Precision.HIGHEST
 MASKED = -1e30
 TINY = 1e-30
@@ -125,6 +126,14 @@
     return slice(h * HEAD_DIM, (h + 1) * HEAD_DIM)
 
 
+def spread_kernel(kv, out, done):
+    copies = [pltpu.make_async_copy(kv, out.at[i], done.at[i]) for i in range(4)]
+    for copy in copies:
+        copy.start()
+    for copy in copies:
+        copy.wait()
+
+
 def part_attention(part, q, kv, bias, stats, weights, out):
     _, low, high = part
     stats[0] = jnp.full((HEADS, TOK), MASKED, jnp.float32)
@@ -137,10 +146,15 @@
             k_rows = chunk_of(kv, chunk, group)
             scales = []
             for h in range(group * PER_GROUP, (group + 1) * PER_GROUP):
-                scores = mm(k_rows, q[:, head(h)], NT) + blocked
+                i = h - group * PER_GROUP
+                if i % 2 == 0:
+                    many = 2 if i + 1 < PER_GROUP else 1
+                    pair = jnp.concatenate([q[:, head(h + j)] for j in range(many)], axis=0)
+                    every = mm(k_rows, pair, NT)
+                scores = every[:, head(i % 2)] + blocked
                 old = stats[0, h : h + 1]
                 top = jnp.maximum(old, jnp.max(scores, axis=0, keepdims=True))
-                exps = jnp.exp((scores - top) * FACTOR)
+                exps = jnp.exp2((scores - top) * (FACTOR * LOG2_E))
                 weights[:, head(h)] = exps.astype(jnp.bfloat16)
                 scale = jnp.exp((old - top) * FACTOR)
                 stats[0, h : h + 1] = top
@@ -163,9 +177,10 @@
     return stats[0, h : h + 1] * FACTOR + jnp.log(total), 1.0 / total
 
 
-def bias_kernel(lengths, bias):
+def bias_kernel(lengths, own_bias, low_bias):
     row = Row(lengths)
-    fill_bias(row, row.own, bias)
+    fill_bias(row, row.own, own_bias)
+    fill_bias(row, row.low, low_bias)
 
 
 def attend_own_kernel(lengths, q, mine, other, bias, att, lse, stats, weights, out):
@@ -178,10 +193,9 @@
 
 
 def attend_low_kernel(
-    lengths, q, mine, other, own_att, own_lse, att, lse, pieces, bias, stats, weights, out, doc_sum
+    lengths, q, mine, other, own_att, own_lse, bias, att, lse, pieces, stats, weights, out, doc_sum
 ):
     row = Row(lengths)
-    fill_bias(row, row.low, bias)
     member = jnp.concatenate([row.member, jnp.zeros((TOK - 8, TOK), jnp.float32)], axis=0)
     member = member.astype(jnp.bfloat16)
     part_attention(row.low, q, (mine, other), bias, stats, weights, out)
@@ -278,9 +292,16 @@
             v_rows = chunk_of(kv, chunk, KV_HEADS + group)
             for h in range(group * PER_GROUP, (group + 1) * PER_GROUP):
                 at = head(h)
-                scores = mm(k_rows, q[:, at], NT) * FACTOR + blocked
-                probs = jnp.exp(scores - lse[0:1, at])
-                flow = mm(v_rows, out_low[:, at], NT)
+                i = h - group * PER_GROUP
+                if i % 2 == 0:
+                    many = 2 if i + 1 < PER_GROUP else 1
+                    pair = jnp.concatenate([q[:, head(h + j)] for j in range(many)], axis=0)
+                    every = mm(k_rows, pair, NT)
+                    pair = jnp.concatenate([out_low[:, head(h + j)] for j in range(many)], axis=0)
+                    flows = mm(v_rows, pair, NT)
+                scores = every[:, head(i % 2)] * (FACTOR * LOG2_E) + blocked
+                probs = jnp.exp2(scores - lse[0:1, at] * LOG2_E)
+                flow = flows[:, head(i % 2)]
                 grads[:, at] = (probs * (flow - delta[0:1, at])).astype(jnp.bfloat16)
                 weights[:, at] = probs.astype(jnp.bfloat16)
             columns = slice(group * GROUP_W, (group + 1) * GROUP_W)
@@ -304,19 +325,18 @@
     lse,
     own_docs,
     upstream,
+    bias,
     out_low,
     delta,
     dq_low,
     d_mine,
     d_other,
-    bias,
     grads,
     weights,
 ):
     row = Row(lengths)
     d_mine[...] = jnp.zeros(d_mine.shape, d_mine.dtype)
     d_other[...] = jnp.zeros(d_other.shape, d_other.dtype)
-    fill_bias(row, row.low, bias)
     w = jnp.concatenate(
         [
             jnp.concatenate([upstream[2 * d + c] for d in range(DOCS)] * 2, axis=0)
@@ -411,9 +431,23 @@
 ROUNDED = pltpu.VMEM((CHUNK, EMB), BF16)
 
 
-def near_bias(lengths):
-    outs = (shape((CHUNKS, CHUNK, TOK), F32),)
-    return run(bias_kernel, "near_bias", outs, [], lengths, flops=FILLS_A_WAIT)[0]
+def spread(kv):
+    anywhere = pl.BlockSpec(memory_space=pl.ANY)
+    return pl.pallas_call(
+        spread_kernel,
+        out_shape=shape((4, *kv.shape), kv.dtype),
+        in_specs=[anywhere],
+        out_specs=anywhere,
+        scratch_shapes=[pltpu.SemaphoreType.DMA((4,))],
+        compiler_params=pltpu.CompilerParams(vmem_limit_bytes=VMEM_BYTES),
+        cost_estimate=pl.CostEstimate(flops=0, bytes_accessed=0, transcendentals=0),
+        name="spread",
+    )(kv)
+
+
+def biases(lengths):
+    one = shape((CHUNKS, CHUNK, TOK), F32)
+    return run(bias_kernel, "biases", (one, one), [], lengths, flops=FILLS_A_WAIT)
 
 
 def attend_own(lengths, *arrays):
@@ -426,7 +460,7 @@
 
 def attend_low(lengths, *arrays):
     outs = (shape((HEAD_DIM, EMB), F32), shape((8, EMB), F32), shape((8, 1, PIECE), F32))
-    scratch = [BIAS, STATS, ROUNDED, WIDE, pltpu.VMEM((8, EMB), F32)]
+    scratch = [STATS, ROUNDED, WIDE, pltpu.VMEM((8, EMB), F32)]
     return run(attend_low_kernel, "attend_low", outs, scratch, lengths, *arrays)
 
 
@@ -468,7 +502,7 @@
         TERMS,
         TERMS,
     )
-    return run(back_low_kernel, "back_low", outs, [BIAS, ROUNDED, ROUNDED], lengths, *arrays)
+    return run(back_low_kernel, "back_low", outs, [ROUNDED, ROUNDED], lengths, *arrays)
 
 
 def back_own(lengths, *arrays):
@@ -500,19 +534,21 @@
     q = queries_q[0]
     kv = jnp.concatenate([keys[0], values[0]], axis=1)
     kv_low = lax.ppermute(kv, "zhi", [(0, 1)])
-    own_mine = to_all(kv, "x", 4)
+    own_mine = lax.all_to_all(spread(kv), "x", 0, 0)
     inverse = query_inverses(query_emb)
     own_mine, inverse, after = lax.optimization_barrier((own_mine, inverse, lengths))
     own_other = swap_cores(own_mine)
-    own_bias = near_bias(after)
+    own_bias, low_bias = biases(after)
     own_other, inverse, own_bias = lax.optimization_barrier((own_other, inverse, own_bias))
     unit = query_units(query_emb, inverse)
     kv_low, own_other, unit = lax.optimization_barrier((kv_low, own_other, unit))
     own_att, own_lse = attend_own(lengths, q, own_mine, own_other, own_bias)
-    low_mine = to_all(kv_low, "x", 4)
+    low_mine = lax.all_to_all(spread(kv_low), "x", 0, 0)
     low_mine, own_att = lax.optimization_barrier((low_mine, own_att))
     low_other = swap_cores(low_mine)
-    att, lse, pieces = attend_low(lengths, q, low_mine, low_other, own_att, own_lse)
+    att, lse, pieces = attend_low(
+        lengths, q, low_mine, low_other, own_att, own_lse, low_bias
+    )
 
     part = added(lax.all_to_all(pieces, NEAR, 0, 0))
     column = to_all(part, ("zlo", "zhi"), 16)
@@ -527,7 +563,7 @@
     upstream = to_all(terms, NEAR, 8)
 
     out_low, delta, dq_low, d_mine, d_other = back_low(
-        lengths, q, low_mine, low_other, att, lse, own_docs, upstream
+        lengths, q, low_mine, low_other, att, lse, own_docs, upstream, low_bias
     )
     paired = pair_terms(d_mine, d_other)
     paired, dq_low = lax.optimization_barrier((paired, dq_low))

time: 183 us -> 213 us (1.16)
  Pallas kernels: 20.1 us -> 53.9 us
    pallas_call x0 -> x2, Pallas kernels: none -> 34 us  [spread(): pl.pallas_call(spread_kernel, out_shape=shape((4, *kv.shape), kv.dtype),...]
    broadcast_in_dim x5 -> x3, local copies, waits for them, and re-layouts: 3.55 us -> 0.08 us  [to_all(): jnp.broadcast_to(block[None], (count,) + block.shape)]
  transfers between devices with their start and end apart: 11 -> 11, of which waited for: 8 -> 8; matrix products, arithmetic and copies ran while one was open for 2% -> 1% of each run, Pallas kernels for 8% -> 14%
where the time goes in v9:
time: 213 us; the launch traced here: 211 us
  blocking collectives  61.5 us (29%)
  starting transfers between devices  55.3 us (26%)
  Pallas kernels  53.9 us (25%)
  waiting for transfers between devices  30.9 us (15%)
  other arithmetic  5.37 us (3%)
  local copies, waits for them, and re-layouts  3.63 us (2%)
    all_to_all x3, blocking collectives, to_all(): lax.all_to_all(jnp.broadcast_to(block[None], (count,) + block.shape), axe...  39 us
    pallas_call x2, Pallas kernels, spread(): pl.pallas_call(spread_kernel, out_shape=shape((4, *kv.shape), kv.dtype),...  34 us
    pallas_call x11, Pallas kernels, run(): pl.pallas_call(kernel, out_shape=outs, in_specs=[smem] * len(first) + [vm...  19.9 us
    ppermute x5, starting transfers between devices, swap_cores(): return lax.ppermute(block, 'core', [(0, 1), (1, 0)])  18.2 us
    ppermute x1, starting transfers between devices, per_device(): kv_low = lax.ppermute(kv, 'zhi', [(0, 1)])  15.2 us
    all_to_all x1, blocking collectives, per_device(): terms = added(lax.all_to_all(terms, ('y', 'zlo'), 0, 0))  15.1 us
    ppermute x1, waiting for transfers between devices, per_device(): from_high = lax.ppermute(low_sum, 'zhi', [(1, 0)])  13.2 us
    all_to_all x1, blocking collectives, per_device(): part = added(lax.all_to_all(pieces, NEAR, 0, 0))  7.43 us
  transfers between devices with their start and end apart: 11, of which 8 were waited for; matrix products, arithmetic and copies ran while one was open for 1% of the time, Pallas kernels for 14%

profile of v9, /device:TPU:39, one launch (start us, length us, event | category | flops | bytes accessed | tf_op | source)
XLA Modules:
  0.0 211.5 jit_solution(4699252942123963151)
XLA Ops:
  0.6 1.5 pad_maximum_fusion.kv
  2.2 15.2 %collective-permute-start = (bf16[128,512]{1,0:T(8,128)(2,1)}, bf16[128,512]{1,0:T(8,128)(2,1)}, u32[]{:S(2)}, u32[]{:S(2)}) collective-permute-start(bf16[128,512]{1,0:T(8,128)(2,1)} %pad_maximum_fusion.kv), channel_id=1, source_target_pairs={{0,8},{1,9},{2,10},{3,11},{4,12},{5,13},{6,14},{7,15},{16,24},{17,... | collective-permute-start | bytes 393224 | tf_op jit(solution)/shard_map/ppermute | solution.py:536
  17.4 17.0 %spread.2 = bf16[4,128,512]{2,1,0:T(8,128)(2,1)} custom-call(bf16[128,512]{1,0:T(8,128)(2,1)} %pad_maximum_fusion.kv), custom_call_target="tpu_custom_call" | custom-call | tf_op jit(solution)/shard_map/spread/pallas_call | solution.py:436
  34.4 4.4 %all-to-all-start = ((bf16[4,128,512]{2,1,0:T(8,128)(2,1)}), bf16[4,128,512]{2,1,0:T(8,128)(2,1)}, u32[]{:S(2)}, u32[]{:S(2)}) async-start(bf16[4,128,512]{2,1,0:T(8,128)(2,1)} %spread.2), calls=%async_computation | async-start | bytes 1048576 | tf_op jit(solution)/shard_map/all_to_all | solution.py:537
  38.8 0.2 query_inverses.1.inverse
  39.0 6.2 %all-to-all-done.mine = bf16[4,128,512]{2,1,0:T(8,128)(2,1)} async-done(((bf16[4,128,512]{2,1,0:T(8,128)(2,1)}), bf16[4,128,512]{2,1,0:T(8,128)(2,1)}, u32[]{:S(2)}, u32[]{:S(2)}) %all-to-all-start) | async-done | bytes 524320 | tf_op jit(solution)/shard_map/all_to_all | solution.py:537
  45.2 4.3 %collective-permute-start.1 = (bf16[4,128,512]{2,1,0:T(8,128)(2,1)}, bf16[4,128,512]{2,1,0:T(8,128)(2,1)}, u32[]{:S(2)}, u32[]{:S(2)}) collective-permute-start(bf16[4,128,512]{2,1,0:T(8,128)(2,1)} %all-to-all-done.mine), channel_id=1, source_target_pairs={{0,1},{1,0},{2,3},{3,2},{4,5},{5,4},{6,7},{7,6},{8,9},{9,8},{10,11... | collective-permute-start | bytes 1572872 | tf_op jit(solution)/shard_map/ppermute | solution.py:518
  49.5 0.0 copy-start.9
  49.5 0.7 biases.1
  50.2 0.8 copy-done.10
  51.0 0.3 collective-permute-done.1.other
  51.4 0.1 query_units.1.unit
  51.5 17.0 %spread.3 = bf16[4,128,512]{2,1,0:T(8,128)(2,1)} custom-call(bf16[128,512]{1,0:T(8,128)(2,1)} %collective-permute-done.kv), custom_call_target="tpu_custom_call" | custom-call | tf_op jit(solution)/shard_map/spread/pallas_call | solution.py:436
  68.5 0.0 copy-start
  68.5 6.0 %all-to-all-start.1 = ((bf16[4,128,512]{2,1,0:T(8,128)(2,1)}), bf16[4,128,512]{2,1,0:T(8,128)(2,1)}, u32[]{:S(2)}, u32[]{:S(2)}) async-start(bf16[4,128,512]{2,1,0:T(8,128)(2,1)} %spread.3), calls=%async_computation.1 | async-start | bytes 1048576 | tf_op jit(solution)/shard_map/all_to_all | solution.py:546
  74.6 0.7 copy-done.6
  75.2 1.0 copy-done.11
  76.3 3.5 %attend_own.1 = (f32[128,1792]{1,0:T(8,128)S(1)}, f32[8,1792]{1,0:T(8,128)S(1)}) custom-call(s32[1,4]{1,0:T(1,128)S(1)} %copy-done.6, bf16[128,1792]{1,0:T(8,128)(2,1)S(1)} %bitcast.13, bf16[4,128,512]{2,1,0:T(8,128)(2,1)} %all-to-all-done.mine, bf16[4,128,512]{2,1,0:T(8,128)(2,1)} %collective-permute-done.1.other, f32[4,256,128]{2,1,0:T(8,128)S(1)} %copy-done.11), custom_call_target="tpu_custom_call" | custom-call | flops 999999995904 | tf_op jit(solution)/shard_map/attend_own/pallas_call | solution.py:415
  79.8 2.3 %all-to-all-done.1.mine = bf16[4,128,512]{2,1,0:T(8,128)(2,1)} async-done(((bf16[4,128,512]{2,1,0:T(8,128)(2,1)}), bf16[4,128,512]{2,1,0:T(8,128)(2,1)}, u32[]{:S(2)}, u32[]{:S(2)}) %all-to-all-start.1) | async-done | bytes 524320 | tf_op jit(solution)/shard_map/all_to_all | solution.py:546
  82.1 3.1 %collective-permute-start.2 = (bf16[4,128,512]{2,1,0:T(8,128)(2,1)}, bf16[4,128,512]{2,1,0:T(8,128)(2,1)S(1)}, u32[]{:S(2)}, u32[]{:S(2)}) collective-permute-start(bf16[4,128,512]{2,1,0:T(8,128)(2,1)} %all-to-all-done.1.mine), channel_id=1, source_target_pairs={{0,1},{1,0},{2,3},{3,2},{4,5},{5,4},{6,7},{7,6},{8,9},{9,8},{10,11... | collective-permute-start | bytes 1572872 | tf_op jit(solution)/shard_map/ppermute | solution.py:518
  85.2 1.7 collective-permute-done.2.other
  87.0 1.6 attend_low.1
  88.6 7.4 %all_to_all.45 = f32[8,1,896]{2,1,0:T(1,128)S(1)} all-to-all(f32[8,1,896]{2,1,0:T(1,128)S(1)} %get-tuple-element.55), channel_id=1, replica_groups=mesh['zlo'=8,'y'=4,'zhi'=2,'x'=4,'core'=2] {'x','core'}, dimensions={0} | all-to-all | bytes 57344 | tf_op jit(solution)/shard_map/all_to_all | solution.py:553
  96.0 16.7 %all_to_all.46 = f32[16,1,896]{2,1,0:T(1,128)S(1)} all-to-all(f32[16,1,896]{2,1,0:T(1,128)S(1)} %broadcast_in_dim.33), channel_id=1, replica_groups=mesh['zlo'=8,'y'=4,'zhi'=2,'x'=4,'core'=2] {'zlo','zhi'}, dimensions={0} | all-to-all | bytes 114688 | tf_op jit(solution)/shard_map/all_to_all | solution.py:514
  112.8 12.7 %all_to_all.47 = f32[16,8,896]{2,1,0:T(8,128)S(1)} all-to-all(f32[16,8,896]{2,1,0:T(8,128)S(1)} %broadcast_in_dim.35), channel_id=1, replica_groups=mesh['zlo'=8,'y'=4,'zhi'=2,'x'=4,'core'=2] {'y','x'}, dimensions={0} | all-to-all | bytes 917504 | tf_op jit(solution)/shard_map/all_to_all | solution.py:514
  125.5 5.6 %collective-permute-start.3 = (f32[128,896]{1,0:T(8,128)S(1)}, f32[128,896]{1,0:T(8,128)S(1)}, u32[]{:S(2)}, u32[]{:S(2)}) collective-permute-start(f32[128,896]{1,0:T(8,128)S(1)} %bitcast.17), channel_id=1, source_target_pairs={{0,1},{1,0},{2,3},{3,2},{4,5},{5,4},{6,7},{7,6},{8,9},{9,8},{10,11... | collective-permute-start | bytes 1376264 | tf_op jit(solution)/shard_map/ppermute | solution.py:518
  131.1 1.4 collective-permute-done.3.docs_other
  132.5 1.6 contrast.1
  134.1 15.1 %all_to_all.48 = f32[32,1,896]{2,1,0:T(1,128)S(1)} all-to-all(f32[32,1,896]{2,1,0:T(1,128)S(1)} %get-tuple-element.60), channel_id=1, replica_groups=mesh['zlo'=8,'y'=4,'zhi'=2,'x'=4,'core'=2] {'y','zlo'}, dimensions={0} | all-to-all | bytes 229376 | tf_op jit(solution)/shard_map/all_to_all | solution.py:562
  149.2 0.1 fusion.1
  149.3 9.6 %all_to_all.49.upstream = f32[8,1,896]{2,1,0:T(1,128)S(1)} all-to-all(f32[8,1,896]{2,1,0:T(1,128)S(1)} %broadcast_in_dim.37), channel_id=1, replica_groups=mesh['zlo'=8,'y'=4,'zhi'=2,'x'=4,'core'=2] {'x','core'}, dimensions={0} | all-to-all | bytes 57344 | tf_op jit(solution)/shard_map/all_to_all | solution.py:514
  158.9 1.7 back_low.1
  160.6 2.6 %collective-permute-start.4 = (bf16[4,128,512]{2,1,0:T(8,128)(2,1)S(1)}, bf16[4,128,512]{2,1,0:T(8,128)(2,1)S(1)}, u32[]{:S(2)}, u32[]{:S(2)}) collective-permute-start(bf16[4,128,512]{2,1,0:T(8,128)(2,1)S(1)} %get-tuple-element.62), channel_id=1, source_target_pairs={{0,1},{1,0},{2,3},{3,2},{4,5},{5,4},{6,7},{7,6},{8,9},{9,8},{10,11... | collective-permute-start | bytes 1572872 | tf_op jit(solution)/shard_map/ppermute | solution.py:518
  163.2 1.5 collective-permute-done.4
  164.8 0.9 add_convert_fusion.1
  165.7 5.9 %all-to-all-start.7 = ((bf16[4,128,512]{2,1,0:T(8,128)(2,1)}), bf16[4,128,512]{2,1,0:T(8,128)(2,1)}, u32[]{:S(2)}, u32[]{:S(2)}) async-start(bf16[4,128,512]{2,1,0:T(8,128)(2,1)} %add_convert_fusion.1), calls=%async_computation.7 | async-start | bytes 1048576 | tf_op jit(solution)/shard_map/all_to_all | solution.py:573
  171.6 1.0 copy-done.2
  172.6 5.7 %back_own.1 = (bf16[128,1792]{1,0:T(8,128)(2,1)}, bf16[4,128,512]{2,1,0:T(8,128)(2,1)S(1)}, bf16[4,128,512]{2,1,0:T(8,128)(2,1)}) custom-call(s32[1,4]{1,0:T(1,128)S(1)} %copy-done.6, bf16[128,1792]{1,0:T(8,128)(2,1)S(1)} %bitcast.16, bf16[4,128,512]{2,1,0:T(8,128)(2,1)} %all-to-all-done.mine, bf16[4,128,512]{2,1,0:T(8,128)(2,1)} %collective-permute-done.1.other, ...), custom_call_target="tpu_custom_call" | custom-call | tf_op jit(solution)/shard_map/back_own/pallas_call | solution.py:415
  178.3 2.5 %collective-permute-start.5 = (bf16[4,128,512]{2,1,0:T(8,128)(2,1)}, bf16[4,128,512]{2,1,0:T(8,128)(2,1)S(1)}, u32[]{:S(2)}, u32[]{:S(2)}) collective-permute-start(bf16[4,128,512]{2,1,0:T(8,128)(2,1)} %get-tuple-element.69), channel_id=1, source_target_pairs={{0,1},{1,0},{2,3},{3,2},{4,5},{5,4},{6,7},{7,6},{8,9},{9,8},{10,11... | collective-permute-start | bytes 1572872 | tf_op jit(solution)/shard_map/ppermute | solution.py:518
  180.9 1.8 fusion
  182.7 1.3 collective-permute-start.6
  184.0 0.9 add_convert_fusion
  184.9 4.3 %all-to-all-start.8 = ((bf16[4,128,512]{2,1,0:T(8,128)(2,1)}), bf16[4,128,512]{2,1,0:T(8,128)(2,1)}, u32[]{:S(2)}, u32[]{:S(2)}) async-start(bf16[4,128,512]{2,1,0:T(8,128)(2,1)} %add_convert_fusion), calls=%async_computation.8 | async-start | bytes 1048576 | tf_op jit(solution)/shard_map/all_to_all | solution.py:578
  189.2 2.2 %query_back.1 = f32[128,1792]{1,0:T(8,128)} custom-call(f32[128,1792]{1,0:T(8,128)S(1)} %query_units.1.unit, f32[128,128]{1,0:T(8,128)S(1)} %copy-done.13, f32[128,896]{1,0:T(8,128)S(1)} %bitcast.19, f32[128,896]{1,0:T(8,128)S(1)} %copy-done.4, f32[128,128]{1,0:T(8,128)S(1)} %get-tuple-element.56.coefficient), custom_call_target="tpu_custom_call" | custom-call | flops 999999995904 | tf_op jit(solution)/shard_map/query_back/pallas_call | solution.py:415
  191.4 4.1 %all-to-all-done.8.terms = bf16[4,128,512]{2,1,0:T(8,128)(2,1)} async-done(((bf16[4,128,512]{2,1,0:T(8,128)(2,1)}), bf16[4,128,512]{2,1,0:T(8,128)(2,1)}, u32[]{:S(2)}, u32[]{:S(2)}) %all-to-all-start.8) | async-done | bytes 524320 | tf_op jit(solution)/shard_map/all_to_all | solution.py:578
  195.6 1.1 total_of.1.near
  196.7 13.2 %collective-permute-done.6.far = bf16[128,512]{1,0:T(8,128)(2,1)} collective-permute-done((bf16[128,512]{1,0:T(8,128)(2,1)}, bf16[128,512]{1,0:T(8,128)(2,1)}, u32[]{:S(2)}, u32[]{:S(2)}) %collective-permute-start.6) | collective-permute-done | bytes 131104 | tf_op jit(solution)/shard_map/ppermute | solution.py:576
  209.9 1.6 finish.1
  (31 shorter events, 0.2 us)
Async XLA Ops:
  2.2 49.3 %collective-permute-start = (bf16[128,512]{1,0:T(8,128)(2,1)}, bf16[128,512]{1,0:T(8,128)(2,1)}, u32[]{:S(2)}, u32[]{:S(2)}) collective-permute-start(bf16[128,512]{1,0:T(8,128)(2,1)} %pad_maximum_fusion.kv), channel_id=1, source_target_pairs={{0,8},{1,9},{2,10},{3,11},{4,12},{5,13},{6,14},{7,15},{16,24},{17,... | collective-permute-start | bytes 393224 | tf_op jit(solution)/shard_map/ppermute | solution.py:536
  34.4 4.5 %copy-start.8 = (bf16[128,1792]{1,0:T(8,128)(2,1)S(1)}, bf16[128,1792]{1,0:T(8,128)(2,1)}, u32[]{:S(2)}) copy-start(bf16[128,1792]{1,0:T(8,128)(2,1)} %q.3) | copy-start | bytes 1376260
  34.4 10.8 %all-to-all-start = ((bf16[4,128,512]{2,1,0:T(8,128)(2,1)}), bf16[4,128,512]{2,1,0:T(8,128)(2,1)}, u32[]{:S(2)}, u32[]{:S(2)}) async-start(bf16[4,128,512]{2,1,0:T(8,128)(2,1)} %spread.2), calls=%async_computation | async-start | bytes 1048576 | tf_op jit(solution)/shard_map/all_to_all | solution.py:537
  38.8 10.7 %copy-start.5 = (s32[1,4]{1,0:T(1,128)S(1)}, s32[1,4]{1,0:T(1,128)}, u32[]{:S(2)}) copy-start(s32[1,4]{1,0:T(1,128)} %lengths.8) | copy-start | bytes 52
  39.0 12.3 %copy-start.12 = (f32[128,128]{1,0:T(8,128)}, f32[128,128]{1,0:T(8,128)S(1)}, u32[]{:S(2)}) copy-start(f32[128,128]{1,0:T(8,128)S(1)} %query_inverses.1.inverse) | copy-start | bytes 196612
  45.2 6.1 %collective-permute-start.1 = (bf16[4,128,512]{2,1,0:T(8,128)(2,1)}, bf16[4,128,512]{2,1,0:T(8,128)(2,1)}, u32[]{:S(2)}, u32[]{:S(2)}) collective-permute-start(bf16[4,128,512]{2,1,0:T(8,128)(2,1)} %all-to-all-done.mine), channel_id=1, source_target_pairs={{0,1},{1,0},{2,3},{3,2},{4,5},{5,4},{6,7},{7,6},{8,9},{9,8},{10,11... | collective-permute-start | bytes 1572872 | tf_op jit(solution)/shard_map/ppermute | solution.py:518
  49.5 1.9 copy-start.9
  50.2 0.8 copy-start.10
  68.5 6.1 %copy-start = (bf16[1,128,1792]{2,1,0:T(8,128)(2,1)S(1)}, bf16[1,128,1792]{2,1,0:T(8,128)(2,1)}, u32[]{:S(2)}) copy-start(bf16[1,128,1792]{2,1,0:T(8,128)(2,1)} %param.6) | copy-start | bytes 1376260
  68.5 13.6 %all-to-all-start.1 = ((bf16[4,128,512]{2,1,0:T(8,128)(2,1)}), bf16[4,128,512]{2,1,0:T(8,128)(2,1)}, u32[]{:S(2)}, u32[]{:S(2)}) async-start(bf16[4,128,512]{2,1,0:T(8,128)(2,1)} %spread.3), calls=%async_computation.1 | async-start | bytes 1048576 | tf_op jit(solution)/shard_map/all_to_all | solution.py:546
  74.6 0.7 copy-start.6
  75.2 1.0 copy-start.11
  82.1 4.8 %collective-permute-start.2 = (bf16[4,128,512]{2,1,0:T(8,128)(2,1)}, bf16[4,128,512]{2,1,0:T(8,128)(2,1)S(1)}, u32[]{:S(2)}, u32[]{:S(2)}) collective-permute-start(bf16[4,128,512]{2,1,0:T(8,128)(2,1)} %all-to-all-done.1.mine), channel_id=1, source_target_pairs={{0,1},{1,0},{2,3},{3,2},{4,5},{5,4},{6,7},{7,6},{8,9},{9,8},{10,11... | collective-permute-start | bytes 1572872 | tf_op jit(solution)/shard_map/ppermute | solution.py:518
  125.5 7.1 %copy-start.7 = (s32[128]{0:T(128)S(1)}, s32[128]{0:T(128)}, u32[]{:S(2)}) copy-start(s32[128]{0:T(128)} %param.11) | copy-start | bytes 1540
  125.5 7.1 %collective-permute-start.3 = (f32[128,896]{1,0:T(8,128)S(1)}, f32[128,896]{1,0:T(8,128)S(1)}, u32[]{:S(2)}, u32[]{:S(2)}) collective-permute-start(f32[128,896]{1,0:T(8,128)S(1)} %bitcast.17), channel_id=1, source_target_pairs={{0,1},{1,0},{2,3},{3,2},{4,5},{5,4},{6,7},{7,6},{8,9},{9,8},{10,11... | collective-permute-start | bytes 1376264 | tf_op jit(solution)/shard_map/ppermute | solution.py:518
  132.5 1.6 copy-start.3
  160.6 5.1 %copy-start.1 = (bf16[128,1792]{1,0:T(8,128)(2,1)}, bf16[128,1792]{1,0:T(8,128)(2,1)S(1)}, u32[]{:S(2)}) copy-start(bf16[128,1792]{1,0:T(8,128)(2,1)S(1)} %get-tuple-element.65.out_low) | copy-start | bytes 1376260
  160.6 4.2 %collective-permute-start.4 = (bf16[4,128,512]{2,1,0:T(8,128)(2,1)S(1)}, bf16[4,128,512]{2,1,0:T(8,128)(2,1)S(1)}, u32[]{:S(2)}, u32[]{:S(2)}) collective-permute-start(bf16[4,128,512]{2,1,0:T(8,128)(2,1)S(1)} %get-tuple-element.62), channel_id=1, source_target_pairs={{0,1},{1,0},{2,3},{3,2},{4,5},{5,4},{6,7},{7,6},{8,9},{9,8},{10,11... | collective-permute-start | bytes 1572872 | tf_op jit(solution)/shard_map/ppermute | solution.py:518
  165.7 15.2 %all-to-all-start.7 = ((bf16[4,128,512]{2,1,0:T(8,128)(2,1)}), bf16[4,128,512]{2,1,0:T(8,128)(2,1)}, u32[]{:S(2)}, u32[]{:S(2)}) async-start(bf16[4,128,512]{2,1,0:T(8,128)(2,1)} %add_convert_fusion.1), calls=%async_computation.7 | async-start | bytes 1048576 | tf_op jit(solution)/shard_map/all_to_all | solution.py:573
  171.6 1.0 copy-start.2
  178.3 5.7 %collective-permute-start.5 = (bf16[4,128,512]{2,1,0:T(8,128)(2,1)}, bf16[4,128,512]{2,1,0:T(8,128)(2,1)S(1)}, u32[]{:S(2)}, u32[]{:S(2)}) collective-permute-start(bf16[4,128,512]{2,1,0:T(8,128)(2,1)} %get-tuple-element.69), channel_id=1, source_target_pairs={{0,1},{1,0},{2,3},{3,2},{4,5},{5,4},{6,7},{7,6},{8,9},{9,8},{10,11... | collective-permute-start | bytes 1572872 | tf_op jit(solution)/shard_map/ppermute | solution.py:518
  182.7 27.2 %collective-permute-start.6 = (bf16[128,512]{1,0:T(8,128)(2,1)}, bf16[128,512]{1,0:T(8,128)(2,1)}, u32[]{:S(2)}, u32[]{:S(2)}) collective-permute-start(bf16[128,512]{1,0:T(8,128)(2,1)} %fusion), channel_id=1, source_target_pairs={{8,0},{9,1},{10,2},{11,3},{12,4},{13,5},{14,6},{15,7},{24,16},{25,... | collective-permute-start | bytes 393224 | tf_op jit(solution)/shard_map/ppermute | solution.py:576
  184.9 4.3 %copy-start.4 = (f32[128,896]{1,0:T(8,128)S(1)}, f32[128,896]{1,0:T(8,128)}, u32[]{:S(2)}) copy-start(f32[128,896]{1,0:T(8,128)} %copy-done.3) | copy-start | bytes 1376260
  184.9 4.3 %copy-start.13 = (f32[128,128]{1,0:T(8,128)S(1)}, f32[128,128]{1,0:T(8,128)}, u32[]{:S(2)}) copy-start(f32[128,128]{1,0:T(8,128)} %copy-done.12) | copy-start | bytes 196612
  184.9 10.6 %all-to-all-start.8 = ((bf16[4,128,512]{2,1,0:T(8,128)(2,1)}), bf16[4,128,512]{2,1,0:T(8,128)(2,1)}, u32[]{:S(2)}, u32[]{:S(2)}) async-start(bf16[4,128,512]{2,1,0:T(8,128)(2,1)} %add_convert_fusion), calls=%async_computation.8 | async-start | bytes 1048576 | tf_op jit(solution)/shard_map/all_to_all | solution.py:578

commit v10 on v9

--- a/solution.py
+++ b/solution.py
@@ -432,12 +432,11 @@
 
 
 def spread(kv):
-    anywhere = pl.BlockSpec(memory_space=pl.ANY)
     return pl.pallas_call(
         spread_kernel,
         out_shape=shape((4, *kv.shape), kv.dtype),
-        in_specs=[anywhere],
-        out_specs=anywhere,
+        in_specs=[pl.BlockSpec(memory_space=pltpu.VMEM)],
+        out_specs=pl.BlockSpec(memory_space=pl.ANY),
         scratch_shapes=[pltpu.SemaphoreType.DMA((4,))],
         compiler_params=pltpu.CompilerParams(vmem_limit_bytes=VMEM_BYTES),
         cost_estimate=pl.CostEstimate(flops=0, bytes_accessed=0, transcendentals=0),

time: 213 us -> 183 us (0.86)
  Pallas kernels: 53.9 us -> 28.8 us
  waiting for transfers between devices: 30.9 us -> 26 us
    pallas_call x2, Pallas kernels: 34 us -> 3.44 us  [spread(): pl.pallas_call(spread_kernel, out_shape=shape((4, *kv.shape), kv.dtype),...]
    pallas_call x11, Pallas kernels: 19.9 us -> 25.4 us  [run(): pl.pallas_call(kernel, out_shape=outs, in_specs=[smem] * len(first) + [vm...]
    ppermute x1, waiting for transfers between devices: 13.2 us -> 9.49 us  [per_device(): from_high = lax.ppermute(low_sum, 'zhi', [(1, 0)])]
    all_to_all x1, waiting for transfers between devices: 2.34 us -> 0.19 us  [per_device(): low_mine = lax.all_to_all(spread(kv_low), 'x', 0, 0)]
  transfers between devices with their start and end apart: 11 -> 11, of which waited for: 8 -> 8; matrix products, arithmetic and copies ran while one was open for 1% -> 2% of each run, Pallas kernels for 14% -> 11%
where the time goes in v10:
time: 183 us; the launch traced here: 182 us
  blocking collectives  62 us (34%)
  starting transfers between devices  55.3 us (30%)
  Pallas kernels  28.8 us (16%)
  waiting for transfers between devices  26 us (14%)
  other arithmetic  5.37 us (3%)
  local copies, waits for them, and re-layouts  3.63 us (2%)
    all_to_all x3, blocking collectives, to_all(): lax.all_to_all(jnp.broadcast_to(block[None], (count,) + block.shape), axe...  39.6 us
    pallas_call x11, Pallas kernels, run(): pl.pallas_call(kernel, out_shape=outs, in_specs=[smem] * len(first) + [vm...  25.4 us
    ppermute x5, starting transfers between devices, swap_cores(): return lax.ppermute(block, 'core', [(0, 1), (1, 0)])  18.2 us
    ppermute x1, starting transfers between devices, per_device(): kv_low = lax.ppermute(kv, 'zhi', [(0, 1)])  15.2 us
    all_to_all x1, blocking collectives, per_device(): terms = added(lax.all_to_all(terms, ('y', 'zlo'), 0, 0))  15.1 us
    ppermute x1, waiting for transfers between devices, per_device(): from_high = lax.ppermute(low_sum, 'zhi', [(1, 0)])  9.49 us
    all_to_all x1, blocking collectives, per_device(): part = added(lax.all_to_all(pieces, NEAR, 0, 0))  7.42 us
    all_to_all x1, waiting for transfers between devices, per_device(): own_mine = lax.all_to_all(spread(kv), 'x', 0, 0)  6.2 us
  transfers between devices with their start and end apart: 11, of which 8 were waited for; matrix products, arithmetic and copies ran while one was open for 2% of the time, Pallas kernels for 11%

profile of v10, /device:TPU:39, one launch (start us, length us, event | category | flops | bytes accessed | tf_op | source)
XLA Modules:
  0.0 182.1 jit_solution(18069518108877561997)
XLA Ops:
  0.6 1.5 pad_maximum_fusion.kv
  2.2 15.2 %collective-permute-start = (bf16[128,512]{1,0:T(8,128)(2,1)}, bf16[128,512]{1,0:T(8,128)(2,1)}, u32[]{:S(2)}, u32[]{:S(2)}) collective-permute-start(bf16[128,512]{1,0:T(8,128)(2,1)} %pad_maximum_fusion.kv), channel_id=1, source_target_pairs={{0,8},{1,9},{2,10},{3,11},{4,12},{5,13},{6,14},{7,15},{16,24},{17,... | collective-permute-start | bytes 393224 | tf_op jit(solution)/shard_map/ppermute | solution.py:535
  17.4 1.7 spread.2
  19.1 0.0 copy-start.8
  19.1 4.4 %all-to-all-start = ((bf16[4,128,512]{2,1,0:T(8,128)(2,1)}), bf16[4,128,512]{2,1,0:T(8,128)(2,1)}, u32[]{:S(2)}, u32[]{:S(2)}) async-start(bf16[4,128,512]{2,1,0:T(8,128)(2,1)} %spread.2), calls=%async_computation | async-start | bytes 1048576 | tf_op jit(solution)/shard_map/all_to_all | solution.py:536
  23.5 0.2 query_inverses.1.inverse
  23.7 6.2 %all-to-all-done.mine = bf16[4,128,512]{2,1,0:T(8,128)(2,1)} async-done(((bf16[4,128,512]{2,1,0:T(8,128)(2,1)}), bf16[4,128,512]{2,1,0:T(8,128)(2,1)}, u32[]{:S(2)}, u32[]{:S(2)}) %all-to-all-start) | async-done | bytes 524320 | tf_op jit(solution)/shard_map/all_to_all | solution.py:536
  29.9 4.3 %collective-permute-start.1 = (bf16[4,128,512]{2,1,0:T(8,128)(2,1)}, bf16[4,128,512]{2,1,0:T(8,128)(2,1)}, u32[]{:S(2)}, u32[]{:S(2)}) collective-permute-start(bf16[4,128,512]{2,1,0:T(8,128)(2,1)} %all-to-all-done.mine), channel_id=1, source_target_pairs={{0,1},{1,0},{2,3},{3,2},{4,5},{5,4},{6,7},{7,6},{8,9},{9,8},{10,11... | collective-permute-start | bytes 1572872 | tf_op jit(solution)/shard_map/ppermute | solution.py:517
  34.2 0.8 biases.1
  35.0 0.8 copy-done.10
  35.8 0.2 collective-permute-done.1.other
  36.1 0.1 query_units.1.unit
  36.2 1.7 spread.3
  37.9 6.0 %all-to-all-start.1 = ((bf16[4,128,512]{2,1,0:T(8,128)(2,1)}), bf16[4,128,512]{2,1,0:T(8,128)(2,1)}, u32[]{:S(2)}, u32[]{:S(2)}) async-start(bf16[4,128,512]{2,1,0:T(8,128)(2,1)} %spread.3), calls=%async_computation.1 | async-start | bytes 1048576 | tf_op jit(solution)/shard_map/all_to_all | solution.py:545
  44.0 0.7 copy-done.6
  44.6 1.0 copy-done.11
  45.7 5.7 %attend_own.1 = (f32[128,1792]{1,0:T(8,128)S(1)}, f32[8,1792]{1,0:T(8,128)S(1)}) custom-call(s32[1,4]{1,0:T(1,128)S(1)} %copy-done.6, bf16[128,1792]{1,0:T(8,128)(2,1)S(1)} %bitcast.13, bf16[4,128,512]{2,1,0:T(8,128)(2,1)} %all-to-all-done.mine, bf16[4,128,512]{2,1,0:T(8,128)(2,1)} %collective-permute-done.1.other, f32[4,256,128]{2,1,0:T(8,128)S(1)} %copy-done.11), custom_call_target="tpu_custom_call" | custom-call | flops 999999995904 | tf_op jit(solution)/shard_map/attend_own/pallas_call | solution.py:415
  51.3 0.2 all-to-all-done.1.mine
  51.5 3.1 %collective-permute-start.2 = (bf16[4,128,512]{2,1,0:T(8,128)(2,1)}, bf16[4,128,512]{2,1,0:T(8,128)(2,1)S(1)}, u32[]{:S(2)}, u32[]{:S(2)}) collective-permute-start(bf16[4,128,512]{2,1,0:T(8,128)(2,1)} %all-to-all-done.1.mine), channel_id=1, source_target_pairs={{0,1},{1,0},{2,3},{3,2},{4,5},{5,4},{6,7},{7,6},{8,9},{9,8},{10,11... | collective-permute-start | bytes 1572872 | tf_op jit(solution)/shard_map/ppermute | solution.py:517
  54.6 1.7 collective-permute-done.2.other
  56.4 1.6 attend_low.1
  58.0 7.4 %all_to_all.45 = f32[8,1,896]{2,1,0:T(1,128)S(1)} all-to-all(f32[8,1,896]{2,1,0:T(1,128)S(1)} %get-tuple-element.55), channel_id=1, replica_groups=mesh['zlo'=8,'y'=4,'zhi'=2,'x'=4,'core'=2] {'x','core'}, dimensions={0} | all-to-all | bytes 57344 | tf_op jit(solution)/shard_map/all_to_all | solution.py:552
  65.5 17.9 %all_to_all.46 = f32[16,1,896]{2,1,0:T(1,128)S(1)} all-to-all(f32[16,1,896]{2,1,0:T(1,128)S(1)} %broadcast_in_dim.33), channel_id=1, replica_groups=mesh['zlo'=8,'y'=4,'zhi'=2,'x'=4,'core'=2] {'zlo','zhi'}, dimensions={0} | all-to-all | bytes 114688 | tf_op jit(solution)/shard_map/all_to_all | solution.py:513
  83.4 12.0 %all_to_all.47 = f32[16,8,896]{2,1,0:T(8,128)S(1)} all-to-all(f32[16,8,896]{2,1,0:T(8,128)S(1)} %broadcast_in_dim.35), channel_id=1, replica_groups=mesh['zlo'=8,'y'=4,'zhi'=2,'x'=4,'core'=2] {'y','x'}, dimensions={0} | all-to-all | bytes 917504 | tf_op jit(solution)/shard_map/all_to_all | solution.py:513
  95.5 5.6 %collective-permute-start.3 = (f32[128,896]{1,0:T(8,128)S(1)}, f32[128,896]{1,0:T(8,128)S(1)}, u32[]{:S(2)}, u32[]{:S(2)}) collective-permute-start(f32[128,896]{1,0:T(8,128)S(1)} %bitcast.17), channel_id=1, source_target_pairs={{0,1},{1,0},{2,3},{3,2},{4,5},{5,4},{6,7},{7,6},{8,9},{9,8},{10,11... | collective-permute-start | bytes 1376264 | tf_op jit(solution)/shard_map/ppermute | solution.py:517
  101.1 1.4 collective-permute-done.3.docs_other
  102.5 1.6 contrast.1
  104.1 15.1 %all_to_all.48 = f32[32,1,896]{2,1,0:T(1,128)S(1)} all-to-all(f32[32,1,896]{2,1,0:T(1,128)S(1)} %get-tuple-element.60), channel_id=1, replica_groups=mesh['zlo'=8,'y'=4,'zhi'=2,'x'=4,'core'=2] {'y','zlo'}, dimensions={0} | all-to-all | bytes 229376 | tf_op jit(solution)/shard_map/all_to_all | solution.py:561
  119.1 0.1 fusion.1
  119.2 9.6 %all_to_all.49.upstream = f32[8,1,896]{2,1,0:T(1,128)S(1)} all-to-all(f32[8,1,896]{2,1,0:T(1,128)S(1)} %broadcast_in_dim.37), channel_id=1, replica_groups=mesh['zlo'=8,'y'=4,'zhi'=2,'x'=4,'core'=2] {'x','core'}, dimensions={0} | all-to-all | bytes 57344 | tf_op jit(solution)/shard_map/all_to_all | solution.py:513
  128.9 1.7 back_low.1
  130.6 0.0 copy-start.1
  130.6 2.6 %collective-permute-start.4 = (bf16[4,128,512]{2,1,0:T(8,128)(2,1)S(1)}, bf16[4,128,512]{2,1,0:T(8,128)(2,1)S(1)}, u32[]{:S(2)}, u32[]{:S(2)}) collective-permute-start(bf16[4,128,512]{2,1,0:T(8,128)(2,1)S(1)} %get-tuple-element.62), channel_id=1, source_target_pairs={{0,1},{1,0},{2,3},{3,2},{4,5},{5,4},{6,7},{7,6},{8,9},{9,8},{10,11... | collective-permute-start | bytes 1572872 | tf_op jit(solution)/shard_map/ppermute | solution.py:517
  133.2 1.5 collective-permute-done.4
  134.7 0.9 add_convert_fusion.1
  135.7 5.9 %all-to-all-start.7 = ((bf16[4,128,512]{2,1,0:T(8,128)(2,1)}), bf16[4,128,512]{2,1,0:T(8,128)(2,1)}, u32[]{:S(2)}, u32[]{:S(2)}) async-start(bf16[4,128,512]{2,1,0:T(8,128)(2,1)} %add_convert_fusion.1), calls=%async_computation.7 | async-start | bytes 1048576 | tf_op jit(solution)/shard_map/all_to_all | solution.py:572
  141.6 1.0 copy-done.2
  142.6 8.9 %back_own.1 = (bf16[128,1792]{1,0:T(8,128)(2,1)}, bf16[4,128,512]{2,1,0:T(8,128)(2,1)S(1)}, bf16[4,128,512]{2,1,0:T(8,128)(2,1)}) custom-call(s32[1,4]{1,0:T(1,128)S(1)} %copy-done.6, bf16[128,1792]{1,0:T(8,128)(2,1)S(1)} %bitcast.16, bf16[4,128,512]{2,1,0:T(8,128)(2,1)} %all-to-all-done.mine, bf16[4,128,512]{2,1,0:T(8,128)(2,1)} %collective-permute-done.1.other, ...), custom_call_target="tpu_custom_call" | custom-call | tf_op jit(solution)/shard_map/back_own/pallas_call | solution.py:415
  151.5 2.6 %collective-permute-start.5 = (bf16[4,128,512]{2,1,0:T(8,128)(2,1)}, bf16[4,128,512]{2,1,0:T(8,128)(2,1)S(1)}, u32[]{:S(2)}, u32[]{:S(2)}) collective-permute-start(bf16[4,128,512]{2,1,0:T(8,128)(2,1)} %get-tuple-element.69), channel_id=1, source_target_pairs={{0,1},{1,0},{2,3},{3,2},{4,5},{5,4},{6,7},{7,6},{8,9},{9,8},{10,11... | collective-permute-start | bytes 1572872 | tf_op jit(solution)/shard_map/ppermute | solution.py:517
  154.1 1.8 %fusion = bf16[128,512]{1,0:T(8,128)(2,1)} fusion(bf16[4,128,512]{2,1,0:T(8,128)(2,1)} %all-to-all-done.7), kind=kLoop, calls=%fused_computation.3 | loop fusion | flops 524288 | bytes 655360 | tf_op jit(solution)/shard_map/add | solution.py:523
  155.9 1.3 collective-permute-start.6
  157.2 0.9 add_convert_fusion
  158.2 4.3 %all-to-all-start.8 = ((bf16[4,128,512]{2,1,0:T(8,128)(2,1)}), bf16[4,128,512]{2,1,0:T(8,128)(2,1)}, u32[]{:S(2)}, u32[]{:S(2)}) async-start(bf16[4,128,512]{2,1,0:T(8,128)(2,1)} %add_convert_fusion), calls=%async_computation.8 | async-start | bytes 1048576 | tf_op jit(solution)/shard_map/all_to_all | solution.py:577
  162.5 2.2 %query_back.1 = f32[128,1792]{1,0:T(8,128)} custom-call(f32[128,1792]{1,0:T(8,128)S(1)} %query_units.1.unit, f32[128,128]{1,0:T(8,128)S(1)} %copy-done.13, f32[128,896]{1,0:T(8,128)S(1)} %bitcast.19, f32[128,896]{1,0:T(8,128)S(1)} %copy-done.4, f32[128,128]{1,0:T(8,128)S(1)} %get-tuple-element.56.coefficient), custom_call_target="tpu_custom_call" | custom-call | flops 999999995904 | tf_op jit(solution)/shard_map/query_back/pallas_call | solution.py:415
  164.7 5.2 %all-to-all-done.8.terms = bf16[4,128,512]{2,1,0:T(8,128)(2,1)} async-done(((bf16[4,128,512]{2,1,0:T(8,128)(2,1)}), bf16[4,128,512]{2,1,0:T(8,128)(2,1)}, u32[]{:S(2)}, u32[]{:S(2)}) %all-to-all-start.8) | async-done | bytes 524320 | tf_op jit(solution)/shard_map/all_to_all | solution.py:577
  169.9 1.1 total_of.1.near
  171.0 9.5 %collective-permute-done.6.far = bf16[128,512]{1,0:T(8,128)(2,1)} collective-permute-done((bf16[128,512]{1,0:T(8,128)(2,1)}, bf16[128,512]{1,0:T(8,128)(2,1)}, u32[]{:S(2)}, u32[]{:S(2)}) %collective-permute-start.6) | collective-permute-done | bytes 131104 | tf_op jit(solution)/shard_map/ppermute | solution.py:575
  180.5 1.6 finish.1
  (31 shorter events, 0.2 us)
Async XLA Ops:
  2.2 34.0 %collective-permute-start = (bf16[128,512]{1,0:T(8,128)(2,1)}, bf16[128,512]{1,0:T(8,128)(2,1)}, u32[]{:S(2)}, u32[]{:S(2)}) collective-permute-start(bf16[128,512]{1,0:T(8,128)(2,1)} %pad_maximum_fusion.kv), channel_id=1, source_target_pairs={{0,8},{1,9},{2,10},{3,11},{4,12},{5,13},{6,14},{7,15},{16,24},{17,... | collective-permute-start | bytes 393224 | tf_op jit(solution)/shard_map/ppermute | solution.py:535
  19.1 4.5 %copy-start.8 = (bf16[128,1792]{1,0:T(8,128)(2,1)S(1)}, bf16[128,1792]{1,0:T(8,128)(2,1)}, u32[]{:S(2)}) copy-start(bf16[128,1792]{1,0:T(8,128)(2,1)} %q.3) | copy-start | bytes 1376260
  19.1 10.8 %all-to-all-start = ((bf16[4,128,512]{2,1,0:T(8,128)(2,1)}), bf16[4,128,512]{2,1,0:T(8,128)(2,1)}, u32[]{:S(2)}, u32[]{:S(2)}) async-start(bf16[4,128,512]{2,1,0:T(8,128)(2,1)} %spread.2), calls=%async_computation | async-start | bytes 1048576 | tf_op jit(solution)/shard_map/all_to_all | solution.py:536
  23.5 10.7 %copy-start.5 = (s32[1,4]{1,0:T(1,128)S(1)}, s32[1,4]{1,0:T(1,128)}, u32[]{:S(2)}) copy-start(s32[1,4]{1,0:T(1,128)} %lengths.8) | copy-start | bytes 52
  23.7 12.3 %copy-start.12 = (f32[128,128]{1,0:T(8,128)}, f32[128,128]{1,0:T(8,128)S(1)}, u32[]{:S(2)}) copy-start(f32[128,128]{1,0:T(8,128)S(1)} %query_inverses.1.inverse) | copy-start | bytes 196612
  29.9 6.1 %collective-permute-start.1 = (bf16[4,128,512]{2,1,0:T(8,128)(2,1)}, bf16[4,128,512]{2,1,0:T(8,128)(2,1)}, u32[]{:S(2)}, u32[]{:S(2)}) collective-permute-start(bf16[4,128,512]{2,1,0:T(8,128)(2,1)} %all-to-all-done.mine), channel_id=1, source_target_pairs={{0,1},{1,0},{2,3},{3,2},{4,5},{5,4},{6,7},{7,6},{8,9},{9,8},{10,11... | collective-permute-start | bytes 1572872 | tf_op jit(solution)/shard_map/ppermute | solution.py:517
  34.2 1.9 %copy-start.9 = (bf16[128,1792]{1,0:T(8,128)(2,1)S(1)}, bf16[128,1792]{1,0:T(8,128)(2,1)}, u32[]{:S(2)}) copy-start(bf16[128,1792]{1,0:T(8,128)(2,1)} %q.3) | copy-start | bytes 1376260
  35.0 0.8 copy-start.10
  37.9 6.1 %copy-start = (bf16[1,128,1792]{2,1,0:T(8,128)(2,1)S(1)}, bf16[1,128,1792]{2,1,0:T(8,128)(2,1)}, u32[]{:S(2)}) copy-start(bf16[1,128,1792]{2,1,0:T(8,128)(2,1)} %param.6) | copy-start | bytes 1376260
  37.9 13.6 %all-to-all-start.1 = ((bf16[4,128,512]{2,1,0:T(8,128)(2,1)}), bf16[4,128,512]{2,1,0:T(8,128)(2,1)}, u32[]{:S(2)}, u32[]{:S(2)}) async-start(bf16[4,128,512]{2,1,0:T(8,128)(2,1)} %spread.3), calls=%async_computation.1 | async-start | bytes 1048576 | tf_op jit(solution)/shard_map/all_to_all | solution.py:545
  44.0 0.7 copy-start.6
  44.6 1.0 copy-start.11
  51.5 4.8 %collective-permute-start.2 = (bf16[4,128,512]{2,1,0:T(8,128)(2,1)}, bf16[4,128,512]{2,1,0:T(8,128)(2,1)S(1)}, u32[]{:S(2)}, u32[]{:S(2)}) collective-permute-start(bf16[4,128,512]{2,1,0:T(8,128)(2,1)} %all-to-all-done.1.mine), channel_id=1, source_target_pairs={{0,1},{1,0},{2,3},{3,2},{4,5},{5,4},{6,7},{7,6},{8,9},{9,8},{10,11... | collective-permute-start | bytes 1572872 | tf_op jit(solution)/shard_map/ppermute | solution.py:517
  95.5 7.1 %copy-start.7 = (s32[128]{0:T(128)S(1)}, s32[128]{0:T(128)}, u32[]{:S(2)}) copy-start(s32[128]{0:T(128)} %param.11) | copy-start | bytes 1540
  95.5 7.1 %collective-permute-start.3 = (f32[128,896]{1,0:T(8,128)S(1)}, f32[128,896]{1,0:T(8,128)S(1)}, u32[]{:S(2)}, u32[]{:S(2)}) collective-permute-start(f32[128,896]{1,0:T(8,128)S(1)} %bitcast.17), channel_id=1, source_target_pairs={{0,1},{1,0},{2,3},{3,2},{4,5},{5,4},{6,7},{7,6},{8,9},{9,8},{10,11... | collective-permute-start | bytes 1376264 | tf_op jit(solution)/shard_map/ppermute | solution.py:517
  102.5 1.6 copy-start.3
  130.6 5.1 %copy-start.1 = (bf16[128,1792]{1,0:T(8,128)(2,1)}, bf16[128,1792]{1,0:T(8,128)(2,1)S(1)}, u32[]{:S(2)}) copy-start(bf16[128,1792]{1,0:T(8,128)(2,1)S(1)} %get-tuple-element.65.out_low) | copy-start | bytes 1376260
  130.6 4.2 %collective-permute-start.4 = (bf16[4,128,512]{2,1,0:T(8,128)(2,1)S(1)}, bf16[4,128,512]{2,1,0:T(8,128)(2,1)S(1)}, u32[]{:S(2)}, u32[]{:S(2)}) collective-permute-start(bf16[4,128,512]{2,1,0:T(8,128)(2,1)S(1)} %get-tuple-element.62), channel_id=1, source_target_pairs={{0,1},{1,0},{2,3},{3,2},{4,5},{5,4},{6,7},{7,6},{8,9},{9,8},{10,11... | collective-permute-start | bytes 1572872 | tf_op jit(solution)/shard_map/ppermute | solution.py:517
  135.7 18.4 %all-to-all-start.7 = ((bf16[4,128,512]{2,1,0:T(8,128)(2,1)}), bf16[4,128,512]{2,1,0:T(8,128)(2,1)}, u32[]{:S(2)}, u32[]{:S(2)}) async-start(bf16[4,128,512]{2,1,0:T(8,128)(2,1)} %add_convert_fusion.1), calls=%async_computation.7 | async-start | bytes 1048576 | tf_op jit(solution)/shard_map/all_to_all | solution.py:572
  141.6 1.0 copy-start.2
  151.5 5.7 %collective-permute-start.5 = (bf16[4,128,512]{2,1,0:T(8,128)(2,1)}, bf16[4,128,512]{2,1,0:T(8,128)(2,1)S(1)}, u32[]{:S(2)}, u32[]{:S(2)}) collective-permute-start(bf16[4,128,512]{2,1,0:T(8,128)(2,1)} %get-tuple-element.69), channel_id=1, source_target_pairs={{0,1},{1,0},{2,3},{3,2},{4,5},{5,4},{6,7},{7,6},{8,9},{9,8},{10,11... | collective-permute-start | bytes 1572872 | tf_op jit(solution)/shard_map/ppermute | solution.py:517
  155.9 24.6 %collective-permute-start.6 = (bf16[128,512]{1,0:T(8,128)(2,1)}, bf16[128,512]{1,0:T(8,128)(2,1)}, u32[]{:S(2)}, u32[]{:S(2)}) collective-permute-start(bf16[128,512]{1,0:T(8,128)(2,1)} %fusion), channel_id=1, source_target_pairs={{8,0},{9,1},{10,2},{11,3},{12,4},{13,5},{14,6},{15,7},{24,16},{25,... | collective-permute-start | bytes 393224 | tf_op jit(solution)/shard_map/ppermute | solution.py:575
  158.2 4.3 %copy-start.4 = (f32[128,896]{1,0:T(8,128)S(1)}, f32[128,896]{1,0:T(8,128)}, u32[]{:S(2)}) copy-start(f32[128,896]{1,0:T(8,128)} %copy-done.3) | copy-start | bytes 1376260
  158.2 4.3 %copy-start.13 = (f32[128,128]{1,0:T(8,128)S(1)}, f32[128,128]{1,0:T(8,128)}, u32[]{:S(2)}) copy-start(f32[128,128]{1,0:T(8,128)} %copy-done.12) | copy-start | bytes 196612
  158.2 11.7 %all-to-all-start.8 = ((bf16[4,128,512]{2,1,0:T(8,128)(2,1)}), bf16[4,128,512]{2,1,0:T(8,128)(2,1)}, u32[]{:S(2)}, u32[]{:S(2)}) async-start(bf16[4,128,512]{2,1,0:T(8,128)(2,1)} %add_convert_fusion), calls=%async_computation.8 | async-start | bytes 1048576 | tf_op jit(solution)/shard_map/all_to_all | solution.py:577

commit v11 on v10

--- a/solution.py
+++ b/solution.py
@@ -228,6 +228,12 @@
     unit[...] = q[...].astype(jnp.float32) * inverse[:, :1]
 
 
+def mm_parts(a, b, dims):
+    a_big, a_small = halves(a)
+    b_big, b_small = halves(b)
+    return mm(a_big, b_big, dims) + (mm(a_big, b_small, dims) + mm(a_small, b_big, dims))
+
+
 def contrast_kernel(unit, positive, docs_mine, docs_other, coefficient, terms, own_docs):
     z_lo, y, _, x, core = place()
     d_mine, d_other = docs_mine[...], docs_other[...]
@@ -239,8 +245,8 @@
     q_left, q_right = unit[:, :PIECE], unit[:, PIECE:]
     q_mine = jnp.where(core == 1, q_right, q_left)
     q_other = jnp.where(core == 1, q_left, q_right)
-    logits = mm(d_mine * doc_inv, q_mine, NT, FULL_ACCURACY)
-    logits = (logits + mm(d_other * doc_inv, q_other, NT, FULL_ACCURACY)) / INVERSE_TEMPER
+    logits = mm_parts(d_mine * doc_inv, q_mine, NT)
+    logits = (logits + mm_parts(d_other * doc_inv, q_other, NT)) / INVERSE_TEMPER
     exps = jnp.exp(logits)
     at = lax.broadcasted_iota(jnp.int32, (NDOC, 128), 0)
     doc = ((at % 8) * 4 + at // 32) * DOCS + (at // 8) % 4
@@ -249,7 +255,7 @@
     near = jnp.concatenate(
         [coefficient[pl.ds(pl.multiple_of(b * 32 + x * 8, 8), 8), :] for b in range(4)], axis=0
     )
-    near_terms = mm(near, q_mine, NN, FULL_ACCURACY) / INVERSE_TEMPER
+    near_terms = mm_parts(near, q_mine, NN) / INVERSE_TEMPER
     for r in range(32):
         terms[r] = near_terms[r : r + 1]
     own_docs[...] = jnp.zeros((8, EMB), jnp.float32)

time: 183 us -> 183 us (level)
  no operation moved by 1% of the time
where the time goes in v11:
time: 183 us; the launch traced here: 182 us
  blocking collectives  62.7 us (34%)
  starting transfers between devices  55.3 us (30%)
  Pallas kernels  28.4 us (16%)
  waiting for transfers between devices  25.6 us (14%)
  other arithmetic  5.37 us (3%)
  local copies, waits for them, and re-layouts  3.63 us (2%)
    all_to_all x3, blocking collectives, to_all(): lax.all_to_all(jnp.broadcast_to(block[None], (count,) + block.shape), axe...  40.2 us
    pallas_call x11, Pallas kernels, run(): pl.pallas_call(kernel, out_shape=outs, in_specs=[smem] * len(first) + [vm...  24.9 us
    ppermute x5, starting transfers between devices, swap_cores(): return lax.ppermute(block, 'core', [(0, 1), (1, 0)])  18.2 us
    ppermute x1, starting transfers between devices, per_device(): kv_low = lax.ppermute(kv, 'zhi', [(0, 1)])  15.2 us
    all_to_all x1, blocking collectives, per_device(): terms = added(lax.all_to_all(terms, ('y', 'zlo'), 0, 0))  15.1 us
    ppermute x1, waiting for transfers between devices, per_device(): from_high = lax.ppermute(low_sum, 'zhi', [(1, 0)])  9.13 us
    all_to_all x1, blocking collectives, per_device(): part = added(lax.all_to_all(pieces, NEAR, 0, 0))  7.42 us
    all_to_all x1, waiting for transfers between devices, per_device(): own_mine = lax.all_to_all(spread(kv), 'x', 0, 0)  6.2 us
  transfers between devices with their start and end apart: 11, of which 8 were waited for; matrix products, arithmetic and copies ran while one was open for 2% of the time, Pallas kernels for 11%

profile of v11, /device:TPU:39, one launch (start us, length us, event | category | flops | bytes accessed | tf_op | source)
XLA Modules:
  0.0 181.9 jit_solution(12232386843059182541)
XLA Ops:
  0.6 1.5 pad_maximum_fusion.kv
  2.2 15.2 %collective-permute-start = (bf16[128,512]{1,0:T(8,128)(2,1)}, bf16[128,512]{1,0:T(8,128)(2,1)}, u32[]{:S(2)}, u32[]{:S(2)}) collective-permute-start(bf16[128,512]{1,0:T(8,128)(2,1)} %pad_maximum_fusion.kv), channel_id=1, source_target_pairs={{0,8},{1,9},{2,10},{3,11},{4,12},{5,13},{6,14},{7,15},{16,24},{17,... | collective-permute-start | bytes 393224 | tf_op jit(solution)/shard_map/ppermute | solution.py:541
  17.4 1.7 spread.2
  19.1 0.0 copy-start.8
  19.1 4.4 %all-to-all-start = ((bf16[4,128,512]{2,1,0:T(8,128)(2,1)}), bf16[4,128,512]{2,1,0:T(8,128)(2,1)}, u32[]{:S(2)}, u32[]{:S(2)}) async-start(bf16[4,128,512]{2,1,0:T(8,128)(2,1)} %spread.2), calls=%async_computation | async-start | bytes 1048576 | tf_op jit(solution)/shard_map/all_to_all | solution.py:542
  23.5 0.2 query_inverses.1.inverse
  23.7 6.2 %all-to-all-done.mine = bf16[4,128,512]{2,1,0:T(8,128)(2,1)} async-done(((bf16[4,128,512]{2,1,0:T(8,128)(2,1)}), bf16[4,128,512]{2,1,0:T(8,128)(2,1)}, u32[]{:S(2)}, u32[]{:S(2)}) %all-to-all-start) | async-done | bytes 524320 | tf_op jit(solution)/shard_map/all_to_all | solution.py:542
  29.9 4.3 %collective-permute-start.1 = (bf16[4,128,512]{2,1,0:T(8,128)(2,1)}, bf16[4,128,512]{2,1,0:T(8,128)(2,1)}, u32[]{:S(2)}, u32[]{:S(2)}) collective-permute-start(bf16[4,128,512]{2,1,0:T(8,128)(2,1)} %all-to-all-done.mine), channel_id=1, source_target_pairs={{0,1},{1,0},{2,3},{3,2},{4,5},{5,4},{6,7},{7,6},{8,9},{9,8},{10,11... | collective-permute-start | bytes 1572872 | tf_op jit(solution)/shard_map/ppermute | solution.py:523
  34.2 0.0 copy-start.9
  34.2 0.8 biases.1
  35.0 0.8 copy-done.10
  35.8 0.2 collective-permute-done.1.other
  36.1 0.1 query_units.1.unit
  36.2 1.7 spread.3
  37.9 6.0 %all-to-all-start.1 = ((bf16[4,128,512]{2,1,0:T(8,128)(2,1)}), bf16[4,128,512]{2,1,0:T(8,128)(2,1)}, u32[]{:S(2)}, u32[]{:S(2)}) async-start(bf16[4,128,512]{2,1,0:T(8,128)(2,1)} %spread.3), calls=%async_computation.1 | async-start | bytes 1048576 | tf_op jit(solution)/shard_map/all_to_all | solution.py:551
  44.0 0.7 copy-done.6
  44.6 1.0 copy-done.11
  45.7 5.7 %attend_own.1 = (f32[128,1792]{1,0:T(8,128)S(1)}, f32[8,1792]{1,0:T(8,128)S(1)}) custom-call(s32[1,4]{1,0:T(1,128)S(1)} %copy-done.6, bf16[128,1792]{1,0:T(8,128)(2,1)S(1)} %bitcast.13, bf16[4,128,512]{2,1,0:T(8,128)(2,1)} %all-to-all-done.mine, bf16[4,128,512]{2,1,0:T(8,128)(2,1)} %collective-permute-done.1.other, f32[4,256,128]{2,1,0:T(8,128)S(1)} %copy-done.11), custom_call_target="tpu_custom_call" | custom-call | flops 999999995904 | tf_op jit(solution)/shard_map/attend_own/pallas_call | solution.py:421
  51.3 0.2 all-to-all-done.1.mine
  51.5 3.1 %collective-permute-start.2 = (bf16[4,128,512]{2,1,0:T(8,128)(2,1)}, bf16[4,128,512]{2,1,0:T(8,128)(2,1)S(1)}, u32[]{:S(2)}, u32[]{:S(2)}) collective-permute-start(bf16[4,128,512]{2,1,0:T(8,128)(2,1)} %all-to-all-done.1.mine), channel_id=1, source_target_pairs={{0,1},{1,0},{2,3},{3,2},{4,5},{5,4},{6,7},{7,6},{8,9},{9,8},{10,11... | collective-permute-start | bytes 1572872 | tf_op jit(solution)/shard_map/ppermute | solution.py:523
  54.6 1.7 collective-permute-done.2.other
  56.4 1.6 attend_low.1
  58.0 7.4 %all_to_all.45 = f32[8,1,896]{2,1,0:T(1,128)S(1)} all-to-all(f32[8,1,896]{2,1,0:T(1,128)S(1)} %get-tuple-element.55), channel_id=1, replica_groups=mesh['zlo'=8,'y'=4,'zhi'=2,'x'=4,'core'=2] {'x','core'}, dimensions={0} | all-to-all | bytes 57344 | tf_op jit(solution)/shard_map/all_to_all | solution.py:558
  65.5 17.9 %all_to_all.46 = f32[16,1,896]{2,1,0:T(1,128)S(1)} all-to-all(f32[16,1,896]{2,1,0:T(1,128)S(1)} %broadcast_in_dim.33), channel_id=1, replica_groups=mesh['zlo'=8,'y'=4,'zhi'=2,'x'=4,'core'=2] {'zlo','zhi'}, dimensions={0} | all-to-all | bytes 114688 | tf_op jit(solution)/shard_map/all_to_all | solution.py:519
  83.4 12.7 %all_to_all.47 = f32[16,8,896]{2,1,0:T(8,128)S(1)} all-to-all(f32[16,8,896]{2,1,0:T(8,128)S(1)} %broadcast_in_dim.35), channel_id=1, replica_groups=mesh['zlo'=8,'y'=4,'zhi'=2,'x'=4,'core'=2] {'y','x'}, dimensions={0} | all-to-all | bytes 917504 | tf_op jit(solution)/shard_map/all_to_all | solution.py:519
  96.1 5.6 %collective-permute-start.3 = (f32[128,896]{1,0:T(8,128)S(1)}, f32[128,896]{1,0:T(8,128)S(1)}, u32[]{:S(2)}, u32[]{:S(2)}) collective-permute-start(f32[128,896]{1,0:T(8,128)S(1)} %bitcast.17), channel_id=1, source_target_pairs={{0,1},{1,0},{2,3},{3,2},{4,5},{5,4},{6,7},{7,6},{8,9},{9,8},{10,11... | collective-permute-start | bytes 1376264 | tf_op jit(solution)/shard_map/ppermute | solution.py:523
  101.8 1.4 collective-permute-done.3.docs_other
  103.2 1.1 contrast.1
  104.3 15.1 %all_to_all.48 = f32[32,1,896]{2,1,0:T(1,128)S(1)} all-to-all(f32[32,1,896]{2,1,0:T(1,128)S(1)} %get-tuple-element.60), channel_id=1, replica_groups=mesh['zlo'=8,'y'=4,'zhi'=2,'x'=4,'core'=2] {'y','zlo'}, dimensions={0} | all-to-all | bytes 229376 | tf_op jit(solution)/shard_map/all_to_all | solution.py:567
  119.3 0.1 fusion.1
  119.4 9.6 %all_to_all.49.upstream = f32[8,1,896]{2,1,0:T(1,128)S(1)} all-to-all(f32[8,1,896]{2,1,0:T(1,128)S(1)} %broadcast_in_dim.37), channel_id=1, replica_groups=mesh['zlo'=8,'y'=4,'zhi'=2,'x'=4,'core'=2] {'x','core'}, dimensions={0} | all-to-all | bytes 57344 | tf_op jit(solution)/shard_map/all_to_all | solution.py:519
  129.1 1.7 back_low.1
  130.8 2.6 %collective-permute-start.4 = (bf16[4,128,512]{2,1,0:T(8,128)(2,1)S(1)}, bf16[4,128,512]{2,1,0:T(8,128)(2,1)S(1)}, u32[]{:S(2)}, u32[]{:S(2)}) collective-permute-start(bf16[4,128,512]{2,1,0:T(8,128)(2,1)S(1)} %get-tuple-element.62), channel_id=1, source_target_pairs={{0,1},{1,0},{2,3},{3,2},{4,5},{5,4},{6,7},{7,6},{8,9},{9,8},{10,11... | collective-permute-start | bytes 1572872 | tf_op jit(solution)/shard_map/ppermute | solution.py:523
  133.4 1.5 collective-permute-done.4
  134.9 0.9 add_convert_fusion.1
  135.9 5.9 %all-to-all-start.7 = ((bf16[4,128,512]{2,1,0:T(8,128)(2,1)}), bf16[4,128,512]{2,1,0:T(8,128)(2,1)}, u32[]{:S(2)}, u32[]{:S(2)}) async-start(bf16[4,128,512]{2,1,0:T(8,128)(2,1)} %add_convert_fusion.1), calls=%async_computation.7 | async-start | bytes 1048576 | tf_op jit(solution)/shard_map/all_to_all | solution.py:578
  141.8 1.0 copy-done.2
  142.8 8.9 %back_own.1 = (bf16[128,1792]{1,0:T(8,128)(2,1)}, bf16[4,128,512]{2,1,0:T(8,128)(2,1)S(1)}, bf16[4,128,512]{2,1,0:T(8,128)(2,1)}) custom-call(s32[1,4]{1,0:T(1,128)S(1)} %copy-done.6, bf16[128,1792]{1,0:T(8,128)(2,1)S(1)} %bitcast.16, bf16[4,128,512]{2,1,0:T(8,128)(2,1)} %all-to-all-done.mine, bf16[4,128,512]{2,1,0:T(8,128)(2,1)} %collective-permute-done.1.other, ...), custom_call_target="tpu_custom_call" | custom-call | tf_op jit(solution)/shard_map/back_own/pallas_call | solution.py:421
  151.7 2.6 %collective-permute-start.5 = (bf16[4,128,512]{2,1,0:T(8,128)(2,1)}, bf16[4,128,512]{2,1,0:T(8,128)(2,1)S(1)}, u32[]{:S(2)}, u32[]{:S(2)}) collective-permute-start(bf16[4,128,512]{2,1,0:T(8,128)(2,1)} %get-tuple-element.69), channel_id=1, source_target_pairs={{0,1},{1,0},{2,3},{3,2},{4,5},{5,4},{6,7},{7,6},{8,9},{9,8},{10,11... | collective-permute-start | bytes 1572872 | tf_op jit(solution)/shard_map/ppermute | solution.py:523
  154.3 1.8 %fusion = bf16[128,512]{1,0:T(8,128)(2,1)} fusion(bf16[4,128,512]{2,1,0:T(8,128)(2,1)} %all-to-all-done.7), kind=kLoop, calls=%fused_computation.3 | loop fusion | flops 524288 | bytes 655360 | tf_op jit(solution)/shard_map/add | solution.py:529
  156.1 1.3 collective-permute-start.6
  157.4 0.9 add_convert_fusion
  158.4 4.3 %all-to-all-start.8 = ((bf16[4,128,512]{2,1,0:T(8,128)(2,1)}), bf16[4,128,512]{2,1,0:T(8,128)(2,1)}, u32[]{:S(2)}, u32[]{:S(2)}) async-start(bf16[4,128,512]{2,1,0:T(8,128)(2,1)} %add_convert_fusion), calls=%async_computation.8 | async-start | bytes 1048576 | tf_op jit(solution)/shard_map/all_to_all | solution.py:583
  162.7 2.2 %query_back.1 = f32[128,1792]{1,0:T(8,128)} custom-call(f32[128,1792]{1,0:T(8,128)S(1)} %query_units.1.unit, f32[128,128]{1,0:T(8,128)S(1)} %copy-done.13, f32[128,896]{1,0:T(8,128)S(1)} %bitcast.19, f32[128,896]{1,0:T(8,128)S(1)} %copy-done.4, f32[128,128]{1,0:T(8,128)S(1)} %get-tuple-element.56.coefficient), custom_call_target="tpu_custom_call" | custom-call | flops 999999995904 | tf_op jit(solution)/shard_map/query_back/pallas_call | solution.py:421
  164.9 5.2 %all-to-all-done.8.terms = bf16[4,128,512]{2,1,0:T(8,128)(2,1)} async-done(((bf16[4,128,512]{2,1,0:T(8,128)(2,1)}), bf16[4,128,512]{2,1,0:T(8,128)(2,1)}, u32[]{:S(2)}, u32[]{:S(2)}) %all-to-all-start.8) | async-done | bytes 524320 | tf_op jit(solution)/shard_map/all_to_all | solution.py:583
  170.1 1.1 total_of.1.near
  171.2 9.1 %collective-permute-done.6.far = bf16[128,512]{1,0:T(8,128)(2,1)} collective-permute-done((bf16[128,512]{1,0:T(8,128)(2,1)}, bf16[128,512]{1,0:T(8,128)(2,1)}, u32[]{:S(2)}, u32[]{:S(2)}) %collective-permute-start.6) | collective-permute-done | bytes 131104 | tf_op jit(solution)/shard_map/ppermute | solution.py:581
  180.3 1.6 finish.1
  (31 shorter events, 0.2 us)
Async XLA Ops:
  2.2 34.0 %collective-permute-start = (bf16[128,512]{1,0:T(8,128)(2,1)}, bf16[128,512]{1,0:T(8,128)(2,1)}, u32[]{:S(2)}, u32[]{:S(2)}) collective-permute-start(bf16[128,512]{1,0:T(8,128)(2,1)} %pad_maximum_fusion.kv), channel_id=1, source_target_pairs={{0,8},{1,9},{2,10},{3,11},{4,12},{5,13},{6,14},{7,15},{16,24},{17,... | collective-permute-start | bytes 393224 | tf_op jit(solution)/shard_map/ppermute | solution.py:541
  19.1 4.5 %copy-start.8 = (bf16[128,1792]{1,0:T(8,128)(2,1)S(1)}, bf16[128,1792]{1,0:T(8,128)(2,1)}, u32[]{:S(2)}) copy-start(bf16[128,1792]{1,0:T(8,128)(2,1)} %q.3) | copy-start | bytes 1376260
  19.1 10.8 %all-to-all-start = ((bf16[4,128,512]{2,1,0:T(8,128)(2,1)}), bf16[4,128,512]{2,1,0:T(8,128)(2,1)}, u32[]{:S(2)}, u32[]{:S(2)}) async-start(bf16[4,128,512]{2,1,0:T(8,128)(2,1)} %spread.2), calls=%async_computation | async-start | bytes 1048576 | tf_op jit(solution)/shard_map/all_to_all | solution.py:542
  23.5 10.7 %copy-start.5 = (s32[1,4]{1,0:T(1,128)S(1)}, s32[1,4]{1,0:T(1,128)}, u32[]{:S(2)}) copy-start(s32[1,4]{1,0:T(1,128)} %lengths.8) | copy-start | bytes 52
  23.7 12.3 %copy-start.12 = (f32[128,128]{1,0:T(8,128)}, f32[128,128]{1,0:T(8,128)S(1)}, u32[]{:S(2)}) copy-start(f32[128,128]{1,0:T(8,128)S(1)} %query_inverses.1.inverse) | copy-start | bytes 196612
  29.9 6.1 %collective-permute-start.1 = (bf16[4,128,512]{2,1,0:T(8,128)(2,1)}, bf16[4,128,512]{2,1,0:T(8,128)(2,1)}, u32[]{:S(2)}, u32[]{:S(2)}) collective-permute-start(bf16[4,128,512]{2,1,0:T(8,128)(2,1)} %all-to-all-done.mine), channel_id=1, source_target_pairs={{0,1},{1,0},{2,3},{3,2},{4,5},{5,4},{6,7},{7,6},{8,9},{9,8},{10,11... | collective-permute-start | bytes 1572872 | tf_op jit(solution)/shard_map/ppermute | solution.py:523
  34.2 1.9 %copy-start.9 = (bf16[128,1792]{1,0:T(8,128)(2,1)S(1)}, bf16[128,1792]{1,0:T(8,128)(2,1)}, u32[]{:S(2)}) copy-start(bf16[128,1792]{1,0:T(8,128)(2,1)} %q.3) | copy-start | bytes 1376260
  35.0 0.8 copy-start.10
  37.9 6.1 %copy-start = (bf16[1,128,1792]{2,1,0:T(8,128)(2,1)S(1)}, bf16[1,128,1792]{2,1,0:T(8,128)(2,1)}, u32[]{:S(2)}) copy-start(bf16[1,128,1792]{2,1,0:T(8,128)(2,1)} %param.6) | copy-start | bytes 1376260
  37.9 13.6 %all-to-all-start.1 = ((bf16[4,128,512]{2,1,0:T(8,128)(2,1)}), bf16[4,128,512]{2,1,0:T(8,128)(2,1)}, u32[]{:S(2)}, u32[]{:S(2)}) async-start(bf16[4,128,512]{2,1,0:T(8,128)(2,1)} %spread.3), calls=%async_computation.1 | async-start | bytes 1048576 | tf_op jit(solution)/shard_map/all_to_all | solution.py:551
  44.0 0.7 copy-start.6
  44.6 1.0 copy-start.11
  51.5 4.8 %collective-permute-start.2 = (bf16[4,128,512]{2,1,0:T(8,128)(2,1)}, bf16[4,128,512]{2,1,0:T(8,128)(2,1)S(1)}, u32[]{:S(2)}, u32[]{:S(2)}) collective-permute-start(bf16[4,128,512]{2,1,0:T(8,128)(2,1)} %all-to-all-done.1.mine), channel_id=1, source_target_pairs={{0,1},{1,0},{2,3},{3,2},{4,5},{5,4},{6,7},{7,6},{8,9},{9,8},{10,11... | collective-permute-start | bytes 1572872 | tf_op jit(solution)/shard_map/ppermute | solution.py:523
  96.1 7.1 %copy-start.7 = (s32[128]{0:T(128)S(1)}, s32[128]{0:T(128)}, u32[]{:S(2)}) copy-start(s32[128]{0:T(128)} %param.11) | copy-start | bytes 1540
  96.1 7.1 %collective-permute-start.3 = (f32[128,896]{1,0:T(8,128)S(1)}, f32[128,896]{1,0:T(8,128)S(1)}, u32[]{:S(2)}, u32[]{:S(2)}) collective-permute-start(f32[128,896]{1,0:T(8,128)S(1)} %bitcast.17), channel_id=1, source_target_pairs={{0,1},{1,0},{2,3},{3,2},{4,5},{5,4},{6,7},{7,6},{8,9},{9,8},{10,11... | collective-permute-start | bytes 1376264 | tf_op jit(solution)/shard_map/ppermute | solution.py:523
  103.2 1.1 copy-start.3
  130.8 5.1 %copy-start.1 = (bf16[128,1792]{1,0:T(8,128)(2,1)}, bf16[128,1792]{1,0:T(8,128)(2,1)S(1)}, u32[]{:S(2)}) copy-start(bf16[128,1792]{1,0:T(8,128)(2,1)S(1)} %get-tuple-element.65.out_low) | copy-start | bytes 1376260
  130.8 4.2 %collective-permute-start.4 = (bf16[4,128,512]{2,1,0:T(8,128)(2,1)S(1)}, bf16[4,128,512]{2,1,0:T(8,128)(2,1)S(1)}, u32[]{:S(2)}, u32[]{:S(2)}) collective-permute-start(bf16[4,128,512]{2,1,0:T(8,128)(2,1)S(1)} %get-tuple-element.62), channel_id=1, source_target_pairs={{0,1},{1,0},{2,3},{3,2},{4,5},{5,4},{6,7},{7,6},{8,9},{9,8},{10,11... | collective-permute-start | bytes 1572872 | tf_op jit(solution)/shard_map/ppermute | solution.py:523
  135.9 18.4 %all-to-all-start.7 = ((bf16[4,128,512]{2,1,0:T(8,128)(2,1)}), bf16[4,128,512]{2,1,0:T(8,128)(2,1)}, u32[]{:S(2)}, u32[]{:S(2)}) async-start(bf16[4,128,512]{2,1,0:T(8,128)(2,1)} %add_convert_fusion.1), calls=%async_computation.7 | async-start | bytes 1048576 | tf_op jit(solution)/shard_map/all_to_all | solution.py:578
  141.8 1.0 copy-start.2
  151.7 5.7 %collective-permute-start.5 = (bf16[4,128,512]{2,1,0:T(8,128)(2,1)}, bf16[4,128,512]{2,1,0:T(8,128)(2,1)S(1)}, u32[]{:S(2)}, u32[]{:S(2)}) collective-permute-start(bf16[4,128,512]{2,1,0:T(8,128)(2,1)} %get-tuple-element.69), channel_id=1, source_target_pairs={{0,1},{1,0},{2,3},{3,2},{4,5},{5,4},{6,7},{7,6},{8,9},{9,8},{10,11... | collective-permute-start | bytes 1572872 | tf_op jit(solution)/shard_map/ppermute | solution.py:523
  156.1 24.2 %collective-permute-start.6 = (bf16[128,512]{1,0:T(8,128)(2,1)}, bf16[128,512]{1,0:T(8,128)(2,1)}, u32[]{:S(2)}, u32[]{:S(2)}) collective-permute-start(bf16[128,512]{1,0:T(8,128)(2,1)} %fusion), channel_id=1, source_target_pairs={{8,0},{9,1},{10,2},{11,3},{12,4},{13,5},{14,6},{15,7},{24,16},{25,... | collective-permute-start | bytes 393224 | tf_op jit(solution)/shard_map/ppermute | solution.py:581
  158.4 4.3 %copy-start.4 = (f32[128,896]{1,0:T(8,128)S(1)}, f32[128,896]{1,0:T(8,128)}, u32[]{:S(2)}) copy-start(f32[128,896]{1,0:T(8,128)} %copy-done.3) | copy-start | bytes 1376260
  158.4 4.3 %copy-start.13 = (f32[128,128]{1,0:T(8,128)S(1)}, f32[128,128]{1,0:T(8,128)}, u32[]{:S(2)}) copy-start(f32[128,128]{1,0:T(8,128)} %copy-done.12) | copy-start | bytes 196612
  158.4 11.7 %all-to-all-start.8 = ((bf16[4,128,512]{2,1,0:T(8,128)(2,1)}), bf16[4,128,512]{2,1,0:T(8,128)(2,1)}, u32[]{:S(2)}, u32[]{:S(2)}) async-start(bf16[4,128,512]{2,1,0:T(8,128)(2,1)} %add_convert_fusion), calls=%async_computation.8 | async-start | bytes 1048576 | tf_op jit(solution)/shard_map/all_to_all | solution.py:583
